TPU v7x, 32 devices: a whole 2x2x4 slice. The times are simulated.
32 devices in a mesh: dp: 8 (over z, y), head: 4 (over x, core).
Axes of the slice: x: 2, y: 2, z: 4, core: 2. Of those that a mesh axis runs over, the one named last changes fastest.
Arguments:
- tokens: bfloat16 [8192, 960], P(('dp', 'head')), may hold values from -6 to 6
- cotangent: bfloat16 [8192, 960], P(('dp', 'head')), may hold values from -6 to 6
- lengths: int32 [8], P('dp'), may hold values from 769 to 1024, as said below
- attn_gain: bfloat16 [960], replicated, may hold values from 0.25 to 1.75
- w_query: bfloat16 [960, 960], replicated, may hold values from -0.1875 to 0.1875
- w_key: bfloat16 [960, 320], replicated, may hold values from -0.1875 to 0.1875
- w_value: bfloat16 [960, 320], replicated, may hold values from -0.1875 to 0.1875
- w_output: bfloat16 [960, 960], replicated, may hold values from -2 to 2
- ffn_gain: bfloat16 [960], replicated, may hold values from 0.25 to 1.75
- w_gate: bfloat16 [960, 2560], P(None, 'head'), may hold values from -0.1875 to 0.1875
- w_up: bfloat16 [960, 2560], P(None, 'head'), may hold values from -0.1875 to 0.1875
- w_down: bfloat16 [2560, 960], P('head'), may hold values from -0.125 to 0.125
Outputs:
- block_out: bfloat16 [8192, 960], P(('dp', 'head'))
- input_grad: float32 [8192, 960], P(('dp', 'head'))
- attn_gain_grad: float32 [960], P('dp')
- w_query_grad: float32 [960, 960], P('dp')
- w_key_grad: float32 [960, 320], P('dp')
- w_value_grad: float32 [960, 320], P('dp')
- w_output_grad: float32 [960, 960], P(None, 'dp')
- ffn_gain_grad: float32 [960], P('dp')
- w_gate_grad: float32 [960, 2560], P('dp', 'head')
- w_up_grad: float32 [960, 2560], P('dp', 'head')
- w_down_grad: float32 [2560, 960], P('head', 'dp')
Inputs may be any that keep to these rules, and one draw needn't show every extreme that they name: `lengths`: each sequence's valid tokens cover more than three quarters of its 1024 rows; some sequence is full and some has the fewest allowed.
All inputs are finite; a program needn't handle non-finite values.
Results may differ from a plain program's by a relative error of at most 0.03.
Values may be sent and summed in bfloat16 or wider, within the bound.
A program may use at most 192 MiB of HBM per device.

v0:
```python
import jax
import jax.numpy as jnp
from jax import lax
from jax.sharding import PartitionSpec as P

HQ = 15
KVH = 5
HD = 64


EPSILON = 1e-05


def rope_tables(seq_rows, head_width):
    half_width = head_width // 2
    frequency = 10000.0 ** (-(jnp.arange(half_width, dtype=jnp.float32) * 2.0 / head_width))
    angles = jnp.arange(seq_rows, dtype=jnp.float32)[:, None] * frequency[None, :]
    return (jnp.cos(angles)[:, None, :], jnp.sin(angles)[:, None, :])


def rotate(heads, cosine, sine_part):
    half_width = heads.shape[-1] // 2
    lower_half = heads[..., :half_width]
    upper_half = heads[..., half_width:]
    return jnp.concatenate(
        [
            lower_half * cosine - upper_half * sine_part,
            upper_half * cosine + lower_half * sine_part,
        ],
        axis=-1,
    )


def unrotate(heads, cosine, sine_part):
    half_width = heads.shape[-1] // 2
    lower_half = heads[..., :half_width]
    upper_half = heads[..., half_width:]
    return jnp.concatenate(
        [
            lower_half * cosine + upper_half * sine_part,
            upper_half * cosine - lower_half * sine_part,
        ],
        axis=-1,
    )


def rows_product(left, right):
    return lax.dot_general(
        left, right, (((0,), (0,)), ((), ())), preferred_element_type=jnp.float32
    )


def cols_product(left, right):
    return lax.dot_general(
        left, right, (((1,), (1,)), ((), ())), preferred_element_type=jnp.float32
    )


def norm_back(values_in, inverse, gain, grad_normed, grad_skip):
    normal = values_in * inverse
    gain_part = jnp.sum(grad_normed * normal, axis=0)
    scaled = grad_normed * gain
    return (
        gain_part,
        grad_skip + inverse * (scaled - normal * jnp.mean(scaled * normal, axis=1, keepdims=True)),
    )


def block_mask(row_start, block_rows, key_pos, length):
    query_pos = row_start + jnp.arange(block_rows, dtype=jnp.int32)
    return (key_pos[None, :] <= query_pos[:, None]) & (key_pos[None, :] < length)


def attend(queries, key_rows, value_rows, length):
    seq_rows = queries.shape[0]
    block_rows = min(512, seq_rows)
    block_count = seq_rows // block_rows
    score_scale = HD ** (-0.5)
    key_pos = jnp.arange(seq_rows, dtype=jnp.int32)

    def one_block(inputs):
        query_block, row_start = inputs
        scores = (
            jnp.einsum("bgjd,kgd->gjbk", query_block, key_rows, preferred_element_type=jnp.float32)
            * score_scale
        )
        scores = jnp.where(block_mask(row_start, block_rows, key_pos, length), scores, -1e30)
        row_max = jnp.max(scores, axis=-1, keepdims=True)
        exponent = jnp.exp(scores - row_max)
        totals = jnp.sum(exponent, axis=-1, keepdims=True)
        probability = (exponent / totals).astype(jnp.bfloat16)
        attended = jnp.einsum(
            "gjbk,kgd->bgjd", probability, value_rows, preferred_element_type=jnp.float32
        )
        return (attended, (row_max + jnp.log(totals))[..., 0])

    query_blocks = queries.reshape(
        block_count, block_rows, queries.shape[1], queries.shape[2], queries.shape[3]
    )
    starts = jnp.arange(block_count, dtype=jnp.int32) * block_rows
    attended, log_totals = lax.map(one_block, (query_blocks, starts))
    return (attended.reshape(seq_rows, -1), log_totals)


def attend_back(queries, key_rows, value_rows, length, log_totals, grad_attended):
    seq_rows = queries.shape[0]
    block_rows = min(512, seq_rows)
    block_count = seq_rows // block_rows
    score_scale = HD ** (-0.5)
    key_pos = jnp.arange(seq_rows, dtype=jnp.int32)

    def one_block(carried, inputs):
        grad_keys, grad_values = carried
        query_block, grad_block, block_totals, row_start = inputs
        scores = (
            jnp.einsum("bgjd,kgd->gjbk", query_block, key_rows, preferred_element_type=jnp.float32)
            * score_scale
        )
        allowed = block_mask(row_start, block_rows, key_pos, length)
        probability = jnp.where(allowed, jnp.exp(scores - block_totals[..., None]), 0.0)
        rounded = probability.astype(jnp.bfloat16)
        grad_probs = jnp.einsum(
            "bgjd,kgd->gjbk", grad_block, value_rows, preferred_element_type=jnp.float32
        )
        row_delta = jnp.sum(probability * grad_probs, axis=-1, keepdims=True)
        grad_scores = (probability * (grad_probs - row_delta)).astype(jnp.bfloat16)
        grad_query = (
            jnp.einsum("gjbk,kgd->bgjd", grad_scores, key_rows, preferred_element_type=jnp.float32)
            * score_scale
        )
        grad_keys = (
            grad_keys
            + jnp.einsum(
                "gjbk,bgjd->kgd", grad_scores, query_block, preferred_element_type=jnp.float32
            )
            * score_scale
        )
        grad_values = grad_values + jnp.einsum(
            "gjbk,bgjd->kgd", rounded, grad_block, preferred_element_type=jnp.float32
        )
        return ((grad_keys, grad_values), grad_query)

    shape_tail = (queries.shape[1], queries.shape[2], queries.shape[3])
    query_blocks = queries.reshape((block_count, block_rows) + shape_tail)
    grad_blocks = grad_attended.reshape((block_count, block_rows) + shape_tail)
    starts = jnp.arange(block_count, dtype=jnp.int32) * block_rows
    empty = jnp.zeros(key_rows.shape, jnp.float32)
    (grad_keys, grad_values), grad_query = lax.scan(
        one_block, (empty, empty), (query_blocks, grad_blocks, log_totals, starts)
    )
    return (grad_query.reshape(queries.shape), grad_keys, grad_values)


def shards(
    tokens,
    cotangent,
    lengths,
    attn_gain,
    w_query,
    w_key,
    w_value,
    w_output,
    ffn_gain,
    w_gate,
    w_up,
    w_down,
):
    head_count = lax.axis_size("head")
    head_index = lax.axis_index("head")
    local_rows = tokens.shape[0]
    seq_rows = local_rows * head_count
    per_group = HQ // KVH
    group_width = per_group * HD
    query_width = 2 * group_width
    pair_width = 2 * HD
    hidden_width = w_gate.shape[1]
    first_group = jnp.where(head_index == 0, 0, head_index + 1)
    second_group = jnp.where(head_index == 0, 1, head_index + 1)
    second_live = jnp.where(head_index == 0, 1.0, 0.0).astype(jnp.float32)

    def take_columns(weight, group, width):
        return lax.dynamic_slice_in_dim(weight, group * width, width, 1)

    qkv_weight = jnp.concatenate(
        [
            take_columns(w_query, first_group, group_width),
            take_columns(w_query, second_group, group_width),
            take_columns(w_key, first_group, HD),
            take_columns(w_key, second_group, HD),
            take_columns(w_value, first_group, HD),
            take_columns(w_value, second_group, HD),
        ],
        axis=1,
    )
    out_weight = jnp.concatenate(
        [
            lax.dynamic_slice_in_dim(w_output, first_group * group_width, group_width, 0),
            lax.dynamic_slice_in_dim(w_output, second_group * group_width, group_width, 0),
        ],
        axis=0,
    )
    slot_scale = jnp.concatenate(
        [jnp.ones((group_width,), jnp.float32), jnp.ones((group_width,), jnp.float32) * second_live]
    )
    gate_up = jnp.concatenate([w_gate, w_up], axis=1)
    gain_one = attn_gain.astype(jnp.float32)
    gain_two = ffn_gain.astype(jnp.float32)
    cosine, sine_part = rope_tables(seq_rows, HD)
    length = lengths[0]
    row_valid = (head_index * local_rows + jnp.arange(local_rows, dtype=jnp.int32) < length).astype(
        jnp.float32
    )

    def spread(rows_low):
        return lax.all_gather(rows_low, "head", axis=0, tiled=True)

    def settle(term):
        return lax.psum_scatter(
            term(jnp.int32(0), local_rows * lax.axis_size("head")).astype(jnp.bfloat16),
            "head",
            scatter_dimension=0,
            tiled=True,
        ).astype(jnp.float32)

    def gather_grads(rows_low):
        return lax.all_gather(rows_low, "head", axis=0, tiled=True)

    def settle_grads(term):
        return lax.psum_scatter(
            term(jnp.int32(0), local_rows * lax.axis_size("head")).astype(jnp.bfloat16),
            "head",
            scatter_dimension=0,
            tiled=True,
        ).astype(jnp.float32)

    def layer_forward(residual):
        inv_one = lax.rsqrt(jnp.mean(residual * residual, axis=1, keepdims=True) + EPSILON)
        normed = spread((residual * inv_one * gain_one).astype(jnp.bfloat16))
        projected = jnp.dot(normed, qkv_weight, preferred_element_type=jnp.float32)
        queries = rotate(
            projected[:, :query_width].reshape(seq_rows, 2 * per_group, HD), cosine, sine_part
        )
        queries = queries.astype(jnp.bfloat16).reshape(seq_rows, 2, per_group, HD)
        key_rows = rotate(
            projected[:, query_width : query_width + pair_width].reshape(seq_rows, 2, HD),
            cosine,
            sine_part,
        ).astype(jnp.bfloat16)
        value_rows = (
            projected[:, query_width + pair_width :].reshape(seq_rows, 2, HD).astype(jnp.bfloat16)
        )
        attended, log_totals = attend(queries, key_rows, value_rows, length)
        attended = (attended * slot_scale).astype(jnp.bfloat16)
        attn_sum = settle(
            lambda row_start, amount: jnp.dot(
                attended, out_weight, preferred_element_type=jnp.float32
            )
        )
        middle = residual + attn_sum
        inv_two = lax.rsqrt(jnp.mean(middle * middle, axis=1, keepdims=True) + EPSILON)
        normed_two = spread((middle * inv_two * gain_two).astype(jnp.bfloat16))
        gate_and_up = jnp.dot(normed_two, gate_up, preferred_element_type=jnp.float32)
        gate_act = gate_and_up[:, :hidden_width]
        up_act = gate_and_up[:, hidden_width:]
        activated = (jax.nn.silu(gate_act) * up_act).astype(jnp.bfloat16)
        ffn_sum = settle(
            lambda row_start, amount: jnp.dot(activated, w_down, preferred_element_type=jnp.float32)
        )
        kept = (
            residual,
            inv_one,
            normed,
            queries,
            key_rows,
            value_rows,
            log_totals,
            attended,
            middle,
            inv_two,
            normed_two,
            gate_act,
            up_act,
            activated,
        )
        return (middle + ffn_sum, kept)

    def place_into(full, part, group, width):
        current = lax.dynamic_slice_in_dim(full, group * width, width, 1)
        return lax.dynamic_update_slice_in_dim(full, current + part, group * width, 1)

    def spread_groups(part, total_width, width):
        full = jnp.zeros((part.shape[0], total_width), jnp.float32)
        full = place_into(full, part[:, :width], first_group, width)
        return place_into(full, part[:, width:], second_group, width)

    def expand_slots(compact):
        qkv_part = compact[1]
        return (
            compact[0],
            spread_groups(qkv_part[:, :query_width], HQ * HD, group_width),
            spread_groups(qkv_part[:, query_width : query_width + pair_width], KVH * HD, HD),
            spread_groups(qkv_part[:, query_width + pair_width :], KVH * HD, HD),
            spread_groups(compact[2], HQ * HD, group_width),
            compact[3],
            compact[4],
            compact[5],
            compact[6],
        )

    def layer_backward(kept, grad_out):
        (
            residual,
            inv_one,
            normed,
            queries,
            key_rows,
            value_rows,
            log_totals,
            attended,
            middle,
            inv_two,
            normed_two,
            gate_act,
            up_act,
            activated,
        ) = kept
        grad_ffn = gather_grads(grad_out.astype(jnp.bfloat16))
        down_part = rows_product(grad_ffn, activated)
        grad_act = cols_product(grad_ffn, w_down)
        sigmoid_gate = jax.nn.sigmoid(gate_act)
        grad_gate = (
            grad_act * up_act * sigmoid_gate * (1.0 + gate_act * (1.0 - sigmoid_gate))
        ).astype(jnp.bfloat16)
        grad_up = (grad_act * (gate_act * sigmoid_gate)).astype(jnp.bfloat16)
        grad_pair = jnp.concatenate([grad_gate, grad_up], axis=1)
        gate_up_part = rows_product(normed_two, grad_pair)
        grad_norm_two = settle_grads(lambda row_start, amount: cols_product(grad_pair, gate_up))
        gain_two_part, grad_middle = norm_back(middle, inv_two, gain_two, grad_norm_two, grad_out)
        grad_attn = gather_grads(grad_middle.astype(jnp.bfloat16))
        output_part = rows_product(grad_attn, attended)
        grad_attended = (
            (cols_product(grad_attn, out_weight) * slot_scale)
            .astype(jnp.bfloat16)
            .reshape(seq_rows, 2, per_group, HD)
        )
        grad_query, grad_keys, grad_values = attend_back(
            queries, key_rows, value_rows, length, log_totals, grad_attended
        )
        grad_query = (
            unrotate(grad_query.reshape(seq_rows, 2 * per_group, HD), cosine, sine_part)
            .astype(jnp.bfloat16)
            .reshape(seq_rows, query_width)
        )
        grad_keys = (
            unrotate(grad_keys, cosine, sine_part)
            .astype(jnp.bfloat16)
            .reshape(seq_rows, pair_width)
        )
        grad_values = grad_values.astype(jnp.bfloat16).reshape(seq_rows, pair_width)
        grad_proj = jnp.concatenate([grad_query, grad_keys, grad_values], axis=1)
        qkv_part = rows_product(normed, grad_proj)
        grad_norm_one = settle_grads(lambda row_start, amount: cols_product(grad_proj, qkv_weight))
        gain_one_part, grad_in = norm_back(residual, inv_one, gain_one, grad_norm_one, grad_middle)
        partials = (
            gain_one_part,
            qkv_part,
            output_part,
            gain_two_part,
            gate_up_part[:, :hidden_width],
            gate_up_part[:, hidden_width:],
            down_part,
        )
        return (grad_in, partials)

    def reduce_grads(compact):
        full = expand_slots(compact)
        summed = (
            lax.psum_scatter(full[0], "dp", scatter_dimension=0, tiled=True),
            lax.psum_scatter(full[1], "dp", scatter_dimension=0, tiled=True),
            lax.psum_scatter(full[2], "dp", scatter_dimension=0, tiled=True),
            lax.psum_scatter(full[3], "dp", scatter_dimension=0, tiled=True),
            lax.psum_scatter(full[4], "dp", scatter_dimension=0, tiled=True),
            lax.psum_scatter(full[5], "dp", scatter_dimension=0, tiled=True),
            lax.psum_scatter(full[6], "dp", scatter_dimension=0, tiled=True),
            lax.psum_scatter(full[7], "dp", scatter_dimension=0, tiled=True),
            lax.psum_scatter(full[8], "dp", scatter_dimension=0, tiled=True),
        )
        across = (
            lax.psum(summed[0].astype(jnp.bfloat16), "head").astype(jnp.float32),
            lax.psum(summed[1].astype(jnp.bfloat16), "head").astype(jnp.float32),
            lax.psum(summed[2].astype(jnp.bfloat16), "head").astype(jnp.float32),
            lax.psum(summed[3].astype(jnp.bfloat16), "head").astype(jnp.float32),
            lax.psum(summed[4].astype(jnp.bfloat16), "head").astype(jnp.float32),
            lax.psum(summed[5].astype(jnp.bfloat16), "head").astype(jnp.float32),
        )
        return (
            across[0],
            across[1],
            across[2],
            across[3],
            across[4],
            across[5],
            summed[6],
            summed[7],
            summed[8],
        )

    inputs_high = tokens.astype(jnp.float32)
    first_out, kept_one = layer_forward(inputs_high)
    second_out, kept_two = layer_forward(first_out)
    grad_out = cotangent.astype(jnp.float32) * row_valid[:, None]
    kept_two = layer_forward(first_out)[1]
    grad_mid, partial_two = layer_backward(kept_two, grad_out)
    summed_two = reduce_grads(partial_two)
    kept_one = layer_forward(inputs_high)[1]
    grad_in, partial_one = layer_backward(kept_one, grad_mid)
    totals = tuple((left + right for left, right in zip(summed_two, reduce_grads(partial_one))))
    return (
        second_out.astype(jnp.bfloat16),
        grad_in,
        totals[0],
        totals[1],
        totals[2],
        totals[3],
        totals[4].T,
        totals[5],
        totals[6],
        totals[7],
        totals[8].T,
    )


def solution(mesh):
    return jax.shard_map(
        shards,
        mesh=mesh,
        in_specs=(
            P(("dp", "head"), None),
            P(("dp", "head"), None),
            P("dp"),
            P(),
            P(),
            P(),
            P(),
            P(),
            P(),
            P(None, "head"),
            P(None, "head"),
            P("head", None),
        ),
        out_specs=(
            P(("dp", "head"), None),
            P(("dp", "head"), None),
            P("dp"),
            P("dp", None),
            P("dp", None),
            P("dp", None),
            P(None, "dp"),
            P("dp"),
            P("dp", "head"),
            P("dp", "head"),
            P("head", "dp"),
        ),
        check_vma=False,
    )
```

profile of v0, /device:TPU:0, one launch (start us, length us, event | category | flops | bytes accessed | tf_op | source)
XLA Modules:
  0.0 1855.6 jit_solution(2401810063018089808)
XLA Ops:
  20.5 16.2 all-gather.11.cloned.1.call-done
  47.4 68.9 %while.84 = (s32[]{:T(128)}, f32[2,512,2,3,64]{1,0,4,3,2:T(2,128)}, s32[2]{0:T(128)}, s32[]{:T(128)}, bf16[2,512,2,3,64]{1,4,3,2,0:T(8,128)(2,1)}, /*index=5*/bf...) while((s32[]{:T(128)}, f32[2,512,2,3,64]{1,0,4,3,2:T(2,128)}, ...), condition=%wide.region_4.5_spmd.clone.clone, body=%wide.region_1.4_spmd.clone.clone.sunk | while | flops 825231872 | bytes 31095412 | solution.py:101
  50.4 9.8 fusion.368
  66.8 15.0 dynamic_update_slice.116
  84.8 9.8 fusion.368
  101.2 15.0 dynamic_update_slice.116
  127.8 59.1 %while.87 = (s32[]{:T(128)}, f32[2,512,2,3,64]{1,0,4,3,2:T(2,128)}, f32[2,2,3,512]{3,2,1,0:T(4,128)S(1)}, s32[2]{0:T(128)}, s32[]{:T(128)}, /*index=5*/bf16[2,51...) while((s32[]{:T(128)}, f32[2,512,2,3,64]{1,0,4,3,2:T(2,128)}, ...), condition=%wide.region_32.33_spmd.clone.clone, body=%wide.region_29.32_spmd.clone.clone.sunk | while | flops 844102144 | bytes 44812928 | solution.py:101
  142.3 15.0 dynamic_update_slice.121
  171.8 15.0 dynamic_update_slice.121
  197.2 30.6 %reduce-scatter.50.cloned.1.call-done = bf16[256,960]{0,1:T(8,128)(2,1)} async-done(((bf16[1024,960]{0,1:T(8,128)(2,1)}), bf16[256,960]{0,1:T(8,128)(2,1)}) %reduce-scatter.50.cloned.1.call-update) | async-done | bytes 491536 | tf_op jit(solution)/shard_map/reduce_scatter | solution.py:218
  237.1 17.0 all-gather.13.cloned.1.call-done
  262.6 30.7 %reduce-scatter.38.cloned.1.call-done = bf16[256,960]{0,1:T(8,128)(2,1)} async-done(((bf16[1024,960]{0,1:T(8,128)(2,1)}), bf16[256,960]{0,1:T(8,128)(2,1)}) %reduce-scatter.38.cloned.1.call-update) | async-done | bytes 491536 | tf_op jit(solution)/shard_map/reduce_scatter | solution.py:218
  296.3 22.2 %all-gather.15.cloned.1.call-done = bf16[1024,960]{0,1:T(8,128)(2,1)} async-done(((bf16[256,960]{0,1:T(8,128)(2,1)}), bf16[1024,960]{0,1:T(8,128)(2,1)}) %all-gather.15.cloned.1.call-update) | async-done | bytes 1966096 | tf_op jit(solution)/shard_map/all_gather | solution.py:215
  331.8 59.4 %while.86 = (s32[]{:T(128)}, f32[2,512,2,3,64]{1,0,4,3,2:T(2,128)}, f32[2,2,3,512]{3,2,1,0:T(4,128)S(1)}, s32[2]{0:T(128)}, s32[]{:T(128)}, /*index=5*/bf16[2,51...) while((s32[]{:T(128)}, f32[2,512,2,3,64]{1,0,4,3,2:T(2,128)}, ...), condition=%wide.region_19.20_spmd.clone.clone, body=%wide.region_16.19_spmd.clone.clone.sunk | while | flops 844102144 | bytes 44812928 | solution.py:101
  346.7 15.0 dynamic_update_slice.119
  376.2 15.0 dynamic_update_slice.119
  401.2 30.7 %reduce-scatter.44.cloned.1.call-done = bf16[256,960]{0,1:T(8,128)(2,1)} async-done(((bf16[1024,960]{0,1:T(8,128)(2,1)}), bf16[256,960]{0,1:T(8,128)(2,1)}) %reduce-scatter.44.cloned.1.call-update) | async-done | bytes 491536 | tf_op jit(solution)/shard_map/reduce_scatter | solution.py:218
  438.5 69.0 %while.85 = (s32[]{:T(128)}, f32[2,512,2,3,64]{1,0,4,3,2:T(2,128)}, s32[2]{0:T(128)}, s32[]{:T(128)}, bf16[2,512,2,3,64]{1,4,3,2,0:T(8,128)(2,1)}, /*index=5*/bf...) while((s32[]{:T(128)}, f32[2,512,2,3,64]{1,0,4,3,2:T(2,128)}, ...), condition=%wide.region_12.13_spmd.clone.clone, body=%wide.region_9.12_spmd.clone.clone.sunk | while | flops 825231872 | bytes 31095412 | solution.py:101
  441.6 9.9 fusion.374
  458.1 15.0 dynamic_update_slice.117
  476.0 9.8 fusion.374
  492.5 15.0 dynamic_update_slice.117
  517.8 7.6 fusion.276
  538.7 9.6 reduce-scatter.40.cloned.1.call-done
  548.3 33.4 %reduce-scatter.46.cloned.1.call-done = bf16[256,960]{0,1:T(8,128)(2,1)} async-done(((bf16[1024,960]{0,1:T(8,128)(2,1)}), bf16[256,960]{0,1:T(8,128)(2,1)}) %reduce-scatter.46.cloned.1.call-update) | async-done | bytes 491536 | tf_op jit(solution)/shard_map/reduce_scatter | solution.py:229
  585.6 22.2 %all-gather.23.cloned.1.call-done = bf16[1024,960]{0,1:T(8,128)(2,1)} async-done(((bf16[256,960]{0,1:T(8,128)(2,1)}), bf16[1024,960]{0,1:T(8,128)(2,1)}) %all-gather.23.cloned.1.call-update) | async-done | bytes 1966096 | tf_op jit(solution)/shard_map/all_gather | solution.py:226
  615.4 102.0 %while.88 = (s32[]{:T(128)}, f32[1024,2,64]{0,2,1:T(8,128)}, f32[1024,2,64]{0,2,1:T(8,128)}, f32[2,512,2,3,64]{1,0,4,3,2:T(2,128)}, bf16[2,512,2,3,64]{1,4,3,2,0...) while((s32[]{:T(128)}, f32[1024,2,64]{0,2,1:T(8,128)}, ...), condition=%wide.region_26.27_spmd.clone.clone, body=%wide.region_24.26_spmd.clone.clone.sunk | while | flops 2062350848 | bytes 186748176 | solution.py:148
  639.6 15.0 dynamic_update_slice.122
  690.3 15.0 dynamic_update_slice.122
  728.7 30.2 %reduce-scatter.48.cloned.1.call-done = bf16[256,960]{0,1:T(8,128)(2,1)} async-done(((bf16[1024,960]{0,1:T(8,128)(2,1)}), bf16[256,960]{0,1:T(8,128)(2,1)}) %reduce-scatter.48.cloned.1.call-update) | async-done | bytes 491536 | tf_op jit(solution)/shard_map/reduce_scatter | solution.py:229
  764.5 18.6 %all-gather.27.cloned.1.call-done = bf16[1024,960]{0,1:T(8,128)(2,1)} async-done(((bf16[256,960]{0,1:T(8,128)(2,1)}), bf16[1024,960]{0,1:T(8,128)(2,1)}) %all-gather.27.cloned.1.call-update) | async-done | bytes 1966096 | tf_op jit(solution)/shard_map/all_gather | solution.py:215
  783.1 7.6 fusion.277
  790.6 16.6 all-gather.25.cloned.1.call-done
  820.3 30.7 %reduce-scatter.52.cloned.1.call-done = bf16[256,960]{0,1:T(8,128)(2,1)} async-done(((bf16[1024,960]{0,1:T(8,128)(2,1)}), bf16[256,960]{0,1:T(8,128)(2,1)}) %reduce-scatter.52.cloned.1.call-update) | async-done | bytes 491536 | tf_op jit(solution)/shard_map/reduce_scatter | solution.py:229
  933.4 101.2 %while.89 = (s32[]{:T(128)}, f32[1024,2,64]{0,2,1:T(8,128)S(1)}, f32[1024,2,64]{0,2,1:T(8,128)}, f32[2,512,2,3,64]{1,0,4,3,2:T(2,128)}, bf16[2,512,2,3,64]{1,4,3...) while((s32[]{:T(128)}, f32[1024,2,64]{0,2,1:T(8,128)S(1)}, ...), condition=%wide.region_39.40_spmd.clone.clone, body=%wide.region_37.39_spmd.clone.clone.sunk | while | flops 2062350848 | bytes 187796784 | solution.py:148
  957.7 15.0 dynamic_update_slice.123
  1008.1 15.0 dynamic_update_slice.123
  1133.8 76.3 %reduce-scatter.56.cloned.1.call-done = f32[120,960]{1,0:T(8,128)} async-done(((f32[960,960]{1,0:T(8,128)}), f32[120,960]{1,0:T(8,128)}) %reduce-scatter.56.cloned.1.call-update) | async-done | bytes 460816 | tf_op jit(solution)/shard_map/reduce_scatter | solution.py:379
  1211.8 64.5 %reduce-scatter.70.cloned.1.call-done = f32[120,320]{1,0:T(8,128)} async-done(((f32[960,320]{1,0:T(8,128)}), f32[120,320]{1,0:T(8,128)}) %reduce-scatter.70.cloned.1.call-update) | async-done | bytes 153616
  1277.9 63.8 %reduce-scatter.66.cloned.1.call-done = f32[120,320]{1,0:T(8,128)} async-done(((f32[960,320]{1,0:T(8,128)}), f32[120,320]{1,0:T(8,128)}) %reduce-scatter.66.cloned.1.call-update) | async-done | bytes 153616
  1343.3 85.5 %reduce-scatter.62.cloned.1.call-done = f32[120,960]{1,0:T(8,128)} async-done(((f32[960,960]{1,0:T(8,128)}), f32[120,960]{1,0:T(8,128)}) %reduce-scatter.62.cloned.1.call-update) | async-done | bytes 460816 | tf_op jit(solution)/shard_map/reduce_scatter | solution.py:382
  1430.5 86.3 %reduce-scatter.58.cloned.1.call-done = f32[120,960]{1,0:T(8,128)} async-done(((f32[960,960]{1,0:T(8,128)}), f32[120,960]{1,0:T(8,128)}) %reduce-scatter.58.cloned.1.call-update) | async-done | bytes 460816 | tf_op jit(solution)/shard_map/reduce_scatter | solution.py:379
  1542.2 7.3 reduce-scatter.42.cloned.1.call-done
  1551.6 31.3 %reduce-scatter.54.cloned.1.call-done = bf16[256,960]{0,1:T(8,128)(2,1)} async-done(((bf16[1024,960]{0,1:T(8,128)(2,1)}), bf16[256,960]{0,1:T(8,128)(2,1)}) %reduce-scatter.54.cloned.1.call-update) | async-done | bytes 491536 | tf_op jit(solution)/shard_map/reduce_scatter | solution.py:229
  1584.5 37.1 %all-reduce.12 = (bf16[960]{0:T(1024)(128)(2,1)S(1)}, bf16[960]{0:T(1024)(128)(2,1)S(1)}, bf16[960]{0:T(1024)(128)(2,1)S(1)}, bf16[960]{0:T(1024)(128)(2,1)S(1)}) all-reduce(f32[960]{0:T(1024)S(1)} %get-tuple-element.798, f32[960]{0:T(1024)S(1)} %copy-done.91, ...), channel_id=16, replica_groups=mesh['dp'=8,'head'=4] {'dp'}, use_global_device_ids=true, to_apply=%region_46.47.clone | all-reduce | flops 3840 | bytes 23040
  1637.7 64.3 %reduce-scatter.72.cloned.1.call-done = f32[120,640]{1,0:T(8,128)} async-done(((f32[960,640]{1,0:T(8,128)}), f32[120,640]{1,0:T(8,128)}) %reduce-scatter.72.cloned.1.call-update) | async-done | bytes 307216
  1701.9 73.2 %reduce-scatter.74.cloned.1.call-done = f32[120,640]{1,0:T(8,128)} async-done(((f32[960,640]{1,0:T(8,128)}), f32[120,640]{1,0:T(8,128)}) %reduce-scatter.74.cloned.1.call-update) | async-done | bytes 307216
  1775.1 73.5 %reduce-scatter.76.cloned.1.call-done = f32[120,640]{1,0:T(8,128)} async-done(((f32[960,640]{1,0:T(8,128)}), f32[120,640]{1,0:T(8,128)}) %reduce-scatter.76.cloned.1.call-update) | async-done | bytes 307216
  (621 shorter events, 629.7 us)
Async XLA Ops:
  7.2 252.2 %copy-start = (bf16[640,960]{0,1:T(8,128)(2,1)S(1)}, bf16[640,960]{0,1:T(8,128)(2,1)}, u32[]{:S(2)}) copy-start(bf16[640,960]{0,1:T(8,128)(2,1)} %param.35) | copy-start | bytes 3686404
  7.2 29.5 %all-gather.11.cloned.1.call-start = ((), (), s32[]{:S(2)}) async-start(), calls=%async_computation.21 | async-start | bytes 2457600 | tf_op jit(solution)/shard_map/all_gather | solution.py:215
  11.8 185.4 %reduce-scatter.36.cloned.1.call-start = ((), (), s32[]{:S(2)}) async-start(), calls=%async_computation.22 | async-start | bytes 2457600 | tf_op jit(solution)/shard_map/reduce_scatter | solution.py:218
  19.9 173.1 %copy-start.26 = (bf16[192,960]{1,0:T(8,128)(2,1)}, bf16[192,960]{1,0:T(8,128)(2,1)S(1)}, u32[]{:S(2)}) copy-start(bf16[192,960]{1,0:T(8,128)(2,1)S(1)} %get-tuple-element.953) | copy-start | bytes 1105924
  19.9 173.1 %copy-start.30 = (bf16[192,960]{1,0:T(8,128)(2,1)}, bf16[192,960]{1,0:T(8,128)(2,1)S(1)}, u32[]{:S(2)}) copy-start(bf16[192,960]{1,0:T(8,128)(2,1)S(1)} %get-tuple-element.954) | copy-start | bytes 1105924
  126.2 101.7 %reduce-scatter.50.cloned.1.call-start = ((), (), s32[]{:S(2)}) async-start(), calls=%async_computation.35 | async-start | bytes 2457600 | tf_op jit(solution)/shard_map/reduce_scatter | solution.py:218
  197.1 57.0 %all-gather.13.cloned.1.call-start = ((), (), s32[]{:S(2)}) async-start(), calls=%async_computation.23 | async-start | bytes 2457600 | tf_op jit(solution)/shard_map/all_gather | solution.py:215
  231.8 61.5 %reduce-scatter.38.cloned.1.call-start = ((), (), s32[]{:S(2)}) async-start(), calls=%async_computation.24 | async-start | bytes 2457600 | tf_op jit(solution)/shard_map/reduce_scatter | solution.py:218
  262.6 56.0 %all-gather.15.cloned.1.call-start = ((), (), s32[]{:S(2)}) async-start(), calls=%async_computation.25 | async-start | bytes 2457600 | tf_op jit(solution)/shard_map/all_gather | solution.py:215
  294.6 289.6 %copy-start.5 = (f32[256,960]{0,1:T(8,128)}, f32[256,960]{0,1:T(8,128)S(1)}, u32[]{:S(2)}) copy-start(f32[256,960]{0,1:T(8,128)S(1)} %get-tuple-element.926) | copy-start | bytes 2949124
  296.3 135.6 %reduce-scatter.44.cloned.1.call-start = ((), (), s32[]{:S(2)}) async-start(), calls=%async_computation.29 | async-start | bytes 2457600 | tf_op jit(solution)/shard_map/reduce_scatter | solution.py:218
  401.1 116.7 %all-gather.21.cloned.1.call-start = ((), (), s32[]{:S(2)}) async-start(), calls=%async_computation.31 | async-start | bytes 2457600 | tf_op jit(solution)/shard_map/all_gather | solution.py:215
  435.2 90.2 %all-gather.19.cloned.1.call-start = ((), (), s32[]{:S(2)}) async-start(), calls=%async_computation.30 | async-start | bytes 2457600 | tf_op jit(solution)/shard_map/all_gather | solution.py:226
  436.8 111.5 %reduce-scatter.40.cloned.1.call-start = ((), (), s32[]{:S(2)}) async-start(), calls=%async_computation.26 | async-start | bytes 2457600 | tf_op jit(solution)/shard_map/reduce_scatter | solution.py:218
  517.5 64.2 %reduce-scatter.46.cloned.1.call-start = ((), (), s32[]{:S(2)}) async-start(), calls=%async_computation.32 | async-start | bytes 2457600 | tf_op jit(solution)/shard_map/reduce_scatter | solution.py:229
  532.9 48.9 %copy-start.16 = (bf16[256,960]{0,1:T(8,128)(2,1)S(1)}, bf16[256,960]{0,1:T(8,128)(2,1)}, u32[]{:S(2)}) copy-start(bf16[256,960]{0,1:T(8,128)(2,1)} %reduce-scatter.44.cloned.1.call-done) | copy-start | bytes 1474564
  532.9 48.9 %copy-start.64 = (f32[960]{0:T(1024)S(1)}, f32[960]{0:T(1024)}, u32[]{:S(2)}) copy-start(f32[960]{0:T(1024)} %copy-done.62) | copy-start | bytes 11524
  532.9 48.9 %copy-start.88 = (f32[256]{0:T(256)S(1)}, f32[256]{0:T(256)}, u32[]{:S(2)}) copy-start(f32[256]{0:T(256)} %copy-done.87) | copy-start | bytes 3076
  538.6 45.7 %copy-start.96 = (f32[256]{0:T(256)S(1)}, f32[256]{0:T(256)}, u32[]{:S(2)}) copy-start(f32[256]{0:T(256)} %copy-done.95) | copy-start | bytes 3076
  538.6 69.1 %copy-start.81 = (f32[384]{0:T(512)S(1)}, f32[384]{0:T(512)}, u32[]{:S(2)}) copy-start(f32[384]{0:T(512)} %concatenate.75) | copy-start | bytes 4612
  538.6 69.1 %all-gather.23.cloned.1.call-start = ((), (), s32[]{:S(2)}) async-start(), calls=%async_computation.33 | async-start | bytes 2457600 | tf_op jit(solution)/shard_map/all_gather | solution.py:226
  585.5 173.4 %reduce-scatter.48.cloned.1.call-start = ((), (), s32[]{:S(2)}) async-start(), calls=%async_computation.34 | async-start | bytes 2457600 | tf_op jit(solution)/shard_map/reduce_scatter | solution.py:229
  728.1 55.0 %all-gather.27.cloned.1.call-start = ((), (), s32[]{:S(2)}) async-start(), calls=%async_computation.37 | async-start | bytes 2457600 | tf_op jit(solution)/shard_map/all_gather | solution.py:215
  728.6 78.6 %all-gather.25.cloned.1.call-start = ((), (), s32[]{:S(2)}) async-start(), calls=%async_computation.36 | async-start | bytes 2457600 | tf_op jit(solution)/shard_map/all_gather | solution.py:226
  764.4 86.6 %reduce-scatter.52.cloned.1.call-start = ((), (), s32[]{:S(2)}) async-start(), calls=%async_computation.38 | async-start | bytes 2457600 | tf_op jit(solution)/shard_map/reduce_scatter | solution.py:229
  820.3 105.6 %all-gather.29.cloned.1.call-start = ((), (), s32[]{:S(2)}) async-start(), calls=%async_computation.39 | async-start | bytes 2457600 | tf_op jit(solution)/shard_map/all_gather | solution.py:226
  855.9 252.8 %all-gather.17.cloned.1.call-start = ((), (), s32[]{:S(2)}) async-start(), calls=%async_computation.27 | async-start | bytes 2457600 | tf_op jit(solution)/shard_map/all_gather | solution.py:215
  856.5 272.1 %reduce-scatter.68.cloned.1.call-start = ((), (), s32[]{:S(2)}) async-start(), calls=%async_computation.47 | async-start | bytes 1658880
  878.3 251.9 %reduce-scatter.64.cloned.1.call-start = ((), (), s32[]{:S(2)}) async-start(), calls=%async_computation.45 | async-start | bytes 1658880
  885.7 246.2 %reduce-scatter.60.cloned.1.call-start = ((), (), s32[]{:S(2)}) async-start(), calls=%async_computation.43 | async-start | bytes 4423680 | tf_op jit(solution)/shard_map/reduce_scatter | solution.py:382
  907.3 302.7 %reduce-scatter.56.cloned.1.call-start = ((), (), s32[]{:S(2)}) async-start(), calls=%async_computation.41 | async-start | bytes 4423680 | tf_op jit(solution)/shard_map/reduce_scatter | solution.py:379
  925.8 350.5 %reduce-scatter.70.cloned.1.call-start = ((), (), s32[]{:S(2)}) async-start(), calls=%async_computation.48 | async-start | bytes 1658880
  1065.5 276.2 %reduce-scatter.66.cloned.1.call-start = ((), (), s32[]{:S(2)}) async-start(), calls=%async_computation.46 | async-start | bytes 1658880
  1069.6 359.2 %reduce-scatter.62.cloned.1.call-start = ((), (), s32[]{:S(2)}) async-start(), calls=%async_computation.44 | async-start | bytes 4423680 | tf_op jit(solution)/shard_map/reduce_scatter | solution.py:382
  1091.2 425.6 %reduce-scatter.58.cloned.1.call-start = ((), (), s32[]{:S(2)}) async-start(), calls=%async_computation.42 | async-start | bytes 4423680 | tf_op jit(solution)/shard_map/reduce_scatter | solution.py:379
  1108.4 441.1 %reduce-scatter.42.cloned.1.call-start = ((), (), s32[]{:S(2)}) async-start(), calls=%async_computation.28 | async-start | bytes 2457600 | tf_op jit(solution)/shard_map/reduce_scatter | solution.py:218
  1117.3 465.6 %reduce-scatter.54.cloned.1.call-start = ((), (), s32[]{:S(2)}) async-start(), calls=%async_computation.40 | async-start | bytes 2457600 | tf_op jit(solution)/shard_map/reduce_scatter | solution.py:229
  1121.3 510.7 %all-reduce.17.cloned.1.call-start = ((), (), s32[]{:S(2)}) async-start(), calls=%async_computation.52 | async-start | bytes 2703360 | tf_op jit(solution)/shard_map/psum | solution.py:390
  1130.2 388.4 %copy-start.108 = (bf16[1024,960]{0,1:T(8,128)(2,1)S(1)}, bf16[1024,960]{0,1:T(8,128)(2,1)}, u32[]{:S(2)}) copy-start(bf16[1024,960]{0,1:T(8,128)(2,1)} %all-gather.27.cloned.1.call-done) | copy-start | bytes 5898244
  1518.5 183.4 %reduce-scatter.72.cloned.1.call-start = ((), (), s32[]{:S(2)}) async-start(), calls=%async_computation.49 | async-start | bytes 2764800
  1528.6 246.5 %reduce-scatter.74.cloned.1.call-start = ((), (), s32[]{:S(2)}) async-start(), calls=%async_computation.50 | async-start | bytes 2764800
  1529.3 319.3 %reduce-scatter.76.cloned.1.call-start = ((), (), s32[]{:S(2)}) async-start(), calls=%async_computation.51 | async-start | bytes 2764800
  1540.8 43.7 %copy-start.90 = (f32[960]{0:T(1024)S(1)}, f32[960]{0:T(1024)}, u32[]{:S(2)}) copy-start(f32[960]{0:T(1024)} %get-tuple-element.792) | copy-start | bytes 11524
  1540.8 43.7 %copy-start.91 = (f32[960]{0:T(1024)S(1)}, f32[960]{0:T(1024)}, u32[]{:S(2)}) copy-start(f32[960]{0:T(1024)} %get-tuple-element.796) | copy-start | bytes 11524
  1540.8 88.2 %copy-start.15 = (bf16[256,960]{0,1:T(8,128)(2,1)S(1)}, bf16[256,960]{0,1:T(8,128)(2,1)}, u32[]{:S(2)}) copy-start(bf16[256,960]{0,1:T(8,128)(2,1)} %reduce-scatter.50.cloned.1.call-done) | copy-start | bytes 1474564
  1540.9 88.2 %copy-start.66 = (f32[960]{0:T(1024)S(1)}, f32[960]{0:T(1024)}, u32[]{:S(2)}) copy-start(f32[960]{0:T(1024)} %copy-done.62) | copy-start | bytes 11524
  1540.9 88.2 %copy-start.86 = (f32[256]{0:T(256)S(1)}, f32[256]{0:T(256)}, u32[]{:S(2)}) copy-start(f32[256]{0:T(256)} %copy-done.84) | copy-start | bytes 3076
  1540.9 88.2 %copy-start.101 = (f32[256]{0:T(256)S(1)}, f32[256]{0:T(256)}, u32[]{:S(2)}) copy-start(f32[256]{0:T(256)} %copy-done.100) | copy-start | bytes 3076
  (110 other events, 1202.4 us)
Sparse Core Ops, SparseCore 0:
  11.9 24.7 all-gather.10
  126.3 30.6 reduce-scatter.35
  197.2 30.5 reduce-scatter.49
  232.0 22.0 all-gather.12
  262.7 30.6 reduce-scatter.37
  296.4 22.0 all-gather.14
  401.2 30.6 reduce-scatter.43
  435.3 22.0 all-gather.20
  459.6 22.0 all-gather.18
  517.6 30.6 reduce-scatter.39
  551.1 30.6 reduce-scatter.45
  585.6 22.0 all-gather.22
  728.2 30.6 reduce-scatter.47
  760.9 22.0 all-gather.26
  785.1 22.0 all-gather.24
  820.4 30.6 reduce-scatter.51
  856.1 22.0 all-gather.28
  880.2 22.0 all-gather.16
  905.8 63.1 reduce-scatter.67
  972.3 62.5 reduce-scatter.63
  1038.5 83.2 reduce-scatter.59
  1126.0 84.0 reduce-scatter.55
  1213.6 62.7 reduce-scatter.69
  1279.7 61.9 reduce-scatter.65
  1345.4 83.3 reduce-scatter.61
  1432.7 84.0 reduce-scatter.57
  1519.2 30.2 reduce-scatter.41
  1552.2 30.6 reduce-scatter.53
  1586.4 41.1 all-reduce.16
  1632.1 69.8 reduce-scatter.71
  1706.6 68.4 reduce-scatter.73
  1779.7 68.8 reduce-scatter.75
where the time goes:
time: 1880 us; the launch traced here: 1860 us
  waiting for transfers between devices  937 us (50%)
  local copies, waits for them, and re-layouts  394 us (21%)
  matrix products  311 us (17%)
  other arithmetic  149 us (8%)
  blocking collectives  43.2 us (2%)
    unnamed x39, waiting for transfers between devices  341 us
    dynamic_update_slice x24, local copies, waits for them, and re-layouts, attend(): attended, log_totals = lax.map(one_block, (query_blocks, starts))  190 us
    reduce_scatter x2, waiting for transfers between devices, reduce_grads(): lax.psum_scatter(full[1], 'dp', scatter_dimension=0, tiled=True)  163 us
    reduce_scatter x4, waiting for transfers between devices, settle_grads(): lax.psum_scatter(term(jnp.int32(0), local_rows * lax.axis_size('head')).a...  126 us
    reduce_scatter x6, waiting for transfers between devices, settle(): lax.psum_scatter(term(jnp.int32(0), local_rows * lax.axis_size('head')).a...  109 us
    dynamic_update_slice x16, local copies, waits for them, and re-layouts, place_into(): lax.dynamic_update_slice_in_dim(full, current + part, group * width, 1)  87.5 us
    reduce_scatter x2, waiting for transfers between devices, reduce_grads(): lax.psum_scatter(full[4], 'dp', scatter_dimension=0, tiled=True)  85.5 us
    all_gather x6, waiting for transfers between devices, spread(): return lax.all_gather(rows_low, 'head', axis=0, tiled=True)  74 us
  transfers between devices with their start and end apart: 32, of which 23 were waited for; matrix products, arithmetic and copies ran while one was open for 27% of the time, Pallas kernels for 0%

commit v1 on v0

v1 whole, which is shorter than its diff:
```python
import functools

import jax
import jax.numpy as jnp
from jax import lax
from jax.experimental import pallas as pl
from jax.experimental.pallas import tpu as pltpu
from jax.sharding import PartitionSpec as P

HQ = 15
KVH = 5
HD = 64
HALF = HD // 2
PER_GROUP = HQ // KVH
KV_WIDTH = KVH * HD
EPSILON = 1e-05
SCALE = HD ** (-0.5)
BLOCKED = -1e30
LOW = jnp.bfloat16
HIGH = jnp.float32
VMEM = pl.BlockSpec(memory_space=pltpu.VMEM)
SMEM = pl.BlockSpec(memory_space=pltpu.SMEM)
ANY = pl.BlockSpec(memory_space=pl.ANY)
LIMIT = 58 * 2**20


def nn(left, right):
    return lax.dot_general(left, right, (((1,), (0,)), ((), ())), preferred_element_type=HIGH)


def nt(left, right):
    return lax.dot_general(left, right, (((1,), (1,)), ((), ())), preferred_element_type=HIGH)


def sigmoid(value):
    return 0.5 * (1.0 + jnp.tanh(0.5 * value))


def inverse_rms(rows):
    return lax.rsqrt(jnp.mean(rows * rows, axis=1, keepdims=True) + EPSILON)


def norm_back(values_in, gain, grad_normed, grad_skip):
    inverse = inverse_rms(values_in)
    normal = values_in * inverse
    gain_part = jnp.sum(grad_normed * normal, axis=0, keepdims=True)
    scaled = grad_normed * gain
    back = grad_skip + inverse * (scaled - normal * jnp.mean(scaled * normal, axis=1, keepdims=True))
    return gain_part, back


def turned(columns, cosine, sine, sign, factor):
    parts = []
    for start in range(0, columns.shape[0], HD):
        first = columns[start : start + HALF] * factor
        second = columns[start + HALF : start + HD] * factor
        parts.append(first * cosine - sign * second * sine)
        parts.append(second * cosine + sign * first * sine)
    return jnp.concatenate(parts, axis=0)


def project(hidden, gain, w_query, w_key, w_value, cosine, sine, a_ref, q_ref, kv_ref):
    normed = hidden * inverse_rms(hidden) * gain
    a_ref[...] = normed.T.astype(LOW)
    normed = normed.astype(LOW)
    queries = nn(normed, w_query[...]).T
    q_ref[...] = turned(queries, cosine, sine, 1.0, SCALE).astype(LOW)
    keys = turned(nn(normed, w_key[...]).T, cosine, sine, 1.0, 1.0)
    kv_ref[:, :KV_WIDTH] = keys.T.astype(LOW)
    kv_ref[:, KV_WIDTH:] = nn(normed, w_value[...]).astype(LOW)


def fill_bias(where_ref, bias, rows, blocks):
    me = where_ref[0]
    length = where_ref[1]
    key = lax.broadcasted_iota(jnp.int32, (rows, rows), 0)
    query = lax.broadcasted_iota(jnp.int32, (rows, rows), 1)
    for step in range(blocks):
        other = jnp.bitwise_xor(me, step)
        allowed = other * rows + key < length
        if step == 0:
            allowed &= key <= query
        else:
            allowed &= other < me
        bias[step * rows : (step + 1) * rows] = jnp.where(allowed, 0.0, BLOCKED)


def weights_in(sources, holders, sems):
    copies = []
    for which, (source, holder) in enumerate(zip(sources, holders)):
        for step in range(len(source)):
            copies.append(pltpu.make_async_copy(source[step], holder.at[step], sems.at[which, step]))
    return copies


def qkv_kernel(h_ref, gain_ref, wq_ref, wk_ref, wv_ref, cos_ref, sin_ref, a_ref, q_ref, kv_ref):
    hidden = h_ref[...].astype(HIGH)
    gain = gain_ref[...].astype(HIGH)
    project(hidden, gain, wq_ref, wk_ref, wv_ref, cos_ref[...], sin_ref[...], a_ref, q_ref, kv_ref)


def forward_kernel(last, blocks, *refs):
    where_ref, h_ref, q_ref = refs[:3]
    kv_refs = refs[3 : 3 + blocks]
    refs = refs[3 + blocks :]
    wo_ref, gain_two_ref = refs[:2]
    wg_any, wu_any, wd_any = (refs[2 + i * blocks : 2 + (i + 1) * blocks] for i in range(3))
    refs = refs[2 + 3 * blocks :]
    if not last:
        gain_one_ref, wq_ref, wk_ref, wv_ref, cos_ref, sin_ref = refs[:6]
        refs = refs[6:]
    o_ref, lse_ref, m_ref, b_ref, g_ref, u_ref, out_ref = refs[:7]
    refs = refs[7:]
    if not last:
        next_a, next_q, next_kv = refs[:3]
        refs = refs[3:]
    bias, k_sc, vt_sc, wg, wu, wd, sems = refs
    rows = h_ref.shape[0]
    copies = weights_in((wg_any, wu_any, wd_any), (wg, wu, wd), sems)
    for step in range(blocks):
        for which in range(3):
            copies[which * blocks + step].start()
    fill_bias(where_ref, bias, rows, blocks)
    for step in range(blocks):
        held = kv_refs[step][...]
        for group in range(KVH):
            k_sc[group, step * rows : (step + 1) * rows] = held[:, group * HD : (group + 1) * HD]
        vt_sc[:, step * rows : (step + 1) * rows] = held[:, KV_WIDTH:].T

    def group_body(group, carry):
        keys = k_sc[group]
        values = vt_sc[pl.ds(pl.multiple_of(group * HD, HD), HD), :]
        for member in range(PER_GROUP):
            head = group * PER_GROUP + member
            at = pl.ds(pl.multiple_of(head * HD, HD), HD)
            scores = nn(keys, q_ref[at, :]) + bias[...]
            top = jnp.max(scores, axis=0, keepdims=True)
            exponent = jnp.exp(scores - top)
            total = jnp.sum(exponent, axis=0, keepdims=True)
            attended = nn(values, exponent.astype(LOW)) * (1.0 / total)
            o_ref[at, :] = attended.astype(LOW)
            lse_ref[pl.ds(head, 1), :] = top + jnp.log(total)
        return carry

    lax.fori_loop(0, KVH, group_body, 0)
    attended = o_ref[...].T
    middle = h_ref[...].astype(HIGH) + nn(attended, wo_ref[...])
    m_ref[...] = middle
    normed = middle * inverse_rms(middle) * gain_two_ref[...].astype(HIGH)
    b_ref[...] = normed.T.astype(LOW)
    normed = normed.astype(LOW)
    total = middle
    for step in range(blocks):
        copies[step].wait()
        gate = nn(normed, wg[step])
        copies[blocks + step].wait()
        up = nn(normed, wu[step])
        g_ref[step] = gate.astype(LOW)
        u_ref[step] = up.astype(LOW)
        active = (gate * sigmoid(gate) * up).astype(LOW)
        copies[2 * blocks + step].wait()
        total = total + nn(active, wd[step])
    if last:
        out_ref[...] = total.astype(LOW)
    else:
        out_ref[...] = total
        gain_one = gain_one_ref[...].astype(HIGH)
        project(total, gain_one, wq_ref, wk_ref, wv_ref, cos_ref[...], sin_ref[...], next_a, next_q, next_kv)


def backward_kernel(first, blocks, *refs):
    where_ref, e_ref, g_ref, u_ref, m_ref, gain_ref, wo_ref, q_ref = refs[:8]
    kv_refs = refs[8 : 8 + blocks]
    refs = refs[8 + blocks :]
    o_ref, lse_ref, cos_ref, sin_ref = refs[:4]
    wg_any, wu_any, wd_any = (refs[4 + i * blocks : 4 + (i + 1) * blocks] for i in range(3))
    refs = refs[4 + 3 * blocks :]
    f_ref, mine_ref, theirs_ref, c_ref, dm_ref, dq_ref, dkv_ref, gain_part_ref = refs[:8]
    bias, k_sc, v_sc, kt_sc, do_sc, delta, wg, wu, wd, sems = refs[8:]
    rows = m_ref.shape[0]
    copies = weights_in((wg_any, wu_any, wd_any), (wg, wu, wd), sems)
    for step in range(blocks):
        for which in (2, 0, 1):
            copies[which * blocks + step].start()
    fill_bias(where_ref, bias, rows, blocks)
    for step in range(blocks):
        held = kv_refs[step][...]
        for group in range(KVH):
            at = slice(step * rows, (step + 1) * rows)
            k_sc[group, at] = held[:, group * HD : (group + 1) * HD]
            v_sc[group, at] = held[:, KV_WIDTH + group * HD : KV_WIDTH + (group + 1) * HD]
        kt_sc[:, step * rows : (step + 1) * rows] = held[:, :KV_WIDTH].T
    grad = e_ref[...].astype(HIGH)
    if first:
        row = where_ref[0] * rows + lax.broadcasted_iota(jnp.int32, (rows, 1), 0)
        grad = jnp.where(row < where_ref[1], grad, 0.0)
    f_ref[...] = grad.T.astype(LOW)
    low_grad = grad.astype(LOW)
    grad_normed = jnp.zeros(m_ref.shape, HIGH)
    for step in range(blocks):
        copies[2 * blocks + step].wait()
        grad_active = nt(low_grad, wd[step])
        gate = g_ref[step].astype(HIGH)
        up = u_ref[step].astype(HIGH)
        sig = sigmoid(gate)
        silu = gate * sig
        grad_gate = (grad_active * up * sig * (1.0 + gate * (1.0 - sig))).astype(LOW)
        grad_up = (grad_active * silu).astype(LOW)
        kept = mine_ref if step % 2 == 0 else theirs_ref
        kept[step // 2] = grad_gate
        kept[2 + step // 2] = grad_up
        kept[4 + step // 2] = (silu * up).astype(LOW)
        copies[step].wait()
        copies[blocks + step].wait()
        grad_normed = grad_normed + nt(grad_gate, wg[step]) + nt(grad_up, wu[step])
    gain_part, grad_middle = norm_back(m_ref[...], gain_ref[...].astype(HIGH), grad_normed, grad)
    gain_part_ref[...] = gain_part
    dm_ref[...] = grad_middle
    c_ref[...] = grad_middle.T.astype(LOW)
    do_sc[...] = nt(wo_ref[...], grad_middle.astype(LOW)).astype(LOW)
    for head in range(HQ):
        at = slice(head * HD, (head + 1) * HD)
        product = do_sc[at].astype(HIGH) * o_ref[at].astype(HIGH)
        delta[head : head + 1] = jnp.sum(product, axis=0, keepdims=True)
    cosine = cos_ref[...]
    sine = sin_ref[...]

    def group_body(group, carry):
        keys = k_sc[group]
        values = v_sc[group]
        keys_t = kt_sc[pl.ds(pl.multiple_of(group * HD, HD), HD), :]
        grad_keys = jnp.zeros((HD, blocks * rows), HIGH)
        grad_values = jnp.zeros((HD, blocks * rows), HIGH)
        for member in range(PER_GROUP):
            head = group * PER_GROUP + member
            at = pl.ds(pl.multiple_of(head * HD, HD), HD)
            query = q_ref[at, :]
            grad_out = do_sc[at, :]
            scores = nn(keys, query) + bias[...]
            prob = jnp.exp(scores - lse_ref[pl.ds(head, 1), :])
            grad_prob = nn(values, grad_out)
            grad_score = (prob * (grad_prob - delta[pl.ds(head, 1), :])).astype(LOW)
            dq_ref[at, :] = turned(nn(keys_t, grad_score), cosine, sine, -1.0, SCALE).astype(LOW)
            grad_keys = grad_keys + nt(query, grad_score)
            grad_values = grad_values + nt(grad_out, prob.astype(LOW))
        at = pl.ds(pl.multiple_of(group * HD, HD), HD)
        after = pl.ds(pl.multiple_of(KV_WIDTH + group * HD, HD), HD)
        for step in range(blocks):
            cut = slice(step * rows, (step + 1) * rows)
            dkv_ref[step, at, :] = grad_keys[:, cut].astype(LOW)
            dkv_ref[step, after, :] = grad_values[:, cut].astype(LOW)
        return carry

    lax.fori_loop(0, KVH, group_body, 0)


def close_kernel(parts, *refs):
    h_ref, gain_ref, dm_ref, dq_ref, wq_ref, wk_ref, wv_ref, cos_ref, sin_ref = refs[:9]
    part_refs = refs[9 : 9 + parts]
    dh_ref, dkv_ref, gain_part_ref = refs[9 + parts :]
    total = part_refs[0][...].astype(HIGH)
    for part in part_refs[1:]:
        total = total + part[...].astype(HIGH)
    dkv_ref[:KV_WIDTH] = turned(total[:KV_WIDTH], cos_ref[...], sin_ref[...], -1.0, 1.0).astype(LOW)
    dkv_ref[KV_WIDTH:] = total[KV_WIDTH:].astype(LOW)
    grad_normed = nn(wq_ref[...], dq_ref[...])
    grad_normed = grad_normed + nn(wk_ref[...], dkv_ref[:KV_WIDTH])
    grad_normed = grad_normed + nn(wv_ref[...], dkv_ref[KV_WIDTH:])
    gain_part, grad_in = norm_back(
        h_ref[...].astype(HIGH), gain_ref[...].astype(HIGH), grad_normed.T, dm_ref[...]
    )
    gain_part_ref[...] = gain_part
    dh_ref[...] = grad_in


def call(body, outs, specs, scratch, name):
    return pl.pallas_call(
        body,
        out_shape=[jax.ShapeDtypeStruct(shape, kind) for shape, kind in outs],
        in_specs=specs,
        out_specs=[VMEM] * len(outs),
        scratch_shapes=scratch,
        compiler_params=pltpu.CompilerParams(vmem_limit_bytes=LIMIT),
        name=name,
    )


def swap(value, distance):
    count = lax.axis_size("head")
    return lax.ppermute(value, "head", [(i, i ^ distance) for i in range(count)])


def scatter_rows(value, axis):
    count = lax.axis_size(axis)
    index = lax.axis_index(axis)
    value = value.reshape((count, value.shape[0] // count) + value.shape[1:])
    bit = 1
    while bit < count:
        mine = (index // bit) % 2
        value = value.reshape((value.shape[0] // 2, 2) + value.shape[1:])
        sent = lax.dynamic_index_in_dim(value, 1 - mine, 1, False)
        kept = lax.dynamic_index_in_dim(value, mine, 1, False)
        got = lax.ppermute(sent, axis, [(i, i ^ bit) for i in range(count)])
        value = kept.astype(HIGH) + got.astype(HIGH)
        bit *= 2
        if bit < count:
            value = value.astype(LOW)
    return value[0]


def shards(
    tokens,
    cotangent,
    lengths,
    attn_gain,
    w_query,
    w_key,
    w_value,
    w_output,
    ffn_gain,
    w_gate,
    w_up,
    w_down,
):
    blocks = lax.axis_size("head")
    me = lax.axis_index("head").astype(jnp.int32)
    low_bit = me % 2
    rows, width = tokens.shape
    hidden = w_gate.shape[1]
    keys = blocks * rows
    where = jnp.stack([me, lengths[0]])
    frequency = 10000.0 ** (-(jnp.arange(HALF, dtype=HIGH) * 2.0 / HD))
    position = (me * rows + jnp.arange(rows, dtype=jnp.int32)).astype(HIGH)
    angles = frequency[:, None] * position[None, :]
    cosine, sine = jnp.cos(angles), jnp.sin(angles)
    gain_one = attn_gain[None, :]
    gain_two = ffn_gain[None, :]

    def everywhere(value):
        across = swap(value, 2)
        return [value, swap(value, 1), across, swap(across, 1)]

    feature_rows = (width, rows)
    project_outs = [(feature_rows, LOW), (feature_rows, LOW), ((rows, 2 * KV_WIDTH), LOW)]
    a_one, q_one, kv_one = call(qkv_kernel, project_outs, [VMEM] * 7, [], "open")(
        tokens, gain_one, w_query, w_key, w_value, cosine, sine
    )
    kv_one = everywhere(kv_one)
    gates, ups, downs = everywhere(w_gate), everywhere(w_up), everywhere(w_down)
    weight_scratch = [
        pltpu.VMEM((blocks, width, hidden), LOW),
        pltpu.VMEM((blocks, width, hidden), LOW),
        pltpu.VMEM((blocks, hidden, width), LOW),
        pltpu.SemaphoreType.DMA((3, blocks)),
    ]

    def forward(h, queries, kv, last):
        outs = [
            (feature_rows, LOW),
            ((16, rows), HIGH),
            ((rows, width), HIGH),
            (feature_rows, LOW),
            ((blocks, rows, hidden), LOW),
            ((blocks, rows, hidden), LOW),
            ((rows, width), LOW if last else HIGH),
        ]
        specs = [SMEM] + [VMEM] * (4 + blocks) + [ANY] * (3 * blocks)
        given = [where, h, queries, *kv, w_output, gain_two, *gates, *ups, *downs]
        if not last:
            outs += project_outs
            specs += [VMEM] * 6
            given += [gain_one, w_query, w_key, w_value, cosine, sine]
        scratch = [
            pltpu.VMEM((keys, rows), HIGH),
            pltpu.VMEM((KVH, keys, HD), LOW),
            pltpu.VMEM((KV_WIDTH, keys), LOW),
        ] + weight_scratch
        body = functools.partial(forward_kernel, last, blocks)
        return call(body, outs, specs, scratch, "forward_last" if last else "forward_first")(*given)

    def backward(e, kept, first):
        queries, kv, attended, log_totals, middle, gate, up = kept
        outs = [
            (feature_rows, LOW),
            ((6, rows, hidden), LOW),
            ((6, rows, hidden), LOW),
            (feature_rows, LOW),
            ((rows, width), HIGH),
            (feature_rows, LOW),
            ((blocks, 2 * KV_WIDTH, rows), LOW),
            ((1, width), HIGH),
        ]
        specs = [SMEM] + [VMEM] * (11 + blocks) + [ANY] * (3 * blocks)
        given = [where, e, gate, up, middle, gain_two, w_output, queries, *kv, attended, log_totals]
        given += [cosine, sine, *gates, *ups, *downs]
        scratch = [
            pltpu.VMEM((keys, rows), HIGH),
            pltpu.VMEM((KVH, keys, HD), LOW),
            pltpu.VMEM((KVH, keys, HD), LOW),
            pltpu.VMEM((KV_WIDTH, keys), LOW),
            pltpu.VMEM(feature_rows, LOW),
            pltpu.VMEM((16, rows), HIGH),
        ] + weight_scratch
        body = functools.partial(backward_kernel, first, blocks)
        return call(body, outs, specs, scratch, "backward_last" if first else "backward_first")(*given)

    def close(h, grad_middle, grad_query, partial):
        sent = swap(jnp.stack([partial[1], partial[3]]), 1)
        near = sent[0]
        far = swap((partial[2].astype(HIGH) + sent[1].astype(HIGH)).astype(LOW), 2)
        outs = [((rows, width), HIGH), ((2 * KV_WIDTH, rows), LOW), ((1, width), HIGH)]
        given = [h, gain_one, grad_middle, grad_query, w_query, w_key, w_value, cosine, sine]
        given += [partial[0], near, far]
        return call(functools.partial(close_kernel, 3), outs, [VMEM] * 12, [], "close")(*given)

    o_one, lse_one, m_one, b_one, g_one, u_one, h_one, a_two, q_two, kv_two = forward(
        tokens, q_one, kv_one, False
    )
    kv_two = everywhere(kv_two)
    o_two, lse_two, m_two, b_two, g_two, u_two, block_out = forward(h_one, q_two, kv_two, True)
    f_two, mine_two, theirs_two, c_two, dm_two, dq_two, part_two, gain_two_b = backward(
        cotangent, (q_two, kv_two, o_two, lse_two, m_two, g_two, u_two), True
    )
    e_one, dkv_two, gain_one_b = close(h_one, dm_two, dq_two, part_two)
    f_one, mine_one, theirs_one, c_one, dm_one, dq_one, part_one, gain_two_a = backward(
        e_one, (q_one, kv_one, o_one, lse_one, m_one, g_one, u_one), False
    )
    input_grad, dkv_one, gain_one_a = close(tokens, dm_one, dq_one, part_one)

    def beside(parts):
        return jnp.concatenate(parts, axis=-1)

    from_two, from_one = swap(theirs_two, 1), swap(theirs_one, 1)
    b_all = beside([b_two, swap(b_two, 1), b_one, swap(b_one, 1)])
    f_all = beside([f_two, swap(f_two, 1), f_one, swap(f_one, 1)])

    def hidden_rows(which):
        return jnp.concatenate([mine_two[which], from_two[which], mine_one[which], from_one[which]], 0)

    kept, sent = [], []
    for which in range(6):
        product = nn(b_all if which < 4 else f_all, hidden_rows(which)).astype(LOW)
        (sent if which % 2 else kept).append(product)
    got = swap(beside(sent), 2)
    ffn = scatter_rows((beside(kept).astype(HIGH) + got.astype(HIGH)).astype(LOW), "dp")

    def choose(zero, one):
        return jnp.where(low_bit == 0, zero, one)

    lefts, longs, shorts, sides = [], [], [], []
    for a, c, o, dq, dkv in (
        (a_two, c_two, o_two, dq_two, dkv_two),
        (a_one, c_one, o_one, dq_one, dkv_one),
    ):
        dk, dv = dkv[:KV_WIDTH], dkv[KV_WIDTH:]
        lefts += [choose(a, c), swap(choose(c, a), 1)]
        longs += [choose(dq, o), swap(choose(o, dq), 1)]
        shorts += [choose(dk, dv), swap(choose(dv, dk), 1)]
        sides += [a, swap(a, 1)]
    long_part = nt(beside(lefts), beside(longs)).astype(LOW)
    short_part = nt(beside(sides), beside(shorts)).astype(LOW)
    attn = scatter_rows(beside([long_part, short_part]), "dp").astype(LOW)
    attn = (attn.astype(HIGH) + swap(attn, 2).astype(HIGH)).astype(LOW)
    other = swap(attn, 1)
    zero, one = choose(attn, other).astype(HIGH), choose(other, attn).astype(HIGH)
    gains = jnp.concatenate([gain_one_a + gain_one_b, gain_two_a + gain_two_b], axis=0)
    gains = lax.psum_scatter(lax.psum(gains, "head"), "dp", scatter_dimension=1, tiled=True)
    return (
        block_out,
        input_grad,
        gains[0],
        zero[:, : HQ * HD],
        zero[:, HQ * HD :],
        one[:, HQ * HD :],
        one[:, : HQ * HD].T,
        gains[1],
        ffn[:, :hidden],
        ffn[:, hidden : 2 * hidden],
        ffn[:, 2 * hidden :].T,
    )


def solution(mesh):
    return jax.shard_map(
        shards,
        mesh=mesh,
        in_specs=(
            P(("dp", "head"), None),
            P(("dp", "head"), None),
            P("dp"),
            P(),
            P(),
            P(),
            P(),
            P(),
            P(),
            P(None, "head"),
            P(None, "head"),
            P("head", None),
        ),
        out_specs=(
            P(("dp", "head"), None),
            P(("dp", "head"), None),
            P("dp"),
            P("dp", None),
            P("dp", None),
            P("dp", None),
            P(None, "dp"),
            P("dp"),
            P("dp", "head"),
            P("dp", "head"),
            P("head", "dp"),
        ),
        check_vma=False,
    )
```

time: 1880 us -> 462 us (0.25); the launches traced: 1860 us -> 458 us
  waiting for transfers between devices: 937 us -> 175 us
  local copies, waits for them, and re-layouts: 394 us -> 49.3 us
  matrix products: 311 us -> 14.7 us
  other arithmetic: 149 us -> 15.8 us
  Pallas kernels: 0 us -> 122 us
  starting transfers between devices: 2.42 us -> 22.9 us
    reduce_scatter x14 -> x0, waiting for transfers between devices: 483 us -> none  [the longest x2 163 us: reduce_grads(): lax.psum_scatter(full[1], 'dp', scatter_dimension=0, tiled=True)]
    unnamed x39 -> x0, waiting for transfers between devices: 341 us -> none
    dynamic_update_slice x40 -> x0, local copies, waits for them, and re-layouts: 277 us -> none  [the longest x24 190 us: attend(): attended, log_totals = lax.map(one_block, (query_blocks, starts))]
    dot_general x60 -> x8, matrix products: 272 us -> 14.7 us  [the longest x6 10.2 us: nn(): lax.dot_general(left, right, (((1,), (0,)), ((), ())), preferred_element_...]
    ppermute x0 -> x42, waiting for transfers between devices: none -> 175 us  [the longest x36 146 us: swap(): lax.ppermute(value, 'head', [(i, i ^ distance) for i in range(count)])]
    pallas_call x0 -> x7, Pallas kernels: none -> 122 us  [the longest x2 59.1 us: backward(): call(body, outs, specs, scratch, 'backward_last' if first else 'backward_...]
    all_gather x10 -> x0, waiting for transfers between devices: 113 us -> none  [the longest x6 74 us: spread(): return lax.all_gather(rows_low, 'head', axis=0, tiled=True)]
    convert_element_type x26 -> x11, other arithmetic: 61.3 us -> 9.36 us  [the longest x4 5.46 us: scatter_rows(): value = value.astype(LOW)]
  transfers between devices with their start and end apart: 32 -> 42, of which waited for: 23 -> 10; matrix products, arithmetic and copies ran while one was open for 27% -> 16% of each run, Pallas kernels for 0% -> 21%
where the time goes in v1:
time: 462 us; the launch traced here: 458 us
  waiting for transfers between devices  175 us (38%)
  Pallas kernels  122 us (26%)
  blocking collectives  54.6 us (12%)
  local copies, waits for them, and re-layouts  49.3 us (11%)
  starting transfers between devices  22.9 us (5%)
  other arithmetic  15.8 us (3%)
  matrix products  14.7 us (3%)
    ppermute x36, waiting for transfers between devices, swap(): lax.ppermute(value, 'head', [(i, i ^ distance) for i in range(count)])  146 us
    pallas_call x2, Pallas kernels, backward(): call(body, outs, specs, scratch, 'backward_last' if first else 'backward_...  59.1 us
    pallas_call x2, Pallas kernels, forward(): call(body, outs, specs, scratch, 'forward_last' if last else 'forward_fir...  47.6 us
    unnamed x1, blocking collectives  46.5 us
    ppermute x6, waiting for transfers between devices, scatter_rows(): got = lax.ppermute(sent, axis, [(i, i ^ bit) for i in range(count)])  29.1 us
    unnamed x128, local copies, waits for them, and re-layouts  25.9 us
    ppermute x36, starting transfers between devices, swap(): lax.ppermute(value, 'head', [(i, i ^ distance) for i in range(count)])  18 us
    pallas_call x2, Pallas kernels, close(): call(functools.partial(close_kernel, 3), outs, [VMEM] * 12, [], 'close')  11.2 us
  transfers between devices with their start and end apart: 42, of which 10 were waited for; matrix products, arithmetic and copies ran while one was open for 16% of the time, Pallas kernels for 21%

profile of v1, /device:TPU:0, one launch (start us, length us, event | category | flops | bytes accessed | tf_op | source)
XLA Modules:
  0.0 457.8 jit_solution(17293885371151617566)
XLA Ops:
  0.7 3.0 collective-permute-start.10
  3.7 1.9 collective-permute-start.7
  5.7 2.0 copy.110.h_ref.refs_1_.refs_0_
  9.0 2.2 copy.108.wk_ref.refs_23_.refs_5_
  13.3 4.5 open.1
  18.2 1.5 collective-permute-done.refs_4_.refs_9_
  19.8 12.0 %collective-permute-done.10 = bf16[640,960]{0,1:T(8,128)(2,1)} collective-permute-done((bf16[640,960]{0,1:T(8,128)(2,1)}, bf16[640,960]{0,1:T(8,128)(2,1)}, u32[]{:S(2)}, u32[]{:S(2)}) %collective-permute-start.10) | collective-permute-done | bytes 1228832 | tf_op jit(solution)/shard_map/ppermute | solution.py:290
  31.8 58.8 %collective-permute-done.1.refs_5_.refs_10_ = bf16[256,640]{1,0:T(8,128)(2,1)S(1)} collective-permute-done((bf16[256,640]{1,0:T(8,128)(2,1)}, bf16[256,640]{1,0:T(8,128)(2,1)S(1)}, u32[]{:S(2)}, u32[]{:S(2)}) %collective-permute-start.1) | collective-permute-done | bytes 327712 | tf_op jit(solution)/shard_map/ppermute | solution.py:290
  91.7 2.7 copy.111.refs_17_.refs_24_
  96.2 2.5 copy.113.refs_19_.refs_26_
  98.7 2.5 copy.112.refs_18_.refs_25_
  101.2 2.5 copy.114.refs_20_.refs_27_
  104.5 24.3 %forward_first.1 = (bf16[960,256]{1,0:T(8,128)(2,1)}, f32[16,256]{1,0:T(8,128)}, f32[256,960]{1,0:T(8,128)}, bf16[960,256]{1,0:T(8,128)(2,1)}, bf16[4,256,640]{2...) custom-call(s32[2]{0:T(128)} %pad_add_fusion.refs_0_, ...), custom_call_target="tpu_custom_call" | custom-call | tf_op jit(solution)/shard_map/forward_first/pallas_call | solution.py:379
  128.7 1.8 collective-permute-start.13
  130.7 8.4 %collective-permute-done.13.refs_5_.refs_10_ = bf16[256,640]{1,0:T(8,128)(2,1)S(1)} collective-permute-done((bf16[256,640]{1,0:T(8,128)(2,1)}, bf16[256,640]{1,0:T(8,128)(2,1)S(1)}, u32[]{:S(2)}, u32[]{:S(2)}) %collective-permute-start.13) | collective-permute-done | bytes 327712 | tf_op jit(solution)/shard_map/ppermute | solution.py:290
  141.5 23.3 %forward_last.1 = (bf16[960,256]{1,0:T(8,128)(2,1)}, f32[16,256]{1,0:T(8,128)}, f32[256,960]{1,0:T(8,128)}, bf16[960,256]{1,0:T(8,128)(2,1)}, bf16[4,256,640]{2,...) custom-call(s32[2]{0:T(128)} %pad_add_fusion.refs_0_, ...), custom_call_target="tpu_custom_call" | custom-call | tf_op jit(solution)/shard_map/forward_last/pallas_call | solution.py:379
  164.8 29.5 %backward_last.1 = (bf16[960,256]{1,0:T(8,128)(2,1)}, bf16[6,256,640]{2,1,0:T(8,128)(2,1)}, bf16[6,256,640]{2,1,0:T(8,128)(2,1)}, bf16[960,256]{1,0:T(8,128)(2,1...) custom-call(s32[2]{0:T(128)} %pad_add_fusion.refs_0_, ...), custom_call_target="tpu_custom_call" | custom-call | tf_op jit(solution)/shard_map/backward_last/pallas_call | solution.py:405
  194.4 2.1 fusion.96
  197.8 1.4 copy-done.4
  201.5 1.8 collective-permute-start.16
  205.0 6.4 %collective-permute-done.16.refs_11_ = bf16[640,256]{1,0:T(8,128)(2,1)} collective-permute-done((bf16[640,256]{1,0:T(8,128)(2,1)S(1)}, bf16[640,256]{1,0:T(8,128)(2,1)}, u32[]{:S(2)}, u32[]{:S(2)}) %collective-permute-start.16) | collective-permute-done | bytes 327712 | tf_op jit(solution)/shard_map/ppermute | solution.py:290
  211.4 5.7 %close.2 = (f32[256,960]{1,0:T(8,128)}, bf16[640,256]{1,0:T(8,128)(2,1)}, f32[1,960]{1,0:T(1,128)}) custom-call(f32[256,960]{1,0:T(8,128)} %get-tuple-element.55.refs_1_.refs_0_, bf16[1,960]{1,0:T(2,128)(2,1)} %broadcast_in_dim.8.gain_ref.refs_21_.refs_1_, f32[256,960]{1,0:T(8,128)} %get-tuple-element.64.refs_2_, ...), custom_call_target="tpu_custom_call" | custom-call | tf_op jit(solution)/shard_map/close/pallas_call | solution.py:414
  217.1 29.6 %backward_first.1 = (bf16[960,256]{1,0:T(8,128)(2,1)}, bf16[6,256,640]{2,1,0:T(8,128)(2,1)}, bf16[6,256,640]{2,1,0:T(8,128)(2,1)}, bf16[960,256]{1,0:T(8,128)(2,...) custom-call(s32[2]{0:T(128)} %pad_add_fusion.refs_0_, ...), custom_call_target="tpu_custom_call" | custom-call | tf_op jit(solution)/shard_map/backward_first/pallas_call | solution.py:405
  247.4 1.4 constant_dynamic-update-slice_fusion.2
  254.2 1.8 collective-permute-start.18
  258.1 1.7 convolution_convert_fusion.1
  259.8 1.7 convolution_convert_fusion.2
  261.6 1.7 convolution_convert_fusion
  263.3 2.3 pad_maximum_fusion
  268.5 5.5 %close.3 = (f32[256,960]{1,0:T(8,128)}, bf16[640,256]{1,0:T(8,128)(2,1)}, f32[1,960]{1,0:T(1,128)}) custom-call(bf16[256,960]{1,0:T(8,128)(2,1)} %copy.110.h_ref.refs_1_.refs_0_, bf16[1,960]{1,0:T(2,128)(2,1)} %broadcast_in_dim.8.gain_ref.refs_21_.refs_1_, f32[256,960]{1,0:T(8,128)} %get-tuple-element.73.refs_2_, ...), custom_call_target="tpu_custom_call" | custom-call | tf_op jit(solution)/shard_map/close/pallas_call | solution.py:414
  276.8 3.7 fusion.26
  282.5 1.6 collective-permute-start.27
  284.1 1.7 convolution_convert_fusion.3
  286.0 1.7 convolution_convert_fusion.4
  287.8 1.7 convolution_convert_fusion.5
  289.5 58.2 %collective-permute-done.38 = bf16[960,1920]{1,0:T(8,128)(2,1)} collective-permute-done((bf16[960,1920]{1,0:T(8,128)(2,1)}, bf16[960,1920]{1,0:T(8,128)(2,1)}, u32[]{:S(2)}, u32[]{:S(2)}) %collective-permute-start.38) | collective-permute-done | bytes 3686432 | tf_op jit(solution)/shard_map/ppermute | solution.py:290
  347.6 2.5 add_convert_fusion
  350.3 1.6 collective-permute-start.39
  353.1 1.6 collective-permute-start.28
  356.0 2.0 copy.138
  358.0 2.5 copy.139
  360.5 46.5 %all-reduce = f32[2,960]{1,0:T(2,128)S(1)} all-reduce(f32[2,960]{1,0:T(2,128)S(1)} %pad_maximum_fusion.4), channel_id=2, replica_groups=mesh['dp'=8,'head'=4] {'dp'}, use_global_device_ids=true, to_apply=%region_1.2.clone | all-reduce | flops 1920 | bytes 15360
  408.5 2.5 fusion
  412.0 6.8 %collective-permute-done.29 = bf16[1,120,1280]{2,1,0:T(8,128)(2,1)S(1)} collective-permute-done((bf16[1,120,1280]{2,1,0:T(8,128)(2,1)S(1)}, bf16[1,120,1280]{2,1,0:T(8,128)(2,1)S(1)}, u32[]{:S(2)}, u32[]{:S(2)}) %collective-permute-start.29) | collective-permute-done | bytes 307232 | tf_op jit(solution)/shard_map/ppermute | solution.py:303
  419.9 8.1 %psum.8 = f32[2,120]{1,0:T(2,128)S(1)} all-reduce(f32[2,120]{1,0:T(2,128)S(1)} %constant_dynamic-slice_fusion.2), channel_id=1, replica_groups=mesh['dp'=8,'head'=4] {'head'}, use_global_device_ids=true, to_apply=%region_0.1 | all-reduce | flops 240 | bytes 1920 | tf_op jit(solution)/shard_map/psum | solution.py:467
  428.7 6.6 %collective-permute-done.40 = bf16[2,120,1920]{2,1,0:T(8,128)(2,1)} collective-permute-done((bf16[2,120,1920]{2,1,0:T(8,128)(2,1)}, bf16[2,120,1920]{2,1,0:T(8,128)(2,1)}, u32[]{:S(2)}, u32[]{:S(2)}) %collective-permute-start.40) | collective-permute-done | bytes 921632 | tf_op jit(solution)/shard_map/ppermute | solution.py:303
  435.2 1.4 fusion.25
  440.6 15.7 %collective-permute-done.41 = bf16[1,120,1920]{2,1,0:T(8,128)(2,1)S(1)} collective-permute-done((bf16[1,120,1920]{2,1,0:T(8,128)(2,1)S(1)}, bf16[1,120,1920]{2,1,0:T(8,128)(2,1)S(1)}, u32[]{:S(2)}, u32[]{:S(2)}) %collective-permute-start.41) | collective-permute-done | bytes 460832 | tf_op jit(solution)/shard_map/ppermute | solution.py:303
  (237 shorter events, 41.6 us)
Async XLA Ops:
  0.6 10.6 %copy-start.16 = (bf16[960,320]{0,1:T(8,128)(2,1)S(1)}, bf16[960,320]{0,1:T(8,128)(2,1)}, u32[]{:S(2)}) copy-start(bf16[960,320]{0,1:T(8,128)(2,1)} %param.18) | copy-start | bytes 1843204
  0.7 31.2 %collective-permute-start.10 = (bf16[640,960]{0,1:T(8,128)(2,1)}, bf16[640,960]{0,1:T(8,128)(2,1)}, u32[]{:S(2)}, u32[]{:S(2)}) collective-permute-start(bf16[640,960]{0,1:T(8,128)(2,1)} %param.23), channel_id=1, source_target_pairs={{0,2},{1,3},{2,0},{3,1},{4,6},{5,7},{6,4},{7,5},{8,10},{9,11},{10,... | collective-permute-start | bytes 3686408 | tf_op jit(solution)/shard_map/ppermute | solution.py:290
  3.7 86.9 %collective-permute-start.4 = (bf16[960,640]{1,0:T(8,128)(2,1)}, bf16[960,640]{1,0:T(8,128)(2,1)}, u32[]{:S(2)}, u32[]{:S(2)}) collective-permute-start(bf16[960,640]{1,0:T(8,128)(2,1)} %refs_16_.3), channel_id=1, source_target_pairs={{0,2},{1,3},{2,0},{3,1},{4,6},{5,7},{6,4},{7,5},{8,10},{9,11},{10,... | collective-permute-start | bytes 3686408 | tf_op jit(solution)/shard_map/ppermute | solution.py:290
  3.7 87.4 %collective-permute-start.7 = (bf16[960,640]{1,0:T(8,128)(2,1)}, bf16[960,640]{1,0:T(8,128)(2,1)}, u32[]{:S(2)}, u32[]{:S(2)}) collective-permute-start(bf16[960,640]{1,0:T(8,128)(2,1)} %refs_20_.3), channel_id=1, source_target_pairs={{0,2},{1,3},{2,0},{3,1},{4,6},{5,7},{6,4},{7,5},{8,10},{9,11},{10,... | collective-permute-start | bytes 3686408 | tf_op jit(solution)/shard_map/ppermute | solution.py:290
  5.7 85.5 %collective-permute-start.9 = (bf16[640,960]{0,1:T(8,128)(2,1)}, bf16[640,960]{0,1:T(8,128)(2,1)}, u32[]{:S(2)}, u32[]{:S(2)}) collective-permute-start(bf16[640,960]{0,1:T(8,128)(2,1)} %param.23), channel_id=1, source_target_pairs={{0,1},{1,0},{2,3},{3,2},{4,5},{5,4},{6,7},{7,6},{8,9},{9,8},{10,11... | collective-permute-start | bytes 3686408 | tf_op jit(solution)/shard_map/ppermute | solution.py:290
  13.3 77.3 %copy-start = (bf16[960,640]{1,0:T(8,128)(2,1)S(1)}, bf16[960,640]{1,0:T(8,128)(2,1)}, u32[]{:S(2)}) copy-start(bf16[960,640]{1,0:T(8,128)(2,1)} %refs_16_.3) | copy-start | bytes 3686404
  13.3 77.3 %copy-start.1 = (bf16[960,640]{1,0:T(8,128)(2,1)S(1)}, bf16[960,640]{1,0:T(8,128)(2,1)}, u32[]{:S(2)}) copy-start(bf16[960,640]{1,0:T(8,128)(2,1)} %refs_20_.3) | copy-start | bytes 3686404
  17.7 77.3 %copy-start.52 = (bf16[960]{0:T(1024)(128)(2,1)S(1)}, bf16[960]{0:T(1024)(128)(2,1)}, u32[]{:S(2)}) copy-start(bf16[960]{0:T(1024)(128)(2,1)} %param.20) | copy-start | bytes 5764
  17.7 2.0 collective-permute-start
  19.7 79.0 %copy-start.10 = (bf16[256,640]{1,0:T(8,128)(2,1)}, bf16[256,640]{1,0:T(8,128)(2,1)S(1)}, u32[]{:S(2)}) copy-start(bf16[256,640]{1,0:T(8,128)(2,1)S(1)} %collective-permute-done.refs_4_.refs_9_) | copy-start | bytes 983044
  19.7 70.9 %collective-permute-start.1 = (bf16[256,640]{1,0:T(8,128)(2,1)}, bf16[256,640]{1,0:T(8,128)(2,1)S(1)}, u32[]{:S(2)}, u32[]{:S(2)}) collective-permute-start(bf16[256,640]{1,0:T(8,128)(2,1)} %get-tuple-element.54.refs_3_.refs_8_), channel_id=1, source_target_pairs={{0,2},{1,3},{2,0},{3,1},{4,6},{5,7},{6,4},{7,5},{8,10},{9,11},{10,... | collective-permute-start | bytes 983048 | tf_op jit(solution)/shard_map/ppermute | solution.py:290
  31.8 59.8 %collective-permute-start.11 = (bf16[640,960]{0,1:T(8,128)(2,1)}, bf16[640,960]{0,1:T(8,128)(2,1)}, u32[]{:S(2)}, u32[]{:S(2)}) collective-permute-start(bf16[640,960]{0,1:T(8,128)(2,1)} %collective-permute-done.10), channel_id=1, source_target_pairs={{0,1},{1,0},{2,3},{3,2},{4,5},{5,4},{6,7},{7,6},{8,9},{9,8},{10,11... | collective-permute-start | bytes 3686408 | tf_op jit(solution)/shard_map/ppermute | solution.py:290
  90.6 13.2 %collective-permute-start.3 = (bf16[960,640]{1,0:T(8,128)(2,1)S(1)}, bf16[960,640]{1,0:T(8,128)(2,1)}, u32[]{:S(2)}, u32[]{:S(2)}) collective-permute-start(bf16[960,640]{1,0:T(8,128)(2,1)S(1)} %copy-done), channel_id=1, source_target_pairs={{0,1},{1,0},{2,3},{3,2},{4,5},{5,4},{6,7},{7,6},{8,9},{9,8},{10,11... | collective-permute-start | bytes 3686408 | tf_op jit(solution)/shard_map/ppermute | solution.py:290
  90.6 13.1 %collective-permute-start.6 = (bf16[960,640]{1,0:T(8,128)(2,1)S(1)}, bf16[960,640]{1,0:T(8,128)(2,1)}, u32[]{:S(2)}, u32[]{:S(2)}) collective-permute-start(bf16[960,640]{1,0:T(8,128)(2,1)S(1)} %copy-done.1), channel_id=1, source_target_pairs={{0,1},{1,0},{2,3},{3,2},{4,5},{5,4},{6,7},{7,6},{8,9},{9,8},{10,11... | collective-permute-start | bytes 3686408 | tf_op jit(solution)/shard_map/ppermute | solution.py:290
  91.1 12.7 %collective-permute-start.5 = (bf16[960,640]{1,0:T(8,128)(2,1)}, bf16[960,640]{1,0:T(8,128)(2,1)}, u32[]{:S(2)}, u32[]{:S(2)}) collective-permute-start(bf16[960,640]{1,0:T(8,128)(2,1)} %collective-permute-done.4.refs_11_.refs_18_), channel_id=1, source_target_pairs={{0,1},{1,0},{2,3},{3,2},{4,5},{5,4},{6,7},{7,6},{8,9},{9,8},{10,11... | collective-permute-start | bytes 3686408 | tf_op jit(solution)/shard_map/ppermute | solution.py:290
  91.2 12.6 %collective-permute-start.8 = (bf16[960,640]{1,0:T(8,128)(2,1)}, bf16[960,640]{1,0:T(8,128)(2,1)}, u32[]{:S(2)}, u32[]{:S(2)}) collective-permute-start(bf16[960,640]{1,0:T(8,128)(2,1)} %collective-permute-done.7.refs_15_.refs_22_), channel_id=1, source_target_pairs={{0,1},{1,0},{2,3},{3,2},{4,5},{5,4},{6,7},{7,6},{8,9},{9,8},{10,11... | collective-permute-start | bytes 3686408 | tf_op jit(solution)/shard_map/ppermute | solution.py:290
  91.6 12.1 %collective-permute-start.2 = (bf16[256,640]{1,0:T(8,128)(2,1)S(1)}, bf16[256,640]{1,0:T(8,128)(2,1)S(1)}, u32[]{:S(2)}, u32[]{:S(2)}) collective-permute-start(bf16[256,640]{1,0:T(8,128)(2,1)S(1)} %collective-permute-done.1.refs_5_.refs_10_), channel_id=1, source_target_pairs={{0,1},{1,0},{2,3},{3,2},{4,5},{5,4},{6,7},{7,6},{8,9},{9,8},{10,11... | collective-permute-start | bytes 983048 | tf_op jit(solution)/shard_map/ppermute | solution.py:290
  104.5 34.6 %copy-start.17 = (bf16[256,960]{0,1:T(8,128)(2,1)S(1)}, bf16[256,960]{0,1:T(8,128)(2,1)}, u32[]{:S(2)}) copy-start(bf16[256,960]{0,1:T(8,128)(2,1)} %param.13) | copy-start | bytes 1474564
  128.7 10.3 %collective-permute-start.13 = (bf16[256,640]{1,0:T(8,128)(2,1)}, bf16[256,640]{1,0:T(8,128)(2,1)S(1)}, u32[]{:S(2)}, u32[]{:S(2)}) collective-permute-start(bf16[256,640]{1,0:T(8,128)(2,1)} %get-tuple-element.57.refs_3_.refs_8_), channel_id=1, source_target_pairs={{0,2},{1,3},{2,0},{3,1},{4,6},{5,7},{6,4},{7,5},{8,10},{9,11},{10,... | collective-permute-start | bytes 983048 | tf_op jit(solution)/shard_map/ppermute | solution.py:290
  130.5 10.1 %collective-permute-start.12 = (bf16[256,640]{1,0:T(8,128)(2,1)}, bf16[256,640]{1,0:T(8,128)(2,1)S(1)}, u32[]{:S(2)}, u32[]{:S(2)}) collective-permute-start(bf16[256,640]{1,0:T(8,128)(2,1)} %get-tuple-element.57.refs_3_.refs_8_), channel_id=1, source_target_pairs={{0,1},{1,0},{2,3},{3,2},{4,5},{5,4},{6,7},{7,6},{8,9},{9,8},{10,11... | collective-permute-start | bytes 983048 | tf_op jit(solution)/shard_map/ppermute | solution.py:290
  139.1 1.6 collective-permute-start.14
  140.1 110.9 %collective-permute-start.33 = (bf16[960,256]{1,0:T(8,128)(2,1)}, bf16[960,256]{1,0:T(8,128)(2,1)S(1)}, u32[]{:S(2)}, u32[]{:S(2)}) collective-permute-start(bf16[960,256]{1,0:T(8,128)(2,1)} %get-tuple-element.88), channel_id=1, source_target_pairs={{0,1},{1,0},{2,3},{3,2},{4,5},{5,4},{6,7},{7,6},{8,9},{9,8},{10,11... | collective-permute-start | bytes 1474568 | tf_op jit(solution)/shard_map/ppermute | solution.py:290
  196.5 4.0 collective-permute-start.15
  196.7 52.3 %collective-permute-start.36 = (bf16[960,256]{1,0:T(8,128)(2,1)S(1)}, bf16[960,256]{1,0:T(8,128)(2,1)}, u32[]{:S(2)}, u32[]{:S(2)}) collective-permute-start(bf16[960,256]{1,0:T(8,128)(2,1)S(1)} %copy-done.22), channel_id=1, source_target_pairs={{0,1},{1,0},{2,3},{3,2},{4,5},{5,4},{6,7},{7,6},{8,9},{9,8},{10,11... | collective-permute-start | bytes 1474568 | tf_op jit(solution)/shard_map/ppermute | solution.py:290
  197.1 58.9 %collective-permute-start.34 = (bf16[6,256,640]{2,1,0:T(8,128)(2,1)}, bf16[6,256,640]{2,1,0:T(8,128)(2,1)S(1)}, u32[]{:S(2)}, u32[]{:S(2)}) collective-permute-start(bf16[6,256,640]{2,1,0:T(8,128)(2,1)} %get-tuple-element.90), channel_id=1, source_target_pairs={{0,1},{1,0},{2,3},{3,2},{4,5},{5,4},{6,7},{7,6},{8,9},{9,8},{10,11... | collective-permute-start | bytes 5898248 | tf_op jit(solution)/shard_map/ppermute | solution.py:290
  197.2 49.6 %collective-permute-start.32 = (bf16[960,256]{1,0:T(8,128)(2,1)S(1)}, bf16[960,256]{1,0:T(8,128)(2,1)}, u32[]{:S(2)}, u32[]{:S(2)}) collective-permute-start(bf16[960,256]{1,0:T(8,128)(2,1)S(1)} %copy-done.23), channel_id=1, source_target_pairs={{0,1},{1,0},{2,3},{3,2},{4,5},{5,4},{6,7},{7,6},{8,9},{9,8},{10,11... | collective-permute-start | bytes 1474568 | tf_op jit(solution)/shard_map/ppermute | solution.py:290
  201.5 9.9 %collective-permute-start.16 = (bf16[640,256]{1,0:T(8,128)(2,1)S(1)}, bf16[640,256]{1,0:T(8,128)(2,1)}, u32[]{:S(2)}, u32[]{:S(2)}) collective-permute-start(bf16[640,256]{1,0:T(8,128)(2,1)S(1)} %fusion.84), channel_id=1, source_target_pairs={{0,2},{1,3},{2,0},{3,1},{4,6},{5,7},{6,4},{7,5},{8,10},{9,11},{10,... | collective-permute-start | bytes 983048 | tf_op jit(solution)/shard_map/ppermute | solution.py:290
  246.7 10.3 %collective-permute-start.35 = (bf16[6,256,640]{2,1,0:T(8,128)(2,1)}, bf16[6,256,640]{2,1,0:T(8,128)(2,1)S(1)}, u32[]{:S(2)}, u32[]{:S(2)}) collective-permute-start(bf16[6,256,640]{2,1,0:T(8,128)(2,1)} %get-tuple-element.92), channel_id=1, source_target_pairs={{0,1},{1,0},{2,3},{3,2},{4,5},{5,4},{6,7},{7,6},{8,9},{9,8},{10,11... | collective-permute-start | bytes 5898248 | tf_op jit(solution)/shard_map/ppermute | solution.py:290
  246.8 28.2 %collective-permute-start.21 = (bf16[960,256]{1,0:T(8,128)(2,1)S(1)}, bf16[960,256]{1,0:T(8,128)(2,1)}, u32[]{:S(2)}, u32[]{:S(2)}) collective-permute-start(bf16[960,256]{1,0:T(8,128)(2,1)S(1)} %get-tuple-element.174), channel_id=1, source_target_pairs={{0,1},{1,0},{2,3},{3,2},{4,5},{5,4},{6,7},{7,6},{8,9},{9,8},{10,11... | collective-permute-start | bytes 1474568 | tf_op jit(solution)/shard_map/ppermute | solution.py:290
  251.0 3.1 collective-permute-start.17
  251.1 2.8 collective-permute-start.37
  253.8 21.6 %collective-permute-start.19 = (bf16[960,256]{1,0:T(8,128)(2,1)S(1)}, bf16[960,256]{1,0:T(8,128)(2,1)}, u32[]{:S(2)}, u32[]{:S(2)}) collective-permute-start(bf16[960,256]{1,0:T(8,128)(2,1)S(1)} %get-tuple-element.170), channel_id=1, source_target_pairs={{0,1},{1,0},{2,3},{3,2},{4,5},{5,4},{6,7},{7,6},{8,9},{9,8},{10,11... | collective-permute-start | bytes 1474568 | tf_op jit(solution)/shard_map/ppermute | solution.py:290
  254.2 12.7 %collective-permute-start.18 = (bf16[640,256]{1,0:T(8,128)(2,1)S(1)}, bf16[640,256]{1,0:T(8,128)(2,1)S(1)}, u32[]{:S(2)}, u32[]{:S(2)}) collective-permute-start(bf16[640,256]{1,0:T(8,128)(2,1)S(1)} %fusion.85), channel_id=1, source_target_pairs={{0,2},{1,3},{2,0},{3,1},{4,6},{5,7},{6,4},{7,5},{8,10},{9,11},{10,... | collective-permute-start | bytes 983048 | tf_op jit(solution)/shard_map/ppermute | solution.py:290
  265.6 82.1 %collective-permute-start.38 = (bf16[960,1920]{1,0:T(8,128)(2,1)}, bf16[960,1920]{1,0:T(8,128)(2,1)}, u32[]{:S(2)}, u32[]{:S(2)}) collective-permute-start(bf16[960,1920]{1,0:T(8,128)(2,1)} %pad_maximum_fusion), channel_id=1, source_target_pairs={{0,2},{1,3},{2,0},{3,1},{4,6},{5,7},{6,4},{7,5},{8,10},{9,11},{10,... | collective-permute-start | bytes 11059208 | tf_op jit(solution)/shard_map/ppermute | solution.py:290
  266.1 9.6 %collective-permute-start.22 = (bf16[960,256]{1,0:T(8,128)(2,1)S(1)}, bf16[960,256]{1,0:T(8,128)(2,1)}, u32[]{:S(2)}, u32[]{:S(2)}) collective-permute-start(bf16[960,256]{1,0:T(8,128)(2,1)S(1)} %get-tuple-element.176), channel_id=1, source_target_pairs={{0,1},{1,0},{2,3},{3,2},{4,5},{5,4},{6,7},{7,6},{8,9},{9,8},{10,11... | collective-permute-start | bytes 1474568 | tf_op jit(solution)/shard_map/ppermute | solution.py:290
  266.8 9.2 %collective-permute-start.20 = (bf16[960,256]{1,0:T(8,128)(2,1)S(1)}, bf16[960,256]{1,0:T(8,128)(2,1)S(1)}, u32[]{:S(2)}, u32[]{:S(2)}) collective-permute-start(bf16[960,256]{1,0:T(8,128)(2,1)S(1)} %get-tuple-element.172), channel_id=1, source_target_pairs={{0,1},{1,0},{2,3},{3,2},{4,5},{5,4},{6,7},{7,6},{8,9},{9,8},{10,11... | collective-permute-start | bytes 1474568 | tf_op jit(solution)/shard_map/ppermute | solution.py:290
  275.1 5.4 %collective-permute-start.24 = (bf16[960,256]{1,0:T(8,128)(2,1)S(1)}, bf16[960,256]{1,0:T(8,128)(2,1)S(1)}, u32[]{:S(2)}, u32[]{:S(2)}) collective-permute-start(bf16[960,256]{1,0:T(8,128)(2,1)S(1)} %copy-done.18), channel_id=1, source_target_pairs={{0,1},{1,0},{2,3},{3,2},{4,5},{5,4},{6,7},{7,6},{8,9},{9,8},{10,11... | collective-permute-start | bytes 1474568 | tf_op jit(solution)/shard_map/ppermute | solution.py:290
  275.5 5.0 %collective-permute-start.23 = (bf16[960,256]{1,0:T(8,128)(2,1)S(1)}, bf16[960,256]{1,0:T(8,128)(2,1)S(1)}, u32[]{:S(2)}, u32[]{:S(2)}) collective-permute-start(bf16[960,256]{1,0:T(8,128)(2,1)S(1)} %copy-done.19), channel_id=1, source_target_pairs={{0,1},{1,0},{2,3},{3,2},{4,5},{5,4},{6,7},{7,6},{8,9},{9,8},{10,11... | collective-permute-start | bytes 1474568 | tf_op jit(solution)/shard_map/ppermute | solution.py:290
  275.6 4.9 %collective-permute-start.25 = (bf16[320,256]{1,0:T(8,128)(2,1)}, bf16[320,256]{1,0:T(8,128)(2,1)S(1)}, u32[]{:S(2)}, u32[]{:S(2)}) collective-permute-start(bf16[320,256]{1,0:T(8,128)(2,1)} %get-tuple-element.183), channel_id=1, source_target_pairs={{0,1},{1,0},{2,3},{3,2},{4,5},{5,4},{6,7},{7,6},{8,9},{9,8},{10,11... | collective-permute-start | bytes 491528 | tf_op jit(solution)/shard_map/ppermute | solution.py:290
  276.0 4.5 collective-permute-start.26
  282.5 69.4 %collective-permute-start.27 = (bf16[4,120,1280]{2,1,0:T(8,128)(2,1)S(1)}, bf16[4,120,1280]{2,1,0:T(8,128)(2,1)S(1)}, u32[]{:S(2)}, u32[]{:S(2)}) collective-permute-start(bf16[4,120,1280]{2,1,0:T(8,128)(2,1)S(1)} %dynamic-slice_bitcast_fusion.1), channel_id=1, source_target_pairs={{0,4},{4,0},{8,12},{12,8},{16,20},{20,16},{24,28},{28,24},{1,5},{5... | collective-permute-start | bytes 3686408 | tf_op jit(solution)/shard_map/ppermute | solution.py:303
  350.3 58.1 %collective-permute-start.39 = (bf16[4,120,1920]{2,1,0:T(8,128)(2,1)S(1)}, bf16[4,120,1920]{2,1,0:T(8,128)(2,1)}, u32[]{:S(2)}, u32[]{:S(2)}) collective-permute-start(bf16[4,120,1920]{2,1,0:T(8,128)(2,1)S(1)} %dynamic-slice_bitcast_fusion), channel_id=1, source_target_pairs={{0,4},{4,0},{8,12},{12,8},{16,20},{20,16},{24,28},{28,24},{1,5},{5... | collective-permute-start | bytes 5529608 | tf_op jit(solution)/shard_map/ppermute | solution.py:303
  353.1 54.0 %collective-permute-start.28 = (bf16[2,120,1280]{2,1,0:T(8,128)(2,1)}, bf16[2,120,1280]{2,1,0:T(8,128)(2,1)}, u32[]{:S(2)}, u32[]{:S(2)}) collective-permute-start(bf16[2,120,1280]{2,1,0:T(8,128)(2,1)} %dynamic-slice_bitcast_fusion.3), channel_id=1, source_target_pairs={{0,8},{4,12},{8,0},{12,4},{16,24},{20,28},{24,16},{28,20},{1,9},{5... | collective-permute-start | bytes 1843208 | tf_op jit(solution)/shard_map/ppermute | solution.py:303
  408.4 10.4 %collective-permute-start.29 = (bf16[1,120,1280]{2,1,0:T(8,128)(2,1)S(1)}, bf16[1,120,1280]{2,1,0:T(8,128)(2,1)S(1)}, u32[]{:S(2)}, u32[]{:S(2)}) collective-permute-start(bf16[1,120,1280]{2,1,0:T(8,128)(2,1)S(1)} %constant_dynamic-slice_fusion.1), channel_id=1, source_target_pairs={{0,16},{4,20},{8,24},{12,28},{16,0},{20,4},{24,8},{28,12},{1,17},{... | collective-permute-start | bytes 921608 | tf_op jit(solution)/shard_map/ppermute | solution.py:303
  412.0 23.3 %collective-permute-start.40 = (bf16[2,120,1920]{2,1,0:T(8,128)(2,1)}, bf16[2,120,1920]{2,1,0:T(8,128)(2,1)}, u32[]{:S(2)}, u32[]{:S(2)}) collective-permute-start(bf16[2,120,1920]{2,1,0:T(8,128)(2,1)} %dynamic-slice_bitcast_fusion.2), channel_id=1, source_target_pairs={{0,8},{4,12},{8,0},{12,4},{16,24},{20,28},{24,16},{28,20},{1,9},{5... | collective-permute-start | bytes 2764808 | tf_op jit(solution)/shard_map/ppermute | solution.py:303
  418.9 9.7 %collective-permute-start.30 = (bf16[120,1280]{1,0:T(8,128)(2,1)S(1)}, bf16[120,1280]{1,0:T(8,128)(2,1)S(1)}, u32[]{:S(2)}, u32[]{:S(2)}) collective-permute-start(bf16[120,1280]{1,0:T(8,128)(2,1)S(1)} %fusion.86), channel_id=1, source_target_pairs={{0,2},{1,3},{2,0},{3,1},{4,6},{5,7},{6,4},{7,5},{8,10},{9,11},{10,... | collective-permute-start | bytes 921608 | tf_op jit(solution)/shard_map/ppermute | solution.py:290
  428.6 8.2 %collective-permute-start.31 = (bf16[120,1280]{1,0:T(8,128)(2,1)S(1)}, bf16[120,1280]{1,0:T(8,128)(2,1)S(1)}, u32[]{:S(2)}, u32[]{:S(2)}) collective-permute-start(bf16[120,1280]{1,0:T(8,128)(2,1)S(1)} %add_convert_fusion.3), channel_id=1, source_target_pairs={{0,1},{1,0},{2,3},{3,2},{4,5},{5,4},{6,7},{7,6},{8,9},{9,8},{10,11... | collective-permute-start | bytes 921608 | tf_op jit(solution)/shard_map/ppermute | solution.py:290
  436.7 19.6 %collective-permute-start.41 = (bf16[1,120,1920]{2,1,0:T(8,128)(2,1)S(1)}, bf16[1,120,1920]{2,1,0:T(8,128)(2,1)S(1)}, u32[]{:S(2)}, u32[]{:S(2)}) collective-permute-start(bf16[1,120,1920]{2,1,0:T(8,128)(2,1)S(1)} %constant_dynamic-slice_fusion), channel_id=1, source_target_pairs={{0,16},{4,20},{8,24},{12,28},{16,0},{20,4},{24,8},{28,12},{1,17},{... | collective-permute-start | bytes 1382408 | tf_op jit(solution)/shard_map/ppermute | solution.py:303
  (49 other events, 130.3 us)

commit v2 on v1

--- a/solution.py
+++ b/solution.py
@@ -22,6 +22,7 @@
 SMEM = pl.BlockSpec(memory_space=pltpu.SMEM)
 ANY = pl.BlockSpec(memory_space=pl.ANY)
 LIMIT = 58 * 2**20
+MESH = pl.DeviceIdType.MESH
 
 
 def nn(left, right):
@@ -59,15 +60,16 @@
     return jnp.concatenate(parts, axis=0)
 
 
-def project(hidden, gain, w_query, w_key, w_value, cosine, sine, a_ref, q_ref, kv_ref):
+def project(hidden, gain, w_query, w_key, w_value, cosine, sine, a_ref, q_ref, kv_ref, ready):
     normed = hidden * inverse_rms(hidden) * gain
+    low = normed.astype(LOW)
+    keys = turned(nn(low, w_key[...]).T, cosine, sine, 1.0, 1.0)
+    kv_ref[:, :KV_WIDTH] = keys.T.astype(LOW)
+    kv_ref[:, KV_WIDTH:] = nn(low, w_value[...]).astype(LOW)
+    ready()
+    queries = nn(low, w_query[...]).T
+    q_ref[...] = turned(queries, cosine, sine, 1.0, SCALE).astype(LOW)
     a_ref[...] = normed.T.astype(LOW)
-    normed = normed.astype(LOW)
-    queries = nn(normed, w_query[...]).T
-    q_ref[...] = turned(queries, cosine, sine, 1.0, SCALE).astype(LOW)
-    keys = turned(nn(normed, w_key[...]).T, cosine, sine, 1.0, 1.0)
-    kv_ref[:, :KV_WIDTH] = keys.T.astype(LOW)
-    kv_ref[:, KV_WIDTH:] = nn(normed, w_value[...]).astype(LOW)
 
 
 def fill_bias(where_ref, bias, rows, blocks):
@@ -85,51 +87,22 @@
         bias[step * rows : (step + 1) * rows] = jnp.where(allowed, 0.0, BLOCKED)
 
 
-def weights_in(sources, holders, sems):
-    copies = []
-    for which, (source, holder) in enumerate(zip(sources, holders)):
-        for step in range(len(source)):
-            copies.append(pltpu.make_async_copy(source[step], holder.at[step], sems.at[which, step]))
+def weights_in(sources, holders, sems, order):
+    copies = {}
+    for step in range(2):
+        for which in order:
+            holder = holders[which]
+            target = holder.at[0] if step == 0 else holder.at[pl.ds(1, holder.shape[0] - 1)]
+            copies[step, which] = pltpu.make_async_copy(sources[2 * which + step], target, sems.at[which, step])
+            copies[step, which].start()
     return copies
 
 
-def qkv_kernel(h_ref, gain_ref, wq_ref, wk_ref, wv_ref, cos_ref, sin_ref, a_ref, q_ref, kv_ref):
-    hidden = h_ref[...].astype(HIGH)
-    gain = gain_ref[...].astype(HIGH)
-    project(hidden, gain, wq_ref, wk_ref, wv_ref, cos_ref[...], sin_ref[...], a_ref, q_ref, kv_ref)
-
-
-def forward_kernel(last, blocks, *refs):
-    where_ref, h_ref, q_ref = refs[:3]
-    kv_refs = refs[3 : 3 + blocks]
-    refs = refs[3 + blocks :]
-    wo_ref, gain_two_ref = refs[:2]
-    wg_any, wu_any, wd_any = (refs[2 + i * blocks : 2 + (i + 1) * blocks] for i in range(3))
-    refs = refs[2 + 3 * blocks :]
-    if not last:
-        gain_one_ref, wq_ref, wk_ref, wv_ref, cos_ref, sin_ref = refs[:6]
-        refs = refs[6:]
-    o_ref, lse_ref, m_ref, b_ref, g_ref, u_ref, out_ref = refs[:7]
-    refs = refs[7:]
-    if not last:
-        next_a, next_q, next_kv = refs[:3]
-        refs = refs[3:]
-    bias, k_sc, vt_sc, wg, wu, wd, sems = refs
-    rows = h_ref.shape[0]
-    copies = weights_in((wg_any, wu_any, wd_any), (wg, wu, wd), sems)
-    for step in range(blocks):
-        for which in range(3):
-            copies[which * blocks + step].start()
-    fill_bias(where_ref, bias, rows, blocks)
-    for step in range(blocks):
-        held = kv_refs[step][...]
-        for group in range(KVH):
-            k_sc[group, step * rows : (step + 1) * rows] = held[:, group * HD : (group + 1) * HD]
-        vt_sc[:, step * rows : (step + 1) * rows] = held[:, KV_WIDTH:].T
-
+def attend(bias, k_sc, vt_sc, q_ref, o_ref, lse_ref, event):
     def group_body(group, carry):
         keys = k_sc[group]
         values = vt_sc[pl.ds(pl.multiple_of(group * HD, HD), HD), :]
+        event(group)
         for member in range(PER_GROUP):
             head = group * PER_GROUP + member
             at = pl.ds(pl.multiple_of(head * HD, HD), HD)
@@ -143,48 +116,242 @@
         return carry
 
     lax.fori_loop(0, KVH, group_body, 0)
-    attended = o_ref[...].T
-    middle = h_ref[...].astype(HIGH) + nn(attended, wo_ref[...])
+
+
+def lay_keys(kv_ref, k_sc, vt_sc, blocks, rows):
+    for step in range(blocks):
+        at = slice(step * rows, (step + 1) * rows)
+        for group in range(KVH):
+            k_sc[group, at] = kv_ref[step, :, group * HD : (group + 1) * HD]
+        vt_sc[:, at] = kv_ref[step, :, KV_WIDTH:].T
+
+
+def after_attention(h_ref, o_ref, wo_ref, gain_ref, m_ref, b_ref):
+    middle = h_ref[...].astype(HIGH) + nn(o_ref[...].T, wo_ref[...])
     m_ref[...] = middle
-    normed = middle * inverse_rms(middle) * gain_two_ref[...].astype(HIGH)
+    normed = middle * inverse_rms(middle) * gain_ref[...].astype(HIGH)
     b_ref[...] = normed.T.astype(LOW)
-    normed = normed.astype(LOW)
-    total = middle
+    return middle, normed.astype(LOW)
+
+
+def hidden_part(normed, wg, wu, wd, g_ref, u_ref, step):
+    gate = nn(normed, wg[step])
+    up = nn(normed, wu[step])
+    g_ref[step] = gate.astype(LOW)
+    u_ref[step] = up.astype(LOW)
+    active = (gate * sigmoid(gate) * up).astype(LOW)
+    return nn(active, wd[step])
+
+
+def partner(axis, distance):
+    return {axis: jnp.bitwise_xor(lax.axis_index(axis), distance)}
+
+
+def greet(partners):
+    barrier = pltpu.get_barrier_semaphore()
+    for axis, distance in partners:
+        pl.semaphore_signal(barrier, inc=1, device_id=partner(axis, distance), device_id_type=MESH)
+    pl.semaphore_wait(barrier, len(partners))
+
+
+class Links:
+    def __init__(self, send, receive):
+        self.send, self.receive, self.used = send, receive, 0
+        self.flying = []
+
+    def push(self, source, target, to):
+        copy = pltpu.make_async_remote_copy(
+            src_ref=source,
+            dst_ref=target,
+            send_sem=self.send.at[self.used],
+            recv_sem=self.receive.at[self.used],
+            device_id=partner(*to),
+            device_id_type=MESH,
+        )
+        self.used += 1
+        self.flying.append(copy)
+        return copy
+
+    def drain(self):
+        for copy in self.flying:
+            copy.wait_send()
+
+
+SIBLING, ACROSS, SIDE, BEYOND = ("head", 1), ("head", 2), ("dp", 1), ("dp", 2)
+
+
+class Share:
+    def __init__(self, links, kv_ref):
+        self.near = links.push(kv_ref.at[0], kv_ref.at[1], SIBLING)
+        self.far = links.push(kv_ref.at[0], kv_ref.at[2], ACROSS)
+        self.forth = links.push(kv_ref.at[2], kv_ref.at[3], SIBLING)
+
+    def start(self):
+        self.far.start()
+        self.near.start()
+
+    def pass_on(self):
+        self.far.wait_recv()
+        self.forth.start()
+
+    def finish(self):
+        self.near.wait_recv()
+        self.forth.wait_recv()
+
+
+class Spread:
+    def __init__(self, links, own, all_ref):
+        rows = own.shape[0]
+        quarter = rows // 4
+        cut = quarter // 32 * 16
+        place = lax.axis_index("dp") % 4
+
+        def part(ref, which, start=0, size=quarter):
+            first = jnp.bitwise_xor(place, which) * quarter + start
+            return ref.at[pl.ds(pl.multiple_of(first, 16), size)]
+
+        far, diag = all_ref.at[2], all_ref.at[3]
+
+        def move(which, to, *piece):
+            return links.push(part(far, which, *piece), part(far, which, *piece), to)
+
+        def aside(which):
+            return links.push(part(far, which), part(diag, which), SIBLING)
+
+        self.near = links.push(own, all_ref.at[1], SIBLING)
+        self.cross = links.push(part(own, 0), part(far, 0), ACROSS)
+        self.side, self.beyond = move(0, SIDE), move(0, BEYOND)
+        self.side_half = move(2, SIDE, cut, quarter - cut)
+        self.beyond_half = move(1, BEYOND, 0, cut)
+        self.asides = [aside(which) for which in range(4)]
+
+    def start(self):
+        self.cross.start()
+        self.near.start()
+
+    def first(self):
+        self.cross.wait_recv()
+        self.side.start()
+        self.beyond.start()
+        self.asides[0].start()
+
+    def second(self):
+        self.side.wait_recv()
+        self.beyond_half.start()
+        self.asides[1].start()
+        self.beyond.wait_recv()
+        self.side_half.start()
+        self.asides[2].start()
+
+    def third(self):
+        self.side_half.wait_recv()
+        self.beyond_half.wait_recv()
+        self.asides[3].start()
+
+    def last(self):
+        for copy in self.asides:
+            copy.wait_recv()
+
+
+COPIES_SHARE = 3
+COPIES_SPREAD = 10
+
+
+def forward_first_kernel(blocks, *refs):
+    where_ref, h_ref, gain_one_ref, wq_ref, wk_ref, wv_ref, cos_ref, sin_ref, wo_ref, gain_two_ref = refs[:10]
+    owns = refs[10:13]
+    a_ref, q_ref, kv_ref, o_ref, lse_ref, m_ref, b_ref, g_ref, u_ref, out_ref = refs[13:23]
+    next_a, next_q, next_kv = refs[23:26]
+    kept = refs[26:29]
+    bias, k_sc, vt_sc, wg, wu, wd, load, save, send, receive = refs[29:]
+    rows = h_ref.shape[0]
+    links = Links(send, receive)
+    held = (wg, wu, wd)
+    loads = [pltpu.make_async_copy(own, all_ref.at[0], load.at[i]) for i, (own, all_ref) in enumerate(zip(owns, held))]
+    spreads = [Spread(links, own, all_ref) for own, all_ref in zip(owns, held)]
+    shares = [Share(links, ref) for ref in (kv_ref, next_kv)]
+    greet((SIBLING, ACROSS, SIDE, BEYOND))
+    for spread, copy in zip(spreads, loads):
+        spread.start()
+        copy.start()
+    cosine, sine = cos_ref[...], sin_ref[...]
+    gain_one = gain_one_ref[...].astype(HIGH)
+    project(h_ref[...].astype(HIGH), gain_one, wq_ref, wk_ref, wv_ref, cosine, sine, a_ref, q_ref, kv_ref.at[0], shares[0].start)
+    spreads[0].first()
+    fill_bias(where_ref, bias, rows, blocks)
+    shares[0].pass_on()
+    spreads[1].first()
+    shares[0].finish()
+    lay_keys(kv_ref, k_sc, vt_sc, blocks, rows)
+    events = {0: spreads[2].first, 2: spreads[0].second, 3: spreads[1].second, 4: spreads[2].second}
+
+    def event(group):
+        for when, action in events.items():
+            pl.when(group == when)(action)
+
+    attend(bias, k_sc, vt_sc, q_ref, o_ref, lse_ref, event)
+    middle, normed = after_attention(h_ref, o_ref, wo_ref, gain_two_ref, m_ref, b_ref)
+    saves = []
+
+    def keep(step):
+        for which in range(3):
+            copy = pltpu.make_async_copy(held[which].at[step], kept[which].at[step - 1], save.at[which, step - 1])
+            copy.start()
+            saves.append(copy)
+
+    for copy in loads:
+        copy.wait()
+    total = middle + hidden_part(normed, wg, wu, wd, g_ref, u_ref, 0)
+    for spread in spreads:
+        spread.third()
+        spread.near.wait_recv()
+    keep(1)
+    total = total + hidden_part(normed, wg, wu, wd, g_ref, u_ref, 1)
+    keep(2)
+    total = total + hidden_part(normed, wg, wu, wd, g_ref, u_ref, 2)
+    for spread in spreads:
+        spread.last()
+    keep(3)
+    total = total + hidden_part(normed, wg, wu, wd, g_ref, u_ref, 3)
+    out_ref[...] = total
+    project(total, gain_one, wq_ref, wk_ref, wv_ref, cosine, sine, next_a, next_q, next_kv.at[0], shares[1].start)
+    shares[1].pass_on()
+    shares[1].finish()
+    for copy in saves:
+        copy.wait()
+    links.drain()
+
+
+def forward_last_kernel(blocks, *refs):
+    where_ref, h_ref, q_ref, kv_ref, wo_ref, gain_two_ref = refs[:6]
+    sources = refs[6:12]
+    o_ref, lse_ref, m_ref, b_ref, g_ref, u_ref, out_ref = refs[12:19]
+    bias, k_sc, vt_sc, wg, wu, wd, sems = refs[19:]
+    rows = h_ref.shape[0]
+    copies = weights_in(sources, (wg, wu, wd), sems, (0, 1, 2))
+    fill_bias(where_ref, bias, rows, blocks)
+    lay_keys(kv_ref, k_sc, vt_sc, blocks, rows)
+    attend(bias, k_sc, vt_sc, q_ref, o_ref, lse_ref, lambda group: None)
+    total, normed = after_attention(h_ref, o_ref, wo_ref, gain_two_ref, m_ref, b_ref)
     for step in range(blocks):
-        copies[step].wait()
-        gate = nn(normed, wg[step])
-        copies[blocks + step].wait()
-        up = nn(normed, wu[step])
-        g_ref[step] = gate.astype(LOW)
-        u_ref[step] = up.astype(LOW)
-        active = (gate * sigmoid(gate) * up).astype(LOW)
-        copies[2 * blocks + step].wait()
-        total = total + nn(active, wd[step])
-    if last:
-        out_ref[...] = total.astype(LOW)
-    else:
-        out_ref[...] = total
-        gain_one = gain_one_ref[...].astype(HIGH)
-        project(total, gain_one, wq_ref, wk_ref, wv_ref, cos_ref[...], sin_ref[...], next_a, next_q, next_kv)
+        if step < 2:
+            for which in range(3):
+                copies[step, which].wait()
+        total = total + hidden_part(normed, wg, wu, wd, g_ref, u_ref, step)
+    out_ref[...] = total.astype(LOW)
 
 
 def backward_kernel(first, blocks, *refs):
-    where_ref, e_ref, g_ref, u_ref, m_ref, gain_ref, wo_ref, q_ref = refs[:8]
-    kv_refs = refs[8 : 8 + blocks]
-    refs = refs[8 + blocks :]
-    o_ref, lse_ref, cos_ref, sin_ref = refs[:4]
-    wg_any, wu_any, wd_any = (refs[4 + i * blocks : 4 + (i + 1) * blocks] for i in range(3))
-    refs = refs[4 + 3 * blocks :]
-    f_ref, mine_ref, theirs_ref, c_ref, dm_ref, dq_ref, dkv_ref, gain_part_ref = refs[:8]
-    bias, k_sc, v_sc, kt_sc, do_sc, delta, wg, wu, wd, sems = refs[8:]
+    where_ref, e_ref, g_ref, u_ref, m_ref, gain_ref, wo_ref, q_ref, kv_ref = refs[:9]
+    o_ref, lse_ref, cos_ref, sin_ref = refs[9:13]
+    sources = refs[13:19]
+    f_ref, mine_ref, theirs_ref, c_ref, dm_ref, dq_ref, dkv_ref, gain_part_ref = refs[19:27]
+    bias, k_sc, v_sc, kt_sc, do_sc, delta, wg, wu, wd, sems = refs[27:]
     rows = m_ref.shape[0]
-    copies = weights_in((wg_any, wu_any, wd_any), (wg, wu, wd), sems)
-    for step in range(blocks):
-        for which in (2, 0, 1):
-            copies[which * blocks + step].start()
+    copies = weights_in(sources, (wg, wu, wd), sems, (2, 0, 1))
     fill_bias(where_ref, bias, rows, blocks)
     for step in range(blocks):
-        held = kv_refs[step][...]
+        held = kv_ref[step]
         for group in range(KVH):
             at = slice(step * rows, (step + 1) * rows)
             k_sc[group, at] = held[:, group * HD : (group + 1) * HD]
@@ -198,7 +365,8 @@
     low_grad = grad.astype(LOW)
     grad_normed = jnp.zeros(m_ref.shape, HIGH)
     for step in range(blocks):
-        copies[2 * blocks + step].wait()
+        if step < 2:
+            copies[step, 2].wait()
         grad_active = nt(low_grad, wd[step])
         gate = g_ref[step].astype(HIGH)
         up = u_ref[step].astype(HIGH)
@@ -210,8 +378,9 @@
         kept[step // 2] = grad_gate
         kept[2 + step // 2] = grad_up
         kept[4 + step // 2] = (silu * up).astype(LOW)
-        copies[step].wait()
-        copies[blocks + step].wait()
+        if step < 2:
+            copies[step, 0].wait()
+            copies[step, 1].wait()
         grad_normed = grad_normed + nt(grad_gate, wg[step]) + nt(grad_up, wu[step])
     gain_part, grad_middle = norm_back(m_ref[...], gain_ref[...].astype(HIGH), grad_normed, grad)
     gain_part_ref[...] = gain_part
@@ -273,14 +442,17 @@
     dh_ref[...] = grad_in
 
 
-def call(body, outs, specs, scratch, name):
+def call(body, outs, specs, scratch, name, spots=0, collective=None):
+    params = {"vmem_limit_bytes": LIMIT}
+    if collective is not None:
+        params.update(collective_id=collective, has_side_effects=True)
     return pl.pallas_call(
         body,
         out_shape=[jax.ShapeDtypeStruct(shape, kind) for shape, kind in outs],
         in_specs=specs,
-        out_specs=[VMEM] * len(outs),
+        out_specs=[VMEM] * (len(outs) - spots) + [ANY] * spots,
         scratch_shapes=scratch,
-        compiler_params=pltpu.CompilerParams(vmem_limit_bytes=LIMIT),
+        compiler_params=pltpu.CompilerParams(**params),
         name=name,
     )
 
@@ -336,47 +508,49 @@
     gain_one = attn_gain[None, :]
     gain_two = ffn_gain[None, :]
 
-    def everywhere(value):
-        across = swap(value, 2)
-        return [value, swap(value, 1), across, swap(across, 1)]
-
     feature_rows = (width, rows)
-    project_outs = [(feature_rows, LOW), (feature_rows, LOW), ((rows, 2 * KV_WIDTH), LOW)]
-    a_one, q_one, kv_one = call(qkv_kernel, project_outs, [VMEM] * 7, [], "open")(
-        tokens, gain_one, w_query, w_key, w_value, cosine, sine
-    )
-    kv_one = everywhere(kv_one)
-    gates, ups, downs = everywhere(w_gate), everywhere(w_up), everywhere(w_down)
-    weight_scratch = [
-        pltpu.VMEM((blocks, width, hidden), LOW),
-        pltpu.VMEM((blocks, width, hidden), LOW),
-        pltpu.VMEM((blocks, hidden, width), LOW),
-        pltpu.SemaphoreType.DMA((3, blocks)),
+    project_outs = [(feature_rows, LOW), (feature_rows, LOW), ((blocks, rows, 2 * KV_WIDTH), LOW)]
+    weight_shapes = [(width, hidden), (width, hidden), (hidden, width)]
+    weight_room = [pltpu.VMEM((blocks,) + shape, LOW) for shape in weight_shapes]
+    attend_room = [
+        pltpu.VMEM((keys, rows), HIGH),
+        pltpu.VMEM((KVH, keys, HD), LOW),
+        pltpu.VMEM((KV_WIDTH, keys), LOW),
     ]
-
-    def forward(h, queries, kv, last):
-        outs = [
-            (feature_rows, LOW),
-            ((16, rows), HIGH),
-            ((rows, width), HIGH),
-            (feature_rows, LOW),
-            ((blocks, rows, hidden), LOW),
-            ((blocks, rows, hidden), LOW),
-            ((rows, width), LOW if last else HIGH),
-        ]
-        specs = [SMEM] + [VMEM] * (4 + blocks) + [ANY] * (3 * blocks)
-        given = [where, h, queries, *kv, w_output, gain_two, *gates, *ups, *downs]
-        if not last:
-            outs += project_outs
-            specs += [VMEM] * 6
-            given += [gain_one, w_query, w_key, w_value, cosine, sine]
-        scratch = [
-            pltpu.VMEM((keys, rows), HIGH),
-            pltpu.VMEM((KVH, keys, HD), LOW),
-            pltpu.VMEM((KV_WIDTH, keys), LOW),
-        ] + weight_scratch
-        body = functools.partial(forward_kernel, last, blocks)
-        return call(body, outs, specs, scratch, "forward_last" if last else "forward_first")(*given)
+    layer_outs = [
+        (feature_rows, LOW),
+        ((16, rows), HIGH),
+        ((rows, width), HIGH),
+        (feature_rows, LOW),
+        ((blocks, rows, hidden), LOW),
+        ((blocks, rows, hidden), LOW),
+    ]
+
+    def forward_first():
+        outs = project_outs + layer_outs + [((rows, width), HIGH)] + project_outs
+        outs += [((blocks - 1,) + shape, LOW) for shape in weight_shapes]
+        copies = 3 * COPIES_SPREAD + 2 * COPIES_SHARE
+        scratch = attend_room + weight_room
+        scratch += [pltpu.SemaphoreType.DMA((3,)), pltpu.SemaphoreType.DMA((3, blocks - 1))]
+        scratch += [pltpu.SemaphoreType.DMA((copies,)), pltpu.SemaphoreType.DMA((copies,))]
+        body = functools.partial(forward_first_kernel, blocks)
+        specs = [SMEM] + [VMEM] * 9 + [ANY] * 3
+        return call(body, outs, specs, scratch, "forward_first", 3, 1)(
+            where, tokens, gain_one, w_query, w_key, w_value, cosine, sine, w_output, gain_two, w_gate, w_up, w_down
+        )
+
+    outs = forward_first()
+    a_one, q_one, kv_one, o_one, lse_one, m_one, b_one, g_one, u_one, h_one, a_two, q_two, kv_two = outs[:13]
+    weights = [w_gate, outs[13], w_up, outs[14], w_down, outs[15]]
+    weight_scratch = weight_room + [pltpu.SemaphoreType.DMA((3, 2))]
+
+    def forward_last():
+        specs = [SMEM] + [VMEM] * 5 + [ANY] * 6
+        body = functools.partial(forward_last_kernel, blocks)
+        outs = layer_outs + [((rows, width), LOW)]
+        return call(body, outs, specs, attend_room + weight_scratch, "forward_last")(
+            where, h_one, q_two, kv_two, w_output, gain_two, *weights
+        )
 
     def backward(e, kept, first):
         queries, kv, attended, log_totals, middle, gate, up = kept
@@ -390,9 +564,9 @@
             ((blocks, 2 * KV_WIDTH, rows), LOW),
             ((1, width), HIGH),
         ]
-        specs = [SMEM] + [VMEM] * (11 + blocks) + [ANY] * (3 * blocks)
-        given = [where, e, gate, up, middle, gain_two, w_output, queries, *kv, attended, log_totals]
-        given += [cosine, sine, *gates, *ups, *downs]
+        specs = [SMEM] + [VMEM] * 12 + [ANY] * 6
+        given = [where, e, gate, up, middle, gain_two, w_output, queries, kv, attended, log_totals]
+        given += [cosine, sine, *weights]
         scratch = [
             pltpu.VMEM((keys, rows), HIGH),
             pltpu.VMEM((KVH, keys, HD), LOW),
@@ -413,11 +587,7 @@
         given += [partial[0], near, far]
         return call(functools.partial(close_kernel, 3), outs, [VMEM] * 12, [], "close")(*given)
 
-    o_one, lse_one, m_one, b_one, g_one, u_one, h_one, a_two, q_two, kv_two = forward(
-        tokens, q_one, kv_one, False
-    )
-    kv_two = everywhere(kv_two)
-    o_two, lse_two, m_two, b_two, g_two, u_two, block_out = forward(h_one, q_two, kv_two, True)
+    o_two, lse_two, m_two, b_two, g_two, u_two, block_out = forward_last()
     f_two, mine_two, theirs_two, c_two, dm_two, dq_two, part_two, gain_two_b = backward(
         cotangent, (q_two, kv_two, o_two, lse_two, m_two, g_two, u_two), True
     )

time: 462 us -> 416 us (0.900)
  waiting for transfers between devices: 175 us -> 93.5 us
  Pallas kernels: 122 us -> 168 us
  starting transfers between devices: 22.9 us -> 12 us
    ppermute x36 -> x21, waiting for transfers between devices: 146 us -> 65.2 us  [swap(): lax.ppermute(value, 'head', [(i, i ^ distance) for i in range(count)])]
    pallas_call x3 -> x2, Pallas kernels: 52 us -> 99.8 us  [the longest x1 78.8 us: forward_first(): call(body, outs, specs, scratch, 'forward_first', 3, 1)]
    ppermute x36 -> x21, starting transfers between devices: 18 us -> 9.22 us  [swap(): lax.ppermute(value, 'head', [(i, i ^ distance) for i in range(count)])]
    ppermute x3 -> x0, local copies, waits for them, and re-layouts: 7.48 us -> none  [swap(): lax.ppermute(value, 'head', [(i, i ^ distance) for i in range(count)])]
    unnamed x128 -> x120, local copies, waits for them, and re-layouts: 25.9 us -> 27.4 us
  transfers between devices with their start and end apart: 42 -> 27, of which waited for: 10 -> 6; matrix products, arithmetic and copies ran while one was open for 16% -> 15% of each run, Pallas kernels for 21% -> 10%
where the time goes in v2:
time: 416 us; the launch traced here: 411 us
  Pallas kernels  168 us (40%)
  waiting for transfers between devices  93.5 us (22%)
  blocking collectives  54.4 us (13%)
  local copies, waits for them, and re-layouts  45.6 us (11%)
  other arithmetic  18.8 us (5%)
  matrix products  14.7 us (4%)
  starting transfers between devices  12 us (3%)
    pallas_call x1, Pallas kernels, forward_first(): call(body, outs, specs, scratch, 'forward_first', 3, 1)  78.8 us
    ppermute x21, waiting for transfers between devices, swap(): lax.ppermute(value, 'head', [(i, i ^ distance) for i in range(count)])  65.2 us
    pallas_call x2, Pallas kernels, backward(): call(body, outs, specs, scratch, 'backward_last' if first else 'backward_...  57.1 us
    unnamed x1, blocking collectives  45.7 us
    ppermute x6, waiting for transfers between devices, scatter_rows(): got = lax.ppermute(sent, axis, [(i, i ^ bit) for i in range(count)])  28.3 us
    unnamed x120, local copies, waits for them, and re-layouts  27.4 us
    pallas_call x1, Pallas kernels, forward_last(): call(body, outs, specs, attend_room + weight_scratch, 'forward_last')  21 us
    pallas_call x2, Pallas kernels, close(): call(functools.partial(close_kernel, 3), outs, [VMEM] * 12, [], 'close')  11.3 us
  transfers between devices with their start and end apart: 27, of which 6 were waited for; matrix products, arithmetic and copies ran while one was open for 15% of the time, Pallas kernels for 10%

profile of v2, /device:TPU:0, one launch (start us, length us, event | category | flops | bytes accessed | tf_op | source)
XLA Modules:
  0.0 410.6 jit_solution(4948674060552983276)
XLA Ops:
  1.5 2.0 copy.82.refs_1_.refs_0_
  3.5 1.3 broadcast_in_dim.8.refs_2_.refs_1_
  4.8 2.2 copy.83.refs_4_.refs_5_
  7.0 1.2 copy.84.refs_5_.refs_6_
  8.8 1.9 copy.85.refs_12_.refs_10_.refs_17_
  13.2 78.8 %forward_first.1 = (bf16[960,256]{1,0:T(8,128)(2,1)}, bf16[960,256]{1,0:T(8,128)(2,1)}, bf16[4,256,640]{2,1,0:T(8,128)(2,1)}, bf16[960,256]{1,0:T(8,128)(2,1)}, ...) custom-call(s32[2]{0:T(128)} %pad_add_fusion.refs_0_, ...), custom_call_target="tpu_custom_call" | custom-call | tf_op jit(solution)/shard_map/forward_first/pallas_call | solution.py:538
  92.0 21.0 %forward_last.1 = (bf16[960,256]{1,0:T(8,128)(2,1)}, f32[16,256]{1,0:T(8,128)}, f32[256,960]{1,0:T(8,128)}, bf16[960,256]{1,0:T(8,128)(2,1)}, bf16[4,256,640]{2,...) custom-call(s32[2]{0:T(128)} %pad_add_fusion.refs_0_, ...), custom_call_target="tpu_custom_call" | custom-call | tf_op jit(solution)/shard_map/forward_last/pallas_call | solution.py:551
  113.0 28.5 %backward_last.1 = (bf16[960,256]{1,0:T(8,128)(2,1)}, bf16[6,256,640]{2,1,0:T(8,128)(2,1)}, bf16[6,256,640]{2,1,0:T(8,128)(2,1)}, bf16[960,256]{1,0:T(8,128)(2,1...) custom-call(s32[2]{0:T(128)} %pad_add_fusion.refs_0_, ...), custom_call_target="tpu_custom_call" | custom-call | tf_op jit(solution)/shard_map/backward_last/pallas_call | solution.py:579
  141.6 2.0 fusion.96
  144.2 1.0 broadcast_select_fusion.3
  146.2 2.2 broadcast_select_fusion.7
  148.4 1.3 slice_bitcast_fusion.26
  149.7 1.1 fusion.84
  150.8 1.6 collective-permute-start.1
  153.9 6.6 %collective-permute-done.1.refs_11_ = bf16[640,256]{1,0:T(8,128)(2,1)S(1)} collective-permute-done((bf16[640,256]{1,0:T(8,128)(2,1)S(1)}, bf16[640,256]{1,0:T(8,128)(2,1)S(1)}, u32[]{:S(2)}, u32[]{:S(2)}) %collective-permute-start.1) | collective-permute-done | bytes 327712 | tf_op jit(solution)/shard_map/ppermute | solution.py:462
  161.3 5.6 %close.2 = (f32[256,960]{1,0:T(8,128)}, bf16[640,256]{1,0:T(8,128)(2,1)}, f32[1,960]{1,0:T(1,128)}) custom-call(f32[256,960]{1,0:T(8,128)} %get-tuple-element.56.refs_1_.refs_0_, bf16[1,960]{1,0:T(2,128)(2,1)} %broadcast_in_dim.8.refs_2_.refs_1_, f32[256,960]{1,0:T(8,128)} %get-tuple-element.68.refs_2_, bf16[960,256]{1,0:T(8,128)(2,1)} %get-tuple-element.69.refs_3_, ...), custom_call_target="tpu_custom_call" | custom-call | tf_op jit(solution)/shard_map/close/pallas_call | solution.py:588
  166.9 28.6 %backward_first.1 = (bf16[960,256]{1,0:T(8,128)(2,1)}, bf16[6,256,640]{2,1,0:T(8,128)(2,1)}, bf16[6,256,640]{2,1,0:T(8,128)(2,1)}, bf16[960,256]{1,0:T(8,128)(2,...) custom-call(s32[2]{0:T(128)} %pad_add_fusion.refs_0_, ...), custom_call_target="tpu_custom_call" | custom-call | tf_op jit(solution)/shard_map/backward_first/pallas_call | solution.py:579
  196.9 1.9 constant_dynamic-update-slice_fusion.2
  198.9 1.9 constant_dynamic-update-slice_fusion.1
  200.7 1.9 constant_dynamic-update-slice_fusion.6
  205.2 1.0 slice_bitcast_fusion.25
  206.7 1.6 collective-permute-start.3
  208.3 1.0 slice_bitcast_fusion.12
  209.3 2.7 slice_bitcast_fusion.11
  212.0 1.7 convolution_convert_fusion.1
  213.7 1.7 convolution_convert_fusion.2
  215.4 1.7 convolution_convert_fusion
  217.2 2.2 pad_maximum_fusion
  222.5 5.7 %close.3 = (f32[256,960]{1,0:T(8,128)}, bf16[640,256]{1,0:T(8,128)(2,1)}, f32[1,960]{1,0:T(1,128)}) custom-call(bf16[256,960]{1,0:T(8,128)(2,1)} %copy.82.refs_1_.refs_0_, bf16[1,960]{1,0:T(2,128)(2,1)} %broadcast_in_dim.8.refs_2_.refs_1_, f32[256,960]{1,0:T(8,128)} %get-tuple-element.79.refs_2_, bf16[960,256]{1,0:T(8,128)(2,1)} %get-tuple-element.80.refs_3_, ...), custom_call_target="tpu_custom_call" | custom-call | tf_op jit(solution)/shard_map/close/pallas_call | solution.py:588
  228.2 1.0 broadcast_select_fusion.9
  230.8 3.7 fusion.26
  237.8 1.7 convolution_convert_fusion.3
  239.7 1.7 convolution_convert_fusion.4
  241.5 1.7 convolution_convert_fusion.5
  243.2 58.3 %collective-permute-done.23 = bf16[960,1920]{1,0:T(8,128)(2,1)} collective-permute-done((bf16[960,1920]{1,0:T(8,128)(2,1)}, bf16[960,1920]{1,0:T(8,128)(2,1)}, u32[]{:S(2)}, u32[]{:S(2)}) %collective-permute-start.23) | collective-permute-done | bytes 3686432 | tf_op jit(solution)/shard_map/ppermute | solution.py:462
  301.5 2.5 add_convert_fusion
  306.8 1.4 collective-permute-start.13
  308.2 2.0 copy.98
  311.5 2.5 copy.99
  314.0 45.7 %all-reduce = f32[2,960]{1,0:T(2,128)S(1)} all-reduce(f32[2,960]{1,0:T(2,128)S(1)} %pad_maximum_fusion.4), channel_id=2, replica_groups=mesh['dp'=8,'head'=4] {'dp'}, use_global_device_ids=true, to_apply=%region_1.2.clone | all-reduce | flops 1920 | bytes 15360
  359.8 1.2 fusion.76
  361.2 2.5 fusion
  364.7 7.1 %collective-permute-done.14 = bf16[1,120,1280]{2,1,0:T(8,128)(2,1)S(1)} collective-permute-done((bf16[1,120,1280]{2,1,0:T(8,128)(2,1)S(1)}, bf16[1,120,1280]{2,1,0:T(8,128)(2,1)S(1)}, u32[]{:S(2)}, u32[]{:S(2)}) %collective-permute-start.14) | collective-permute-done | bytes 307232 | tf_op jit(solution)/shard_map/ppermute | solution.py:475
  371.8 1.3 collective-permute-start.15
  373.2 8.7 %psum.8 = f32[2,120]{1,0:T(2,128)S(1)} all-reduce(f32[2,120]{1,0:T(2,128)S(1)} %constant_dynamic-slice_fusion.2), channel_id=1, replica_groups=mesh['dp'=8,'head'=4] {'head'}, use_global_device_ids=true, to_apply=%region_0.1 | all-reduce | flops 240 | bytes 1920 | tf_op jit(solution)/shard_map/psum | solution.py:637
  382.5 5.7 %collective-permute-done.25 = bf16[2,120,1920]{2,1,0:T(8,128)(2,1)} collective-permute-done((bf16[2,120,1920]{2,1,0:T(8,128)(2,1)}, bf16[2,120,1920]{2,1,0:T(8,128)(2,1)}, u32[]{:S(2)}, u32[]{:S(2)}) %collective-permute-start.25) | collective-permute-done | bytes 921632 | tf_op jit(solution)/shard_map/ppermute | solution.py:475
  388.2 1.4 fusion.25
  393.5 15.6 %collective-permute-done.26 = bf16[1,120,1920]{2,1,0:T(8,128)(2,1)S(1)} collective-permute-done((bf16[1,120,1920]{2,1,0:T(8,128)(2,1)S(1)}, bf16[1,120,1920]{2,1,0:T(8,128)(2,1)S(1)}, u32[]{:S(2)}, u32[]{:S(2)}) %collective-permute-start.26) | collective-permute-done | bytes 460832 | tf_op jit(solution)/shard_map/ppermute | solution.py:475
  (195 shorter events, 29.6 us)
Async XLA Ops:
  0.6 6.4 %copy-start.9 = (bf16[960,320]{0,1:T(8,128)(2,1)S(1)}, bf16[960,320]{0,1:T(8,128)(2,1)}, u32[]{:S(2)}) copy-start(bf16[960,320]{0,1:T(8,128)(2,1)} %param.18) | copy-start | bytes 1843204
  0.7 7.6 %copy-start.47 = (bf16[960]{0:T(1024)(128)(2,1)S(1)}, bf16[960]{0:T(1024)(128)(2,1)}, u32[]{:S(2)}) copy-start(bf16[960]{0:T(1024)(128)(2,1)} %param.20) | copy-start | bytes 5764
  0.7 8.2 %copy-start.8 = (bf16[640,960]{0,1:T(8,128)(2,1)S(1)}, bf16[640,960]{0,1:T(8,128)(2,1)}, u32[]{:S(2)}) copy-start(bf16[640,960]{0,1:T(8,128)(2,1)} %param.23) | copy-start | bytes 3686404
  7.0 3.7 copy-start.10
  143.7 6.0 %collective-permute-start = (bf16[2,640,256]{2,1,0:T(8,128)(2,1)S(1)}, bf16[2,640,256]{2,1,0:T(8,128)(2,1)S(1)}, u32[]{:S(2)}, u32[]{:S(2)}) collective-permute-start(bf16[2,640,256]{2,1,0:T(8,128)(2,1)S(1)} %pad_maximum_fusion.2), channel_id=1, source_target_pairs={{0,1},{1,0},{2,3},{3,2},{4,5},{5,4},{6,7},{7,6},{8,9},{9,8},{10,11... | collective-permute-start | bytes 1966088 | tf_op jit(solution)/shard_map/ppermute | solution.py:462
  144.2 4.2 %copy-start.2 = (bf16[6,256,640]{2,1,0:T(8,128)(2,1)S(1)}, bf16[6,256,640]{2,1,0:T(8,128)(2,1)}, u32[]{:S(2)}) copy-start(bf16[6,256,640]{2,1,0:T(8,128)(2,1)} %get-tuple-element.95) | copy-start | bytes 5898244
  145.2 84.0 %collective-permute-start.6 = (bf16[960,256]{1,0:T(8,128)(2,1)}, bf16[960,256]{1,0:T(8,128)(2,1)}, u32[]{:S(2)}, u32[]{:S(2)}) collective-permute-start(bf16[960,256]{1,0:T(8,128)(2,1)} %get-tuple-element.180), channel_id=1, source_target_pairs={{0,1},{1,0},{2,3},{3,2},{4,5},{5,4},{6,7},{7,6},{8,9},{9,8},{10,11... | collective-permute-start | bytes 1474568 | tf_op jit(solution)/shard_map/ppermute | solution.py:462
  145.3 55.5 %collective-permute-start.21 = (bf16[960,256]{1,0:T(8,128)(2,1)}, bf16[960,256]{1,0:T(8,128)(2,1)}, u32[]{:S(2)}, u32[]{:S(2)}) collective-permute-start(bf16[960,256]{1,0:T(8,128)(2,1)} %get-tuple-element.99), channel_id=1, source_target_pairs={{0,1},{1,0},{2,3},{3,2},{4,5},{5,4},{6,7},{7,6},{8,9},{9,8},{10,11... | collective-permute-start | bytes 1474568 | tf_op jit(solution)/shard_map/ppermute | solution.py:462
  145.7 62.6 %collective-permute-start.19 = (bf16[6,256,640]{2,1,0:T(8,128)(2,1)}, bf16[6,256,640]{2,1,0:T(8,128)(2,1)S(1)}, u32[]{:S(2)}, u32[]{:S(2)}) collective-permute-start(bf16[6,256,640]{2,1,0:T(8,128)(2,1)} %get-tuple-element.96), channel_id=1, source_target_pairs={{0,1},{1,0},{2,3},{3,2},{4,5},{5,4},{6,7},{7,6},{8,9},{9,8},{10,11... | collective-permute-start | bytes 5898248 | tf_op jit(solution)/shard_map/ppermute | solution.py:462
  145.8 50.7 %collective-permute-start.17 = (bf16[960,256]{1,0:T(8,128)(2,1)}, bf16[960,256]{1,0:T(8,128)(2,1)}, u32[]{:S(2)}, u32[]{:S(2)}) collective-permute-start(bf16[960,256]{1,0:T(8,128)(2,1)} %get-tuple-element.93), channel_id=1, source_target_pairs={{0,1},{1,0},{2,3},{3,2},{4,5},{5,4},{6,7},{7,6},{8,9},{9,8},{10,11... | collective-permute-start | bytes 1474568 | tf_op jit(solution)/shard_map/ppermute | solution.py:462
  148.4 3.9 copy-start.17
  150.8 9.8 %collective-permute-start.1 = (bf16[640,256]{1,0:T(8,128)(2,1)S(1)}, bf16[640,256]{1,0:T(8,128)(2,1)S(1)}, u32[]{:S(2)}, u32[]{:S(2)}) collective-permute-start(bf16[640,256]{1,0:T(8,128)(2,1)S(1)} %fusion.84), channel_id=1, source_target_pairs={{0,2},{1,3},{2,0},{3,1},{4,6},{5,7},{6,4},{7,5},{8,10},{9,11},{10,... | collective-permute-start | bytes 983048 | tf_op jit(solution)/shard_map/ppermute | solution.py:462
  166.9 28.7 %copy-start.18 = (bf16[960,256]{1,0:T(8,128)(2,1)S(1)}, bf16[960,256]{1,0:T(8,128)(2,1)}, u32[]{:S(2)}) copy-start(bf16[960,256]{1,0:T(8,128)(2,1)} %get-tuple-element.93) | copy-start | bytes 1474564
  195.5 7.2 %copy-start.7 = (bf16[4,640,256]{2,1,0:T(8,128)(2,1)S(1)}, bf16[4,640,256]{2,1,0:T(8,128)(2,1)}, u32[]{:S(2)}) copy-start(bf16[4,640,256]{2,1,0:T(8,128)(2,1)} %get-tuple-element.81) | copy-start | bytes 3932164
  195.5 13.8 %collective-permute-start.20 = (bf16[6,256,640]{2,1,0:T(8,128)(2,1)}, bf16[6,256,640]{2,1,0:T(8,128)(2,1)}, u32[]{:S(2)}, u32[]{:S(2)}) collective-permute-start(bf16[6,256,640]{2,1,0:T(8,128)(2,1)} %get-tuple-element.98), channel_id=1, source_target_pairs={{0,1},{1,0},{2,3},{3,2},{4,5},{5,4},{6,7},{7,6},{8,9},{9,8},{10,11... | collective-permute-start | bytes 5898248 | tf_op jit(solution)/shard_map/ppermute | solution.py:462
  196.5 7.2 %collective-permute-start.18 = (bf16[960,256]{1,0:T(8,128)(2,1)}, bf16[960,256]{1,0:T(8,128)(2,1)S(1)}, u32[]{:S(2)}, u32[]{:S(2)}) collective-permute-start(bf16[960,256]{1,0:T(8,128)(2,1)} %get-tuple-element.94), channel_id=1, source_target_pairs={{0,1},{1,0},{2,3},{3,2},{4,5},{5,4},{6,7},{7,6},{8,9},{9,8},{10,11... | collective-permute-start | bytes 1474568 | tf_op jit(solution)/shard_map/ppermute | solution.py:462
  200.7 2.9 copy-start.19
  203.6 3.1 collective-permute-start.2
  203.7 2.8 collective-permute-start.22
  206.5 23.0 %collective-permute-start.4 = (bf16[960,256]{1,0:T(8,128)(2,1)S(1)}, bf16[960,256]{1,0:T(8,128)(2,1)}, u32[]{:S(2)}, u32[]{:S(2)}) collective-permute-start(bf16[960,256]{1,0:T(8,128)(2,1)S(1)} %copy-done.15), channel_id=1, source_target_pairs={{0,1},{1,0},{2,3},{3,2},{4,5},{5,4},{6,7},{7,6},{8,9},{9,8},{10,11... | collective-permute-start | bytes 1474568 | tf_op jit(solution)/shard_map/ppermute | solution.py:462
  206.6 8.8 %copy-start.39 = (bf16[960,1024]{1,0:T(8,128)(2,1)}, bf16[960,1024]{1,0:T(8,128)(2,1)S(1)}, u32[]{:S(2)}) copy-start(bf16[960,1024]{1,0:T(8,128)(2,1)S(1)} %constant_dynamic-update-slice_fusion.4) | copy-start | bytes 5898244
  206.7 13.9 %collective-permute-start.3 = (bf16[640,256]{1,0:T(8,128)(2,1)S(1)}, bf16[640,256]{1,0:T(8,128)(2,1)S(1)}, u32[]{:S(2)}, u32[]{:S(2)}) collective-permute-start(bf16[640,256]{1,0:T(8,128)(2,1)S(1)} %fusion.85), channel_id=1, source_target_pairs={{0,2},{1,3},{2,0},{3,1},{4,6},{5,7},{6,4},{7,5},{8,10},{9,11},{10,... | collective-permute-start | bytes 983048 | tf_op jit(solution)/shard_map/ppermute | solution.py:462
  209.3 2.7 copy-start.41
  217.1 2.8 copy-start.3
  217.2 2.8 copy-start.4
  219.4 82.1 %collective-permute-start.23 = (bf16[960,1920]{1,0:T(8,128)(2,1)}, bf16[960,1920]{1,0:T(8,128)(2,1)}, u32[]{:S(2)}, u32[]{:S(2)}) collective-permute-start(bf16[960,1920]{1,0:T(8,128)(2,1)} %pad_maximum_fusion), channel_id=1, source_target_pairs={{0,2},{1,3},{2,0},{3,1},{4,6},{5,7},{6,4},{7,5},{8,10},{9,11},{10,... | collective-permute-start | bytes 11059208 | tf_op jit(solution)/shard_map/ppermute | solution.py:462
  220.1 9.7 %collective-permute-start.7 = (bf16[960,256]{1,0:T(8,128)(2,1)S(1)}, bf16[960,256]{1,0:T(8,128)(2,1)S(1)}, u32[]{:S(2)}, u32[]{:S(2)}) collective-permute-start(bf16[960,256]{1,0:T(8,128)(2,1)S(1)} %get-tuple-element.182), channel_id=1, source_target_pairs={{0,1},{1,0},{2,3},{3,2},{4,5},{5,4},{6,7},{7,6},{8,9},{9,8},{10,11... | collective-permute-start | bytes 1474568 | tf_op jit(solution)/shard_map/ppermute | solution.py:462
  220.6 9.4 %collective-permute-start.5 = (bf16[960,256]{1,0:T(8,128)(2,1)S(1)}, bf16[960,256]{1,0:T(8,128)(2,1)S(1)}, u32[]{:S(2)}, u32[]{:S(2)}) collective-permute-start(bf16[960,256]{1,0:T(8,128)(2,1)S(1)} %get-tuple-element.178), channel_id=1, source_target_pairs={{0,1},{1,0},{2,3},{3,2},{4,5},{5,4},{6,7},{7,6},{8,9},{9,8},{10,11... | collective-permute-start | bytes 1474568 | tf_op jit(solution)/shard_map/ppermute | solution.py:462
  222.5 7.0 %copy-start.12 = (bf16[960,256]{1,0:T(8,128)(2,1)S(1)}, bf16[960,256]{1,0:T(8,128)(2,1)}, u32[]{:S(2)}) copy-start(bf16[960,256]{1,0:T(8,128)(2,1)} %get-tuple-element.87) | copy-start | bytes 1474564
  222.5 8.3 %copy-start.13 = (bf16[960,256]{1,0:T(8,128)(2,1)S(1)}, bf16[960,256]{1,0:T(8,128)(2,1)}, u32[]{:S(2)}) copy-start(bf16[960,256]{1,0:T(8,128)(2,1)} %get-tuple-element.179) | copy-start | bytes 1474564
  222.5 8.3 %copy-start.14 = (bf16[960,256]{1,0:T(8,128)(2,1)S(1)}, bf16[960,256]{1,0:T(8,128)(2,1)}, u32[]{:S(2)}) copy-start(bf16[960,256]{1,0:T(8,128)(2,1)} %get-tuple-element.175) | copy-start | bytes 1474564
  229.2 5.3 %collective-permute-start.9 = (bf16[960,256]{1,0:T(8,128)(2,1)S(1)}, bf16[960,256]{1,0:T(8,128)(2,1)S(1)}, u32[]{:S(2)}, u32[]{:S(2)}) collective-permute-start(bf16[960,256]{1,0:T(8,128)(2,1)S(1)} %copy-done.11), channel_id=1, source_target_pairs={{0,1},{1,0},{2,3},{3,2},{4,5},{5,4},{6,7},{7,6},{8,9},{9,8},{10,11... | collective-permute-start | bytes 1474568 | tf_op jit(solution)/shard_map/ppermute | solution.py:462
  229.5 5.0 %collective-permute-start.8 = (bf16[960,256]{1,0:T(8,128)(2,1)S(1)}, bf16[960,256]{1,0:T(8,128)(2,1)S(1)}, u32[]{:S(2)}, u32[]{:S(2)}) collective-permute-start(bf16[960,256]{1,0:T(8,128)(2,1)S(1)} %copy-done.12), channel_id=1, source_target_pairs={{0,1},{1,0},{2,3},{3,2},{4,5},{5,4},{6,7},{7,6},{8,9},{9,8},{10,11... | collective-permute-start | bytes 1474568 | tf_op jit(solution)/shard_map/ppermute | solution.py:462
  229.8 4.7 %collective-permute-start.10 = (bf16[320,256]{1,0:T(8,128)(2,1)}, bf16[320,256]{1,0:T(8,128)(2,1)S(1)}, u32[]{:S(2)}, u32[]{:S(2)}) collective-permute-start(bf16[320,256]{1,0:T(8,128)(2,1)} %get-tuple-element.189), channel_id=1, source_target_pairs={{0,1},{1,0},{2,3},{3,2},{4,5},{5,4},{6,7},{7,6},{8,9},{9,8},{10,11... | collective-permute-start | bytes 491528 | tf_op jit(solution)/shard_map/ppermute | solution.py:462
  230.0 4.5 %collective-permute-start.11 = (bf16[320,256]{1,0:T(8,128)(2,1)S(1)}, bf16[320,256]{1,0:T(8,128)(2,1)S(1)}, u32[]{:S(2)}, u32[]{:S(2)}) collective-permute-start(bf16[320,256]{1,0:T(8,128)(2,1)S(1)} %get-tuple-element.191), channel_id=1, source_target_pairs={{0,1},{1,0},{2,3},{3,2},{4,5},{5,4},{6,7},{7,6},{8,9},{9,8},{10,11... | collective-permute-start | bytes 491528 | tf_op jit(solution)/shard_map/ppermute | solution.py:462
  236.5 68.3 %collective-permute-start.12 = (bf16[4,120,1280]{2,1,0:T(8,128)(2,1)S(1)}, bf16[4,120,1280]{2,1,0:T(8,128)(2,1)S(1)}, u32[]{:S(2)}, u32[]{:S(2)}) collective-permute-start(bf16[4,120,1280]{2,1,0:T(8,128)(2,1)S(1)} %dynamic-slice_bitcast_fusion.1), channel_id=1, source_target_pairs={{0,4},{4,0},{8,12},{12,8},{16,20},{20,16},{24,28},{28,24},{1,5},{5... | collective-permute-start | bytes 3686408 | tf_op jit(solution)/shard_map/ppermute | solution.py:475
  304.2 57.0 %collective-permute-start.24 = (bf16[4,120,1920]{2,1,0:T(8,128)(2,1)S(1)}, bf16[4,120,1920]{2,1,0:T(8,128)(2,1)}, u32[]{:S(2)}, u32[]{:S(2)}) collective-permute-start(bf16[4,120,1920]{2,1,0:T(8,128)(2,1)S(1)} %dynamic-slice_bitcast_fusion), channel_id=1, source_target_pairs={{0,4},{4,0},{8,12},{12,8},{16,20},{20,16},{24,28},{28,24},{1,5},{5... | collective-permute-start | bytes 5529608 | tf_op jit(solution)/shard_map/ppermute | solution.py:475
  305.9 4.3 %copy-start.50 = (u32[32]{0:T(128)S(1)}, u32[32]{0:T(128)}, u32[]{:S(2)}) copy-start(u32[32]{0:T(128)} %constant.128) | copy-start | bytes 388
  305.9 5.6 %copy-start.43 = (f32[1,960]{1,0:T(1,128)S(1)}, f32[1,960]{1,0:T(1,128)}, u32[]{:S(2)}) copy-start(f32[1,960]{1,0:T(1,128)} %get-tuple-element.86) | copy-start | bytes 11524
  305.9 5.6 %copy-start.45 = (f32[1,960]{1,0:T(1,128)S(1)}, f32[1,960]{1,0:T(1,128)}, u32[]{:S(2)}) copy-start(f32[1,960]{1,0:T(1,128)} %get-tuple-element.85) | copy-start | bytes 11524
  305.9 8.1 %copy-start.44 = (f32[1,960]{1,0:T(1,128)S(1)}, f32[1,960]{1,0:T(1,128)}, u32[]{:S(2)}) copy-start(f32[1,960]{1,0:T(1,128)} %get-tuple-element.84) | copy-start | bytes 11524
  305.9 8.1 %copy-start.46 = (f32[1,960]{1,0:T(1,128)S(1)}, f32[1,960]{1,0:T(1,128)}, u32[]{:S(2)}) copy-start(f32[1,960]{1,0:T(1,128)} %get-tuple-element.83) | copy-start | bytes 11524
  306.8 53.0 %collective-permute-start.13 = (bf16[2,120,1280]{2,1,0:T(8,128)(2,1)}, bf16[2,120,1280]{2,1,0:T(8,128)(2,1)}, u32[]{:S(2)}, u32[]{:S(2)}) collective-permute-start(bf16[2,120,1280]{2,1,0:T(8,128)(2,1)} %dynamic-slice_bitcast_fusion.3), channel_id=1, source_target_pairs={{0,8},{4,12},{8,0},{12,4},{16,24},{20,28},{24,16},{28,20},{1,9},{5... | collective-permute-start | bytes 1843208 | tf_op jit(solution)/shard_map/ppermute | solution.py:475
  361.1 10.7 %collective-permute-start.14 = (bf16[1,120,1280]{2,1,0:T(8,128)(2,1)S(1)}, bf16[1,120,1280]{2,1,0:T(8,128)(2,1)S(1)}, u32[]{:S(2)}, u32[]{:S(2)}) collective-permute-start(bf16[1,120,1280]{2,1,0:T(8,128)(2,1)S(1)} %constant_dynamic-slice_fusion.1), channel_id=1, source_target_pairs={{0,16},{4,20},{8,24},{12,28},{16,0},{20,4},{24,8},{28,12},{1,17},{... | collective-permute-start | bytes 921608 | tf_op jit(solution)/shard_map/ppermute | solution.py:475
  364.7 23.5 %collective-permute-start.25 = (bf16[2,120,1920]{2,1,0:T(8,128)(2,1)}, bf16[2,120,1920]{2,1,0:T(8,128)(2,1)}, u32[]{:S(2)}, u32[]{:S(2)}) collective-permute-start(bf16[2,120,1920]{2,1,0:T(8,128)(2,1)} %dynamic-slice_bitcast_fusion.2), channel_id=1, source_target_pairs={{0,8},{4,12},{8,0},{12,4},{16,24},{20,28},{24,16},{28,20},{1,9},{5... | collective-permute-start | bytes 2764808 | tf_op jit(solution)/shard_map/ppermute | solution.py:475
  371.8 10.5 %collective-permute-start.15 = (bf16[120,1280]{1,0:T(8,128)(2,1)S(1)}, bf16[120,1280]{1,0:T(8,128)(2,1)S(1)}, u32[]{:S(2)}, u32[]{:S(2)}) collective-permute-start(bf16[120,1280]{1,0:T(8,128)(2,1)S(1)} %fusion.86), channel_id=1, source_target_pairs={{0,2},{1,3},{2,0},{3,1},{4,6},{5,7},{6,4},{7,5},{8,10},{9,11},{10,... | collective-permute-start | bytes 921608 | tf_op jit(solution)/shard_map/ppermute | solution.py:462
  382.4 7.3 %collective-permute-start.16 = (bf16[120,1280]{1,0:T(8,128)(2,1)S(1)}, bf16[120,1280]{1,0:T(8,128)(2,1)S(1)}, u32[]{:S(2)}, u32[]{:S(2)}) collective-permute-start(bf16[120,1280]{1,0:T(8,128)(2,1)S(1)} %add_convert_fusion.3), channel_id=1, source_target_pairs={{0,1},{1,0},{2,3},{3,2},{4,5},{5,4},{6,7},{7,6},{8,9},{9,8},{10,11... | collective-permute-start | bytes 921608 | tf_op jit(solution)/shard_map/ppermute | solution.py:462
  389.7 19.4 %collective-permute-start.26 = (bf16[1,120,1920]{2,1,0:T(8,128)(2,1)S(1)}, bf16[1,120,1920]{2,1,0:T(8,128)(2,1)S(1)}, u32[]{:S(2)}, u32[]{:S(2)}) collective-permute-start(bf16[1,120,1920]{2,1,0:T(8,128)(2,1)S(1)} %constant_dynamic-slice_fusion), channel_id=1, source_target_pairs={{0,16},{4,20},{8,24},{12,28},{16,0},{20,4},{24,8},{28,12},{1,17},{... | collective-permute-start | bytes 1382408 | tf_op jit(solution)/shard_map/ppermute | solution.py:475
  (30 other events, 48.3 us)

commit v3 on v2

--- a/solution.py
+++ b/solution.py
@@ -21,7 +21,7 @@
 VMEM = pl.BlockSpec(memory_space=pltpu.VMEM)
 SMEM = pl.BlockSpec(memory_space=pltpu.SMEM)
 ANY = pl.BlockSpec(memory_space=pl.ANY)
-LIMIT = 58 * 2**20
+LIMIT = 60 * 2**20
 MESH = pl.DeviceIdType.MESH
 
 
@@ -63,9 +63,9 @@
 def project(hidden, gain, w_query, w_key, w_value, cosine, sine, a_ref, q_ref, kv_ref, ready):
     normed = hidden * inverse_rms(hidden) * gain
     low = normed.astype(LOW)
-    keys = turned(nn(low, w_key[...]).T, cosine, sine, 1.0, 1.0)
+    keys = turned(nt(w_key[...], low), cosine, sine, 1.0, 1.0)
     kv_ref[:, :KV_WIDTH] = keys.T.astype(LOW)
-    kv_ref[:, KV_WIDTH:] = nn(low, w_value[...]).astype(LOW)
+    kv_ref[:, KV_WIDTH:] = nt(low, w_value[...]).astype(LOW)
     ready()
     queries = nn(low, w_query[...]).T
     q_ref[...] = turned(queries, cosine, sine, 1.0, SCALE).astype(LOW)
@@ -126,8 +126,8 @@
         vt_sc[:, at] = kv_ref[step, :, KV_WIDTH:].T
 
 
-def after_attention(h_ref, o_ref, wo_ref, gain_ref, m_ref, b_ref):
-    middle = h_ref[...].astype(HIGH) + nn(o_ref[...].T, wo_ref[...])
+def after_attention(hidden, o_ref, wo_ref, gain_ref, m_ref, b_ref):
+    middle = hidden + nn(o_ref[...].T, wo_ref[...])
     m_ref[...] = middle
     normed = middle * inverse_rms(middle) * gain_ref[...].astype(HIGH)
     b_ref[...] = normed.T.astype(LOW)
@@ -140,7 +140,7 @@
     g_ref[step] = gate.astype(LOW)
     u_ref[step] = up.astype(LOW)
     active = (gate * sigmoid(gate) * up).astype(LOW)
-    return nn(active, wd[step])
+    return nt(active, wd[step])
 
 
 def partner(axis, distance):
@@ -264,7 +264,8 @@
     next_a, next_q, next_kv = refs[23:26]
     kept = refs[26:29]
     bias, k_sc, vt_sc, wg, wu, wd, load, save, send, receive = refs[29:]
-    rows = h_ref.shape[0]
+    rows = h_ref.shape[1]
+    hidden = h_ref[...].astype(HIGH).T
     links = Links(send, receive)
     held = (wg, wu, wd)
     loads = [pltpu.make_async_copy(own, all_ref.at[0], load.at[i]) for i, (own, all_ref) in enumerate(zip(owns, held))]
@@ -276,7 +277,7 @@
         copy.start()
     cosine, sine = cos_ref[...], sin_ref[...]
     gain_one = gain_one_ref[...].astype(HIGH)
-    project(h_ref[...].astype(HIGH), gain_one, wq_ref, wk_ref, wv_ref, cosine, sine, a_ref, q_ref, kv_ref.at[0], shares[0].start)
+    project(hidden, gain_one, wq_ref, wk_ref, wv_ref, cosine, sine, a_ref, q_ref, kv_ref.at[0], shares[0].start)
     spreads[0].first()
     fill_bias(where_ref, bias, rows, blocks)
     shares[0].pass_on()
@@ -290,7 +291,7 @@
             pl.when(group == when)(action)
 
     attend(bias, k_sc, vt_sc, q_ref, o_ref, lse_ref, event)
-    middle, normed = after_attention(h_ref, o_ref, wo_ref, gain_two_ref, m_ref, b_ref)
+    middle, normed = after_attention(hidden, o_ref, wo_ref, gain_two_ref, m_ref, b_ref)
     saves = []
 
     def keep(step):
@@ -332,42 +333,24 @@
     fill_bias(where_ref, bias, rows, blocks)
     lay_keys(kv_ref, k_sc, vt_sc, blocks, rows)
     attend(bias, k_sc, vt_sc, q_ref, o_ref, lse_ref, lambda group: None)
-    total, normed = after_attention(h_ref, o_ref, wo_ref, gain_two_ref, m_ref, b_ref)
+    total, normed = after_attention(h_ref[...], o_ref, wo_ref, gain_two_ref, m_ref, b_ref)
     for step in range(blocks):
         if step < 2:
             for which in range(3):
                 copies[step, which].wait()
         total = total + hidden_part(normed, wg, wu, wd, g_ref, u_ref, step)
-    out_ref[...] = total.astype(LOW)
-
-
-def backward_kernel(first, blocks, *refs):
-    where_ref, e_ref, g_ref, u_ref, m_ref, gain_ref, wo_ref, q_ref, kv_ref = refs[:9]
-    o_ref, lse_ref, cos_ref, sin_ref = refs[9:13]
-    sources = refs[13:19]
-    f_ref, mine_ref, theirs_ref, c_ref, dm_ref, dq_ref, dkv_ref, gain_part_ref = refs[19:27]
-    bias, k_sc, v_sc, kt_sc, do_sc, delta, wg, wu, wd, sems = refs[27:]
-    rows = m_ref.shape[0]
-    copies = weights_in(sources, (wg, wu, wd), sems, (2, 0, 1))
-    fill_bias(where_ref, bias, rows, blocks)
-    for step in range(blocks):
-        held = kv_ref[step]
-        for group in range(KVH):
-            at = slice(step * rows, (step + 1) * rows)
-            k_sc[group, at] = held[:, group * HD : (group + 1) * HD]
-            v_sc[group, at] = held[:, KV_WIDTH + group * HD : KV_WIDTH + (group + 1) * HD]
-        kt_sc[:, step * rows : (step + 1) * rows] = held[:, :KV_WIDTH].T
-    grad = e_ref[...].astype(HIGH)
-    if first:
-        row = where_ref[0] * rows + lax.broadcasted_iota(jnp.int32, (rows, 1), 0)
-        grad = jnp.where(row < where_ref[1], grad, 0.0)
+    out_ref[...] = total.T.astype(LOW)
+
+
+def ffn_back(grad, copies, g_ref, u_ref, m_ref, gain_ref, wg, wu, wd, outs):
+    f_ref, mine_ref, theirs_ref, c_ref, dm_ref, gain_part_ref = outs
     f_ref[...] = grad.T.astype(LOW)
     low_grad = grad.astype(LOW)
     grad_normed = jnp.zeros(m_ref.shape, HIGH)
-    for step in range(blocks):
+    for step in range(wg.shape[0]):
         if step < 2:
             copies[step, 2].wait()
-        grad_active = nt(low_grad, wd[step])
+        grad_active = nn(low_grad, wd[step])
         gate = g_ref[step].astype(HIGH)
         up = u_ref[step].astype(HIGH)
         sig = sigmoid(gate)
@@ -386,13 +369,25 @@
     gain_part_ref[...] = gain_part
     dm_ref[...] = grad_middle
     c_ref[...] = grad_middle.T.astype(LOW)
+    return grad_middle
+
+
+def attend_back(where_ref, kv_ref, wo_ref, q_ref, o_ref, lse_ref, cosine, sine, grad_middle, dq_ref, dkv_ref, room):
+    bias, k_sc, v_sc, kt_sc, do_sc, delta = room
+    blocks, rows = kv_ref.shape[:2]
+    fill_bias(where_ref, bias, rows, blocks)
+    for step in range(blocks):
+        at = slice(step * rows, (step + 1) * rows)
+        held = kv_ref[step]
+        for group in range(KVH):
+            k_sc[group, at] = held[:, group * HD : (group + 1) * HD]
+            v_sc[group, at] = held[:, KV_WIDTH + group * HD : KV_WIDTH + (group + 1) * HD]
+        kt_sc[:, at] = held[:, :KV_WIDTH].T
     do_sc[...] = nt(wo_ref[...], grad_middle.astype(LOW)).astype(LOW)
     for head in range(HQ):
         at = slice(head * HD, (head + 1) * HD)
         product = do_sc[at].astype(HIGH) * o_ref[at].astype(HIGH)
         delta[head : head + 1] = jnp.sum(product, axis=0, keepdims=True)
-    cosine = cos_ref[...]
-    sine = sin_ref[...]
 
     def group_body(group, carry):
         keys = k_sc[group]
@@ -423,23 +418,320 @@
     lax.fori_loop(0, KVH, group_body, 0)
 
 
-def close_kernel(parts, *refs):
+def attention_room(blocks, rows, width):
+    keys = blocks * rows
+    return [
+        pltpu.VMEM((keys, rows), HIGH),
+        pltpu.VMEM((KVH, keys, HD), LOW),
+        pltpu.VMEM((KVH, keys, HD), LOW),
+        pltpu.VMEM((KV_WIDTH, keys), LOW),
+        pltpu.VMEM((width, rows), LOW),
+        pltpu.VMEM((16, rows), HIGH),
+    ]
+
+
+def backward_last_kernel(*refs):
+    where_ref, e_ref, g_ref, u_ref, m_ref, gain_ref, wo_ref, q_ref, kv_ref = refs[:9]
+    o_ref, lse_ref, cos_ref, sin_ref = refs[9:13]
+    sources = refs[13:19]
+    f_ref, mine_ref, theirs_ref, c_ref, dm_ref, dq_ref, dkv_ref, gain_part_ref = refs[19:27]
+    room, (wg, wu, wd, sems) = refs[27:33], refs[33:]
+    rows = m_ref.shape[0]
+    copies = weights_in(sources, (wg, wu, wd), sems, (2, 0, 1))
+    row = where_ref[0] * rows + lax.broadcasted_iota(jnp.int32, (rows, 1), 0)
+    grad = jnp.where(row < where_ref[1], e_ref[...].astype(HIGH).T, 0.0)
+    outs = (f_ref, mine_ref, theirs_ref, c_ref, dm_ref, gain_part_ref)
+    grad_middle = ffn_back(grad, copies, g_ref, u_ref, m_ref, gain_ref, wg, wu, wd, outs)
+    attend_back(
+        where_ref, kv_ref, wo_ref, q_ref, o_ref, lse_ref, cos_ref[...], sin_ref[...], grad_middle, dq_ref, dkv_ref, room
+    )
+
+
+def ffn_back_kernel(*refs):
+    e_ref, g_ref, u_ref, m_ref, gain_ref = refs[:5]
+    sources, outs, (wg, wu, wd, sems) = refs[5:11], refs[11:17], refs[17:]
+    copies = weights_in(sources, (wg, wu, wd), sems, (2, 0, 1))
+    ffn_back(e_ref[...], copies, g_ref, u_ref, m_ref, gain_ref, wg, wu, wd, outs)
+
+
+def attend_back_kernel(*refs):
+    where_ref, dm_ref, wo_ref, q_ref, kv_ref, o_ref, lse_ref, cos_ref, sin_ref, dq_ref, dkv_ref = refs[:11]
+    attend_back(
+        where_ref, kv_ref, wo_ref, q_ref, o_ref, lse_ref, cos_ref[...], sin_ref[...], dm_ref[...], dq_ref, dkv_ref, refs[11:]
+    )
+
+
+def close_keys(total, cosine, sine, dkv_ref):
+    turned_keys = turned(total[:KV_WIDTH], cosine, sine, -1.0, 1.0)
+    dkv_ref[:KV_WIDTH] = turned_keys.astype(LOW)
+    dkv_ref[KV_WIDTH:] = total[KV_WIDTH:].astype(LOW)
+    return turned_keys.T.astype(LOW), total[KV_WIDTH:].T.astype(LOW)
+
+
+def close_rows(hidden, gain, dm_ref, dq_ref, grad_keys, grad_values, wq_ref, wk_ref, wv_ref):
+    grad_normed = nn(wq_ref[...], dq_ref[...]).T
+    grad_normed = grad_normed + nn(grad_keys, wk_ref[...]) + nn(grad_values, wv_ref[...])
+    return norm_back(hidden, gain, grad_normed, dm_ref[...])
+
+
+def close_kernel(last, *refs):
     h_ref, gain_ref, dm_ref, dq_ref, wq_ref, wk_ref, wv_ref, cos_ref, sin_ref = refs[:9]
-    part_refs = refs[9 : 9 + parts]
-    dh_ref, dkv_ref, gain_part_ref = refs[9 + parts :]
-    total = part_refs[0][...].astype(HIGH)
-    for part in part_refs[1:]:
-        total = total + part[...].astype(HIGH)
-    dkv_ref[:KV_WIDTH] = turned(total[:KV_WIDTH], cos_ref[...], sin_ref[...], -1.0, 1.0).astype(LOW)
-    dkv_ref[KV_WIDTH:] = total[KV_WIDTH:].astype(LOW)
-    grad_normed = nn(wq_ref[...], dq_ref[...])
-    grad_normed = grad_normed + nn(wk_ref[...], dkv_ref[:KV_WIDTH])
-    grad_normed = grad_normed + nn(wv_ref[...], dkv_ref[KV_WIDTH:])
-    gain_part, grad_in = norm_back(
-        h_ref[...].astype(HIGH), gain_ref[...].astype(HIGH), grad_normed.T, dm_ref[...]
+    own, near, far, dh_ref, dkv_ref, gain_part_ref = refs[9:]
+    total = own[...].astype(HIGH) + near[...].astype(HIGH) + far[...].astype(HIGH)
+    grad_keys, grad_values = close_keys(total, cos_ref[...], sin_ref[...], dkv_ref)
+    hidden = h_ref[...].astype(HIGH)
+    hidden = hidden if last else hidden.T
+    gain = gain_ref[...].astype(HIGH)
+    gain_part, grad_in = close_rows(hidden, gain, dm_ref, dq_ref, grad_keys, grad_values, wq_ref, wk_ref, wv_ref)
+    gain_part_ref[...] = gain_part
+    dh_ref[...] = grad_in if last else grad_in.T
+
+
+class Halving:
+    def __init__(self, links, steps):
+        self.steps = [(links.push(sent, got, to), kept, got) for sent, kept, got, to in steps]
+
+    def start(self, which):
+        self.steps[which][0].start()
+
+    def fold(self, which):
+        copy, kept, got = self.steps[which]
+        copy.wait_recv()
+        if which == len(self.steps) - 1:
+            return kept[...].astype(HIGH) + got[...].astype(HIGH)
+        total = kept[...].astype(HIGH) + got[...].astype(HIGH)
+        kept[...] = total.astype(kept.dtype)
+        self.steps[which + 1][0].start()
+        return None
+
+
+FAR_SIDE = ("dp", 4)
+
+
+def halved(links, whole, rooms, order):
+    where = {"X": 0, "Z1": 1, "Z0": 2, "Y": 3}
+    to = {"X": ACROSS, "Z1": FAR_SIDE, "Z0": BEYOND, "Y": SIDE}
+    chosen = [slice(None)] * 4
+    steps = []
+    for axis, room in zip(order, rooms):
+        sent, kept = list(chosen), list(chosen)
+        sent[where[axis]], kept[where[axis]] = 1, 0
+        steps.append((whole.at[tuple(sent)], whole.at[tuple(kept)], room, to[axis]))
+        chosen = kept
+    return Halving(links, steps)
+
+
+def halving_rooms(block, columns, order):
+    left = [2, 2, 2, 2]
+    where = {"X": 0, "Z1": 1, "Z0": 2, "Y": 3}
+    rooms = []
+    for axis in order:
+        left[where[axis]] = 0
+        rooms.append(pltpu.VMEM(tuple(n for n in left if n) + (block, columns), LOW))
+    return rooms
+
+
+ORDERS = (("X", "Y", "Z0", "Z1"), ("Y", "Z0", "X", "Z1"), ("Z0", "X", "Y", "Z1"))
+ATTN_ORDERS = (("X", "Y", "Z0", "Z1"), ("Y", "X", "Z0", "Z1"))
+ATTN_CUTS = (256, 384)
+COPIES_FINISH = 3 * 4 + 2 * 4 + 4 + 5 + 3 + 4
+
+
+def finish_kernel(layers, *refs):
+    where_ref, h_ref, gain_ref, dm_ref, wo_ref, q_ref, kv_ref, o_ref, lse_ref = refs[:9]
+    wq_ref, wk_ref, wv_ref, cos_ref, sin_ref, a_ref, c_ref = refs[9:16]
+    left_two, long_two, short_two, side_two = refs[16:20]
+    gains_ref = refs[20]
+    count = 4
+    b_any, f_any, rhs_any = refs[21:25], refs[25:29], refs[29:33]
+    dh_ref, gate_out, up_out, down_out = refs[33:37]
+    query_out, key_out, value_out, output_out, gain_out = refs[37:42]
+    room = refs[42:48]
+    dq_ref, dkv_ref, dkv_near, dkv_sum, dkv_far, dkv_low = refs[48:54]
+    b_all, f_all, rhs, left_all, long_all, short_all, side_all = refs[54:61]
+    wholes, rooms = refs[61:64], (refs[64:68], refs[68:72], refs[72:76])
+    attn_wholes, attn_rooms = refs[76:78], (refs[78:82], refs[82:86])
+    attn_alls = refs[86:88]
+    gain_whole, gain_got, gain_side = refs[88:91]
+    load, send, receive = refs[91:]
+    rows = h_ref.shape[1]
+    block = gate_out.shape[0]
+    place = lax.axis_index("dp")
+    head_at = lax.axis_index("head")
+    core, across = head_at % 2, head_at // 2
+    links = Links(send, receive)
+    reduces = [halved(links, whole, got, order) for whole, got, order in zip(wholes, rooms, ORDERS)]
+    attn = [halved(links, whole, got, order) for whole, got, order in zip(attn_wholes, attn_rooms, ATTN_ORDERS)]
+
+    loads = []
+
+    def load_in(source, target):
+        copy = pltpu.make_async_copy(source, target, load.at[len(loads)])
+        loads.append(copy)
+        copy.start()
+        return copy
+
+    columns = [pl.ds(i * rows, rows) for i in range(count)]
+    wanted = (1, 2, 3, 4, 5, 0)
+
+    def fetch(turn):
+        return [load_in(rhs_any[i].at[wanted[turn]], rhs.at[turn % 2, columns[i]]) for i in range(count)]
+
+    b_loads = [load_in(b_any[i], b_all.at[:, columns[i]]) for i in range(count)]
+    coming = fetch(0)
+    f_loads = [load_in(f_any[i], f_all.at[:, columns[i]]) for i in range(count)]
+    two = ((left_two, left_all), (long_two, long_all), (short_two, short_all), (side_two, side_all))
+    two_loads = [load_in(source, target.at[:, pl.ds(0, 2 * rows)]) for source, target in two]
+    greet((SIBLING, ACROSS, SIDE, BEYOND, FAR_SIDE))
+    for copy in b_loads:
+        copy.wait()
+
+    def lay(product, whole, first):
+        for index in range(8):
+            relative = jnp.bitwise_xor(index, place)
+            whole[first, relative // 4, relative // 2 % 2, relative % 2] = product[
+                index * block : (index + 1) * block
+            ].astype(LOW)
+
+    for turn, which in enumerate(wanted):
+        for copy in coming:
+            copy.wait()
+        if turn < 5:
+            coming = fetch(turn + 1)
+        if which == 4:
+            for copy in f_loads:
+                copy.wait()
+        lay(nn((b_all if which < 4 else f_all)[...], rhs[turn % 2]), wholes[which // 2], which % 2)
+        if which == 1:
+            reduces[0].start(0)
+        if which == 3:
+            reduces[1].start(0)
+        if which == 5:
+            reduces[2].start(0)
+
+    cosine, sine = cos_ref[...], sin_ref[...]
+    attend_back(where_ref, kv_ref, wo_ref, q_ref, o_ref, lse_ref, cosine, sine, dm_ref[...], dq_ref, dkv_ref, room)
+    near = [links.push(dkv_ref.at[3], dkv_near.at[1], SIBLING), links.push(dkv_ref.at[1], dkv_near.at[0], SIBLING)]
+    far = links.push(dkv_sum, dkv_far, ACROSS)
+    for copy in near:
+        copy.start()
+    near[0].wait_recv()
+    dkv_sum[...] = (dkv_ref[2].astype(HIGH) + dkv_near[1].astype(HIGH)).astype(LOW)
+    far.start()
+    for reduce in reduces:
+        reduce.fold(0)
+    near[1].wait_recv()
+    far.wait_recv()
+    total = dkv_ref[0].astype(HIGH) + dkv_near[0].astype(HIGH) + dkv_far[...].astype(HIGH)
+    grad_keys, grad_values = close_keys(total, cosine, sine, dkv_low)
+
+    low_rows, own_at, got_at = pl.ds(0, KV_WIDTH), pl.ds(2 * rows, rows), pl.ds(3 * rows, rows)
+    high_rows = pl.ds(KV_WIDTH, KV_WIDTH)
+    pairs = (
+        (a_ref, c_ref, left_all),
+        (dq_ref, o_ref, long_all),
+        (dkv_low.at[low_rows], dkv_low.at[high_rows], short_all),
+        (a_ref, a_ref, side_all),
     )
-    gain_part_ref[...] = gain_part
-    dh_ref[...] = grad_in
+    swaps, first_used = [], links.used
+    for index, (zero, one, target) in enumerate(pairs):
+        keep_zero = load_in(zero, target.at[:, own_at]) if zero is one else None
+        if keep_zero is None:
+            keep_zero = pltpu.make_async_copy(zero, target.at[:, own_at], load.at[len(loads)])
+            keep_one = pltpu.make_async_copy(one, target.at[:, own_at], load.at[len(loads)])
+            loads.append(keep_zero)
+            pl.when(core == 0)(keep_zero.start)
+            pl.when(core == 1)(keep_one.start)
+        send_one = links.push(one, target.at[:, got_at], SIBLING)
+        if zero is one:
+            send_one.start()
+        else:
+            links.used -= 1
+            links.flying.pop()
+            send_zero = links.push(zero, target.at[:, got_at], SIBLING)
+            pl.when(core == 0)(send_one.start)
+            pl.when(core == 1)(send_zero.start)
+        swaps.append((keep_zero, send_one))
+    hidden = h_ref[...].astype(HIGH).T
+    gain = gain_ref[...].astype(HIGH)
+    gain_part, grad_in = close_rows(hidden, gain, dm_ref, dq_ref, grad_keys, grad_values, wq_ref, wk_ref, wv_ref)
+    dh_ref[...] = grad_in.T
+    for copy in two_loads:
+        copy.wait()
+    for keep, swap_copy in swaps:
+        keep.wait()
+        swap_copy.wait_recv()
+    long_part = nt(left_all[...], long_all[...])
+    short_part = nt(side_all[...], short_all[...])
+    product = jnp.concatenate([long_part, short_part], axis=1)
+    start = 0
+    for whole, cut in zip(attn_wholes, ATTN_CUTS):
+        for half in range(2):
+            lay(product[:, start : start + cut], whole, jnp.bitwise_xor(half, across))
+            start += cut
+    for reduce in attn:
+        reduce.start(0)
+
+    summed = gains_ref[...] + jnp.concatenate([gain_part, jnp.zeros((7, gain_part.shape[1]), HIGH)], axis=0)
+    for index in range(8):
+        relative = jnp.bitwise_xor(index, place)
+        gain_whole[relative // 4, relative // 2 % 2, relative % 2, :, :block] = summed[
+            :, index * block : (index + 1) * block
+        ]
+        gain_whole[relative // 4, relative // 2 % 2, relative % 2, :, block:] = jnp.zeros((8, 128 - block), HIGH)
+    gain_y = links.push(gain_whole.at[:, :, 1], gain_side, SIDE)
+    gain_y.start()
+    for reduce in reduces:
+        reduce.fold(1)
+    gain_y.wait_recv()
+    gain_whole[:, :, 0] = gain_whole[:, :, 0] + gain_side[...]
+    gain_z = links.push(gain_whole.at[:, 1, 0], gain_got.at[pl.ds(0, 2)], BEYOND)
+    gain_z.start()
+    attn[0].fold(0)
+    gain_z.wait_recv()
+    gain_whole[:, 0, 0] = gain_whole[:, 0, 0] + gain_got[0:2]
+    gain_f = links.push(gain_whole.at[1, 0, 0], gain_got.at[2], FAR_SIDE)
+    gain_f.start()
+    attn[1].fold(0)
+    for reduce in reduces:
+        reduce.fold(2)
+    gain_f.wait_recv()
+    gain_whole[0, 0, 0] = gain_whole[0, 0, 0] + gain_got[2]
+    gain_x = links.push(gain_whole.at[0, 0, 0], gain_got.at[3], ACROSS)
+    gain_x.start()
+    attn[0].fold(1)
+    attn[1].fold(1)
+    gain_x.wait_recv()
+    gain_got[4] = gain_whole[0, 0, 0] + gain_got[3]
+    gain_c = links.push(gain_got.at[4], gain_got.at[5], SIBLING)
+    gain_c.start()
+    attn[0].fold(2)
+    attn[1].fold(2)
+    gain_c.wait_recv()
+    gain_out[...] = gain_got[4] + gain_got[5]
+    for reduce, out in zip(reduces, (gate_out, up_out, down_out)):
+        out[...] = reduce.fold(3)
+    shared = []
+    for reduce, held in zip(attn, attn_alls):
+        held[0, 0] = reduce.fold(3).astype(LOW)
+        copy = links.push(held.at[0, 0], held.at[0, 1], ACROSS)
+        copy.start()
+        shared.append((copy, held))
+    last = []
+    for copy, held in shared:
+        copy.wait_recv()
+        copy = links.push(held.at[0], held.at[1], SIBLING)
+        copy.start()
+        last.append(copy)
+    for copy in last:
+        copy.wait_recv()
+    for kind, (long_out, short_out) in enumerate(((query_out, key_out), (output_out, value_out))):
+        from_core = jnp.bitwise_xor(kind, core)
+        parts = [held[from_core, jnp.bitwise_xor(half, across)] for held in attn_alls for half in range(2)]
+        both = jnp.concatenate([part.astype(HIGH) for part in parts], axis=1)
+        long_out[...] = both[:, : long_out.shape[1]]
+        short_out[...] = both[:, long_out.shape[1] :]
+    links.drain()
 
 
 def call(body, outs, specs, scratch, name, spots=0, collective=None):
@@ -510,8 +802,8 @@
 
     feature_rows = (width, rows)
     project_outs = [(feature_rows, LOW), (feature_rows, LOW), ((blocks, rows, 2 * KV_WIDTH), LOW)]
-    weight_shapes = [(width, hidden), (width, hidden), (hidden, width)]
-    weight_room = [pltpu.VMEM((blocks,) + shape, LOW) for shape in weight_shapes]
+    tokens, cotangent, w_key, w_value, w_down = (v.T for v in (tokens, cotangent, w_key, w_value, w_down))
+    weight_room = [pltpu.VMEM((blocks, width, hidden), LOW)] * 3
     attend_room = [
         pltpu.VMEM((keys, rows), HIGH),
         pltpu.VMEM((KVH, keys, HD), LOW),
@@ -528,7 +820,7 @@
 
     def forward_first():
         outs = project_outs + layer_outs + [((rows, width), HIGH)] + project_outs
-        outs += [((blocks - 1,) + shape, LOW) for shape in weight_shapes]
+        outs += [((blocks - 1, width, hidden), LOW)] * 3
         copies = 3 * COPIES_SPREAD + 2 * COPIES_SHARE
         scratch = attend_room + weight_room
         scratch += [pltpu.SemaphoreType.DMA((3,)), pltpu.SemaphoreType.DMA((3, blocks - 1))]
@@ -547,106 +839,128 @@
     def forward_last():
         specs = [SMEM] + [VMEM] * 5 + [ANY] * 6
         body = functools.partial(forward_last_kernel, blocks)
-        outs = layer_outs + [((rows, width), LOW)]
+        outs = layer_outs + [(feature_rows, LOW)]
         return call(body, outs, specs, attend_room + weight_scratch, "forward_last")(
             where, h_one, q_two, kv_two, w_output, gain_two, *weights
         )
 
-    def backward(e, kept, first):
-        queries, kv, attended, log_totals, middle, gate, up = kept
-        outs = [
-            (feature_rows, LOW),
-            ((6, rows, hidden), LOW),
-            ((6, rows, hidden), LOW),
-            (feature_rows, LOW),
-            ((rows, width), HIGH),
-            (feature_rows, LOW),
-            ((blocks, 2 * KV_WIDTH, rows), LOW),
-            ((1, width), HIGH),
-        ]
+    o_two, lse_two, m_two, b_two, g_two, u_two, block_out = forward_last()
+    ffn_outs = [
+        (feature_rows, LOW),
+        ((6, rows, hidden), LOW),
+        ((6, rows, hidden), LOW),
+        (feature_rows, LOW),
+        ((rows, width), HIGH),
+    ]
+    attend_outs = [(feature_rows, LOW), ((blocks, 2 * KV_WIDTH, rows), LOW)]
+    gain_outs = [((1, width), HIGH)]
+    room = attention_room(blocks, rows, width)
+
+    def backward_last():
+        given = [where, cotangent, g_two, u_two, m_two, gain_two, w_output, q_two, kv_two, o_two, lse_two]
         specs = [SMEM] + [VMEM] * 12 + [ANY] * 6
-        given = [where, e, gate, up, middle, gain_two, w_output, queries, kv, attended, log_totals]
-        given += [cosine, sine, *weights]
-        scratch = [
-            pltpu.VMEM((keys, rows), HIGH),
-            pltpu.VMEM((KVH, keys, HD), LOW),
-            pltpu.VMEM((KVH, keys, HD), LOW),
-            pltpu.VMEM((KV_WIDTH, keys), LOW),
-            pltpu.VMEM(feature_rows, LOW),
-            pltpu.VMEM((16, rows), HIGH),
-        ] + weight_scratch
-        body = functools.partial(backward_kernel, first, blocks)
-        return call(body, outs, specs, scratch, "backward_last" if first else "backward_first")(*given)
-
-    def close(h, grad_middle, grad_query, partial):
+        return call(
+            backward_last_kernel, ffn_outs + attend_outs + gain_outs, specs, room + weight_scratch, "backward_last"
+        )(*given, cosine, sine, *weights)
+
+    def close(h, grad_middle, grad_query, partial, last):
         sent = swap(jnp.stack([partial[1], partial[3]]), 1)
-        near = sent[0]
         far = swap((partial[2].astype(HIGH) + sent[1].astype(HIGH)).astype(LOW), 2)
-        outs = [((rows, width), HIGH), ((2 * KV_WIDTH, rows), LOW), ((1, width), HIGH)]
+        outs = [((rows, width) if last else feature_rows, HIGH), ((2 * KV_WIDTH, rows), LOW), ((1, width), HIGH)]
         given = [h, gain_one, grad_middle, grad_query, w_query, w_key, w_value, cosine, sine]
-        given += [partial[0], near, far]
-        return call(functools.partial(close_kernel, 3), outs, [VMEM] * 12, [], "close")(*given)
-
-    o_two, lse_two, m_two, b_two, g_two, u_two, block_out = forward_last()
-    f_two, mine_two, theirs_two, c_two, dm_two, dq_two, part_two, gain_two_b = backward(
-        cotangent, (q_two, kv_two, o_two, lse_two, m_two, g_two, u_two), True
-    )
-    e_one, dkv_two, gain_one_b = close(h_one, dm_two, dq_two, part_two)
-    f_one, mine_one, theirs_one, c_one, dm_one, dq_one, part_one, gain_two_a = backward(
-        e_one, (q_one, kv_one, o_one, lse_one, m_one, g_one, u_one), False
-    )
-    input_grad, dkv_one, gain_one_a = close(tokens, dm_one, dq_one, part_one)
+        given += [partial[0], sent[0], far]
+        return call(functools.partial(close_kernel, last), outs, [VMEM] * 12, [], "close")(*given)
+
+    f_two, mine_two, theirs_two, c_two, dm_two, dq_two, part_two, gain_two_b = backward_last()
+    e_one, dkv_two, gain_one_b = close(h_one, dm_two, dq_two, part_two, True)
+    f_one, mine_one, theirs_one, c_one, dm_one, gain_two_a = call(
+        ffn_back_kernel, ffn_outs + gain_outs, [VMEM] * 5 + [ANY] * 6, weight_scratch, "ffn_back"
+    )(e_one, g_one, u_one, m_one, gain_two, *weights)
 
     def beside(parts):
         return jnp.concatenate(parts, axis=-1)
 
-    from_two, from_one = swap(theirs_two, 1), swap(theirs_one, 1)
-    b_all = beside([b_two, swap(b_two, 1), b_one, swap(b_one, 1)])
-    f_all = beside([f_two, swap(f_two, 1), f_one, swap(f_one, 1)])
-
-    def hidden_rows(which):
-        return jnp.concatenate([mine_two[which], from_two[which], mine_one[which], from_one[which]], 0)
-
-    kept, sent = [], []
-    for which in range(6):
-        product = nn(b_all if which < 4 else f_all, hidden_rows(which)).astype(LOW)
-        (sent if which % 2 else kept).append(product)
-    got = swap(beside(sent), 2)
-    ffn = scatter_rows((beside(kept).astype(HIGH) + got.astype(HIGH)).astype(LOW), "dp")
-
     def choose(zero, one):
         return jnp.where(low_bit == 0, zero, one)
 
-    lefts, longs, shorts, sides = [], [], [], []
-    for a, c, o, dq, dkv in (
-        (a_two, c_two, o_two, dq_two, dkv_two),
-        (a_one, c_one, o_one, dq_one, dkv_one),
-    ):
+    def halves(a, c, o, dq, dkv):
         dk, dv = dkv[:KV_WIDTH], dkv[KV_WIDTH:]
-        lefts += [choose(a, c), swap(choose(c, a), 1)]
-        longs += [choose(dq, o), swap(choose(o, dq), 1)]
-        shorts += [choose(dk, dv), swap(choose(dv, dk), 1)]
-        sides += [a, swap(a, 1)]
-    long_part = nt(beside(lefts), beside(longs)).astype(LOW)
-    short_part = nt(beside(sides), beside(shorts)).astype(LOW)
-    attn = scatter_rows(beside([long_part, short_part]), "dp").astype(LOW)
-    attn = (attn.astype(HIGH) + swap(attn, 2).astype(HIGH)).astype(LOW)
-    other = swap(attn, 1)
-    zero, one = choose(attn, other).astype(HIGH), choose(other, attn).astype(HIGH)
-    gains = jnp.concatenate([gain_one_a + gain_one_b, gain_two_a + gain_two_b], axis=0)
-    gains = lax.psum_scatter(lax.psum(gains, "head"), "dp", scatter_dimension=1, tiled=True)
+        left = [choose(a, c), swap(choose(c, a), 1)]
+        long = [choose(dq, o), swap(choose(o, dq), 1)]
+        short = [choose(dk, dv), swap(choose(dv, dk), 1)]
+        return beside(left), beside(long), beside(short), beside([a, swap(a, 1)])
+
+    halves_two = halves(a_two, c_two, o_two, dq_two, dkv_two)
+    b_all = [b_two, swap(b_two, 1), b_one, swap(b_one, 1)]
+    f_all = [f_two, swap(f_two, 1), f_one, swap(f_one, 1)]
+    sides = [mine_two, swap(theirs_two, 1), mine_one, swap(theirs_one, 1)]
+    places = lax.axis_size("dp")
+    block = width // places
+
+    def finish():
+        gains = jnp.concatenate([gain_one_b, gain_two_a + gain_two_b, jnp.zeros((6, width), HIGH)], axis=0)
+        outs = [(feature_rows, HIGH)] + [((block, hidden), HIGH)] * 3
+        outs += [((block, n), HIGH) for n in (HQ * HD, KV_WIDTH, KV_WIDTH, HQ * HD)] + [((8, 128), HIGH)]
+        low_room = [feature_rows, (blocks, 2 * KV_WIDTH, rows), (2, 2 * KV_WIDTH, rows)]
+        low_room += [(2 * KV_WIDTH, rows)] * 3
+        low_room += [(width, 4 * rows), (width, 4 * rows), (2, 4 * rows, hidden)]
+        low_room += [(width, 4 * rows), (width, 4 * rows), (KV_WIDTH, 4 * rows), (width, 4 * rows)]
+        low_room += [(2, 2, 2, 2, block, hidden)] * 3
+        scratch = room + [pltpu.VMEM(shape, LOW) for shape in low_room]
+        for order in ORDERS:
+            scratch += halving_rooms(block, hidden, order)
+        scratch += [pltpu.VMEM((2, 2, 2, 2, block, cut), LOW) for cut in ATTN_CUTS]
+        for order, cut in zip(ATTN_ORDERS, ATTN_CUTS):
+            scratch += halving_rooms(block, cut, order)
+        scratch += [pltpu.VMEM((2, 2, block, cut), LOW) for cut in ATTN_CUTS]
+        scratch += [pltpu.VMEM(shape, HIGH) for shape in ((2, 2, 2, 8, 128), (8, 8, 128), (2, 2, 8, 128))]
+        scratch += [pltpu.SemaphoreType.DMA((40,)), pltpu.SemaphoreType.DMA((COPIES_FINISH,))]
+        scratch += [pltpu.SemaphoreType.DMA((COPIES_FINISH,))]
+        given = [where, tokens, gain_one, dm_one, w_output, q_one, kv_one, o_one, lse_one]
+        given += [w_query, w_key, w_value, cosine, sine, a_one, c_one, *halves_two, gains]
+        specs = [SMEM] + [VMEM] * 15 + [ANY] * 4 + [VMEM] + [ANY] * 12
+        return call(functools.partial(finish_kernel, 2), outs, specs, scratch, "finish", 0, 2)(
+            *given, *b_all, *f_all, *sides
+        )
+
+    if places == 8 and blocks == 4:
+        outs = finish()
+        input_grad, gate_grad, up_grad, down_grad, query_grad, key_grad, value_grad, output_grad, gains = outs
+        gains = gains[:2, :block]
+    else:
+        given = [where, dm_one, w_output, q_one, kv_one, o_one, lse_one, cosine, sine]
+        dq_one, part_one = call(attend_back_kernel, attend_outs, [SMEM] + [VMEM] * 8, room, "attend_back")(*given)
+        input_grad, dkv_one, gain_one_a = close(tokens, dm_one, dq_one, part_one, False)
+        kept, sent = [], []
+        for which in range(6):
+            side = jnp.concatenate([each[which] for each in sides], 0)
+            product = nn(beside(b_all if which < 4 else f_all), side).astype(LOW)
+            (sent if which % 2 else kept).append(product)
+        got = swap(beside(sent), 2)
+        ffn = scatter_rows((beside(kept).astype(HIGH) + got.astype(HIGH)).astype(LOW), "dp")
+        halves_one = halves(a_one, c_one, o_one, dq_one, dkv_one)
+        left, long, short, side = (beside(pair) for pair in zip(halves_two, halves_one))
+        attn = scatter_rows(beside([nt(left, long), nt(side, short)]).astype(LOW), "dp").astype(LOW)
+        attn = (attn.astype(HIGH) + swap(attn, 2).astype(HIGH)).astype(LOW)
+        other = swap(attn, 1)
+        zero, one = choose(attn, other).astype(HIGH), choose(other, attn).astype(HIGH)
+        gains = jnp.concatenate([gain_one_a + gain_one_b, gain_two_a + gain_two_b], axis=0)
+        gains = lax.psum_scatter(lax.psum(gains, "head"), "dp", scatter_dimension=1, tiled=True)
+        query_grad, key_grad = zero[:, : HQ * HD], zero[:, HQ * HD :]
+        output_grad, value_grad = one[:, : HQ * HD], one[:, HQ * HD :]
+        gate_grad, up_grad, down_grad = (ffn[:, i * hidden : (i + 1) * hidden] for i in range(3))
     return (
-        block_out,
-        input_grad,
+        block_out.T,
+        input_grad.T,
         gains[0],
-        zero[:, : HQ * HD],
-        zero[:, HQ * HD :],
-        one[:, HQ * HD :],
-        one[:, : HQ * HD].T,
+        query_grad,
+        key_grad,
+        value_grad,
+        output_grad.T,
         gains[1],
-        ffn[:, :hidden],
-        ffn[:, hidden : 2 * hidden],
-        ffn[:, 2 * hidden :].T,
+        gate_grad,
+        up_grad,
+        down_grad.T,
     )
 
 

time: 416 us -> 310 us (0.75)
  Pallas kernels: 168 us -> 258 us
  waiting for transfers between devices: 93.5 us -> 12.9 us
  blocking collectives: 54.4 us -> 0 us
  local copies, waits for them, and re-layouts: 45.6 us -> 19.4 us
  matrix products: 14.7 us -> 0 us
  other arithmetic: 18.8 us -> 7.28 us
  starting transfers between devices: 12 us -> 4.44 us
    pallas_call x4, Pallas kernels: 68.5 us -> 160 us  [the longest x1 113 us: finish(): call(functools.partial(finish_kernel, 2), outs, specs, scratch, 'finish',...]
    ppermute x21 -> x12, waiting for transfers between devices: 65.2 us -> 12.9 us  [swap(): lax.ppermute(value, 'head', [(i, i ^ distance) for i in range(count)])]
    unnamed x1 -> x0, blocking collectives: 45.7 us -> none
    ppermute x6 -> x0, waiting for transfers between devices: 28.3 us -> none  [scatter_rows(): got = lax.ppermute(sent, axis, [(i, i ^ bit) for i in range(count)])]
    dot_general x8 -> x0, matrix products: 14.7 us -> none  [the longest x6 10.2 us: nn(): lax.dot_general(left, right, (((1,), (0,)), ((), ())), preferred_element_...]
    unnamed x120 -> x54, local copies, waits for them, and re-layouts: 27.4 us -> 12.8 us
    squeeze x12 -> x1, local copies, waits for them, and re-layouts: 9.69 us -> 0.74 us  [close(): given += [partial[0], sent[0], far]]
    psum x1 -> x0, blocking collectives: 8.66 us -> none  [shards(): lax.psum(gains, 'head')]
  transfers between devices with their start and end apart: 27 -> 12, of which waited for: 6 -> 4; matrix products, arithmetic and copies ran while one was open for 15% -> 2% of each run, Pallas kernels for 10% -> 6%
where the time goes in v3:
time: 310 us; the launch traced here: 304 us
  Pallas kernels  258 us (83%)
  local copies, waits for them, and re-layouts  19.4 us (6%)
  waiting for transfers between devices  12.9 us (4%)
  other arithmetic  7.28 us (2%)
  starting transfers between devices  4.44 us (1%)
    pallas_call x1, Pallas kernels, finish(): call(functools.partial(finish_kernel, 2), outs, specs, scratch, 'finish',...  113 us
    pallas_call x1, Pallas kernels, forward_first(): call(body, outs, specs, scratch, 'forward_first', 3, 1)  78 us
    pallas_call x1, Pallas kernels, backward_last(): call(backward_last_kernel, ffn_outs + attend_outs + gain_outs, specs, roo...  27.9 us
    pallas_call x1, Pallas kernels, forward_last(): call(body, outs, specs, attend_room + weight_scratch, 'forward_last')  20.8 us
    pallas_call x1, Pallas kernels, shards(): call(ffn_back_kernel, ffn_outs + gain_outs, [VMEM] * 5 + [ANY] * 6, weigh...  13.1 us
    ppermute x12, waiting for transfers between devices, swap(): lax.ppermute(value, 'head', [(i, i ^ distance) for i in range(count)])  12.9 us
    unnamed x54, local copies, waits for them, and re-layouts  12.8 us
  transfers between devices with their start and end apart: 12, of which 4 were waited for; matrix products, arithmetic and copies ran while one was open for 2% of the time, Pallas kernels for 6%

profile of v3, /device:TPU:0, one launch (start us, length us, event | category | flops | bytes accessed | tf_op | source)
XLA Modules:
  0.0 304.2 jit_solution(7280332359768703830)
XLA Ops:
  1.3 1.3 broadcast_in_dim.12.refs_9_.refs_5_.refs_4_
  2.6 1.3 broadcast_in_dim.11.refs_2_.refs_1_
  3.9 0.8 multiply_sine_fusion
  4.7 0.6 pad_add_fusion.refs_0_
  5.3 78.0 %forward_first.1 = (bf16[960,256]{1,0:T(8,128)(2,1)}, bf16[960,256]{1,0:T(8,128)(2,1)}, bf16[4,256,640]{2,1,0:T(8,128)(2,1)}, bf16[960,256]{1,0:T(8,128)(2,1)}, ...) custom-call(s32[2]{0:T(128)} %pad_add_fusion.refs_0_, ...), custom_call_target="tpu_custom_call" | custom-call | tf_op jit(solution)/shard_map/forward_first/pallas_call | solution.py:830
  83.3 20.8 %forward_last.1 = (bf16[960,256]{1,0:T(8,128)(2,1)}, f32[16,256]{1,0:T(8,128)}, f32[256,960]{1,0:T(8,128)}, bf16[960,256]{1,0:T(8,128)(2,1)}, bf16[4,256,640]{2,...) custom-call(s32[2]{0:T(128)} %pad_add_fusion.refs_0_, ...), custom_call_target="tpu_custom_call" | custom-call | tf_op jit(solution)/shard_map/forward_last/pallas_call | solution.py:843
  104.1 27.9 %backward_last.1 = (bf16[960,256]{1,0:T(8,128)(2,1)}, bf16[6,256,640]{2,1,0:T(8,128)(2,1)}, bf16[6,256,640]{2,1,0:T(8,128)(2,1)}, bf16[960,256]{1,0:T(8,128)(2,1...) custom-call(s32[2]{0:T(128)} %pad_add_fusion.refs_0_, ...), custom_call_target="tpu_custom_call" | custom-call | tf_op jit(solution)/shard_map/backward_last/pallas_call | solution.py:862
  132.0 2.0 fusion.1
  134.0 0.5 collective-permute-start
  134.5 1.7 collective-permute-done
  136.3 1.1 fusion
  137.3 1.6 collective-permute-start.1
  138.9 0.1 collective-permute-start.10
  139.0 0.7 slice_bitcast_fusion.refs_10_
  139.7 7.7 %collective-permute-done.1.refs_11_ = bf16[640,256]{1,0:T(8,128)(2,1)S(1)} collective-permute-done((bf16[640,256]{1,0:T(8,128)(2,1)S(1)}, bf16[640,256]{1,0:T(8,128)(2,1)S(1)}, u32[]{:S(2)}, u32[]{:S(2)}) %collective-permute-start.1) | collective-permute-done | bytes 327712 | tf_op jit(solution)/shard_map/ppermute | solution.py:754
  147.4 0.7 copy-done.15
  148.1 5.5 %close.1 = (f32[256,960]{1,0:T(8,128)}, bf16[640,256]{1,0:T(8,128)(2,1)}, f32[1,960]{1,0:T(1,128)}) custom-call(f32[256,960]{1,0:T(8,128)} %get-tuple-element.60.refs_1_.refs_0_, bf16[1,960]{1,0:T(2,128)(2,1)} %broadcast_in_dim.11.refs_2_.refs_1_, f32[256,960]{1,0:T(8,128)} %get-tuple-element.72.refs_2_, bf16[960,256]{1,0:T(8,128)(2,1)} %get-tuple-element.73.refs_3_, ...), custom_call_target="tpu_custom_call" | custom-call | tf_op jit(solution)/shard_map/close/pallas_call | solution.py:872
  153.7 13.1 %ffn_back.1 = (bf16[960,256]{1,0:T(8,128)(2,1)}, bf16[6,256,640]{2,1,0:T(8,128)(2,1)}, bf16[6,256,640]{2,1,0:T(8,128)(2,1)}, bf16[960,256]{1,0:T(8,128)(2,1)}, f32[256,960]{1,0:T(8,128)}, /*index=5*/f32[1,960]{1,0:T(1,128)}) custom-call(f32[256,960]{1,0:T(8,128)} %get-tuple-element.75.refs_0_, bf16[4,256,640]{2,1,0:T(8,128)(2,1)} %get-tuple-element.76.refs_1_, ...), custom_call_target="tpu_custom_call" | custom-call | tf_op jit(solution)/shard_map/ffn_back/pallas_call | solution.py:876
  167.0 0.5 collective-permute-start.3
  167.5 0.3 copy-done.2
  167.8 0.2 copy-done.9
  168.1 0.5 collective-permute-start.2
  168.5 3.0 collective-permute-done.3
  171.5 0.1 collective-permute-start.8
  171.7 0.5 collective-permute-done.5
  172.2 0.1 collective-permute-start.4
  172.4 0.1 pad.2.clone
  172.4 1.0 pad_maximum_fusion.2.refs_19_
  173.5 0.4 collective-permute-start.6
  173.9 0.2 collective-permute-start.7
  174.1 0.4 collective-permute-start.9
  174.5 1.0 pad_maximum_fusion.1.refs_17_
  175.5 1.0 pad_maximum_fusion.refs_16_
  176.5 0.7 maximum_maximum_fusion.refs_20_
  177.2 0.8 pad_maximum_fusion.4.refs_18_
  178.1 0.8 copy-done.12
  178.8 0.3 copy-done.13
  179.1 1.0 copy-done.3
  180.1 113.1 %finish.1 = (f32[960,256]{1,0:T(8,128)}, f32[120,640]{1,0:T(8,128)}, f32[120,640]{1,0:T(8,128)}, f32[120,640]{1,0:T(8,128)}, f32[120,960]{1,0:T(8,128)}, /*index...) custom-call(s32[2]{0:T(128)} %pad_add_fusion.refs_0_, bf16[960,256]{1,0:T(8,128)(2,1)} %bitcast.31, ...), custom_call_target="tpu_custom_call" | custom-call | tf_op jit(solution)/shard_map/finish/pallas_call | solution.py:922
  293.3 2.1 copy.25
  295.4 1.8 copy.23
  297.1 1.8 copy.24
  298.9 1.3 slice_bitcast_fusion.2
  300.1 0.9 copy.32
  301.1 0.8 copy.33
  301.9 0.7 copy.34
  302.6 0.7 copy.35
  303.3 0.7 copy.36
  (58 shorter events, 0.4 us)
Async XLA Ops:
  134.0 2.2 collective-permute-start
  137.3 10.1 %collective-permute-start.1 = (bf16[640,256]{1,0:T(8,128)(2,1)S(1)}, bf16[640,256]{1,0:T(8,128)(2,1)S(1)}, u32[]{:S(2)}, u32[]{:S(2)}) collective-permute-start(bf16[640,256]{1,0:T(8,128)(2,1)S(1)} %fusion), channel_id=1, source_target_pairs={{0,2},{1,3},{2,0},{3,1},{4,6},{5,7},{6,4},{7,5},{8,10},{9,11},{10,... | collective-permute-start | bytes 983048 | tf_op jit(solution)/shard_map/ppermute | solution.py:754
  138.9 39.2 %collective-permute-start.10 = (bf16[6,256,640]{2,1,0:T(8,128)(2,1)}, bf16[6,256,640]{2,1,0:T(8,128)(2,1)S(1)}, u32[]{:S(2)}, u32[]{:S(2)}) collective-permute-start(bf16[6,256,640]{2,1,0:T(8,128)(2,1)} %get-tuple-element.97), channel_id=1, source_target_pairs={{0,1},{1,0},{2,3},{3,2},{4,5},{5,4},{6,7},{7,6},{8,9},{9,8},{10,11... | collective-permute-start | bytes 5898248 | tf_op jit(solution)/shard_map/ppermute | solution.py:754
  147.4 0.7 copy-start.15
  153.7 13.2 %copy-start = (bf16[960,256]{1,0:T(8,128)(2,1)S(1)}, bf16[960,256]{1,0:T(8,128)(2,1)}, u32[]{:S(2)}) copy-start(bf16[960,256]{1,0:T(8,128)(2,1)} %get-tuple-element.70.refs_9_) | copy-start | bytes 1474564
  153.7 13.2 %copy-start.1 = (bf16[960,256]{1,0:T(8,128)(2,1)S(1)}, bf16[960,256]{1,0:T(8,128)(2,1)}, u32[]{:S(2)}) copy-start(bf16[960,256]{1,0:T(8,128)(2,1)} %get-tuple-element.73.refs_3_) | copy-start | bytes 1474564
  166.8 1.0 copy-start.2
  166.8 12.1 %collective-permute-start.11 = (bf16[6,256,640]{2,1,0:T(8,128)(2,1)}, bf16[6,256,640]{2,1,0:T(8,128)(2,1)}, u32[]{:S(2)}, u32[]{:S(2)}) collective-permute-start(bf16[6,256,640]{2,1,0:T(8,128)(2,1)} %get-tuple-element.99), channel_id=1, source_target_pairs={{0,1},{1,0},{2,3},{3,2},{4,5},{5,4},{6,7},{7,6},{8,9},{9,8},{10,11... | collective-permute-start | bytes 5898248 | tf_op jit(solution)/shard_map/ppermute | solution.py:754
  166.9 1.1 copy-start.9
  166.9 4.6 %copy-start.7 = (bf16[960,256]{1,0:T(8,128)(2,1)S(1)}, bf16[960,256]{1,0:T(8,128)(2,1)}, u32[]{:S(2)}) copy-start(bf16[960,256]{1,0:T(8,128)(2,1)} %get-tuple-element.94.refs_25_) | copy-start | bytes 1474564
  166.9 4.8 %copy-start.16 = (bf16[640,256]{1,0:T(8,128)(2,1)S(1)}, bf16[640,256]{1,0:T(8,128)(2,1)}, u32[]{:S(2)}) copy-start(bf16[640,256]{1,0:T(8,128)(2,1)} %get-tuple-element.88) | copy-start | bytes 983044
  167.0 4.5 %collective-permute-start.3 = (bf16[960,256]{1,0:T(8,128)(2,1)S(1)}, bf16[960,256]{1,0:T(8,128)(2,1)S(1)}, u32[]{:S(2)}, u32[]{:S(2)}) collective-permute-start(bf16[960,256]{1,0:T(8,128)(2,1)S(1)} %get-tuple-element.124), channel_id=1, source_target_pairs={{0,1},{1,0},{2,3},{3,2},{4,5},{5,4},{6,7},{7,6},{8,9},{9,8},{10,11... | collective-permute-start | bytes 1474568 | tf_op jit(solution)/shard_map/ppermute | solution.py:754
  167.8 4.4 %collective-permute-start.5 = (bf16[960,256]{1,0:T(8,128)(2,1)S(1)}, bf16[960,256]{1,0:T(8,128)(2,1)S(1)}, u32[]{:S(2)}, u32[]{:S(2)}) collective-permute-start(bf16[960,256]{1,0:T(8,128)(2,1)S(1)} %copy-done.2), channel_id=1, source_target_pairs={{0,1},{1,0},{2,3},{3,2},{4,5},{5,4},{6,7},{7,6},{8,9},{9,8},{10,11... | collective-permute-start | bytes 1474568 | tf_op jit(solution)/shard_map/ppermute | solution.py:754
  168.0 5.5 %copy-start.6 = (bf16[960,256]{1,0:T(8,128)(2,1)S(1)}, bf16[960,256]{1,0:T(8,128)(2,1)}, u32[]{:S(2)}) copy-start(bf16[960,256]{1,0:T(8,128)(2,1)} %get-tuple-element.92.refs_21_) | copy-start | bytes 1474564
  168.0 5.9 %copy-start.5 = (bf16[960,256]{1,0:T(8,128)(2,1)S(1)}, bf16[960,256]{1,0:T(8,128)(2,1)}, u32[]{:S(2)}) copy-start(bf16[960,256]{1,0:T(8,128)(2,1)} %get-tuple-element.93.refs_23_) | copy-start | bytes 1474564
  168.0 6.1 %copy-start.8 = (bf16[960,256]{1,0:T(8,128)(2,1)S(1)}, bf16[960,256]{1,0:T(8,128)(2,1)}, u32[]{:S(2)}) copy-start(bf16[960,256]{1,0:T(8,128)(2,1)} %get-tuple-element.95.refs_27_) | copy-start | bytes 1474564
  168.1 5.4 %collective-permute-start.2 = (bf16[960,256]{1,0:T(8,128)(2,1)S(1)}, bf16[960,256]{1,0:T(8,128)(2,1)S(1)}, u32[]{:S(2)}, u32[]{:S(2)}) collective-permute-start(bf16[960,256]{1,0:T(8,128)(2,1)S(1)} %get-tuple-element.126), channel_id=1, source_target_pairs={{0,1},{1,0},{2,3},{3,2},{4,5},{5,4},{6,7},{7,6},{8,9},{9,8},{10,11... | collective-permute-start | bytes 1474568 | tf_op jit(solution)/shard_map/ppermute | solution.py:754
  171.5 2.3 collective-permute-start.8
  172.2 1.9 collective-permute-start.4
  173.5 4.5 %collective-permute-start.6 = (bf16[960,256]{1,0:T(8,128)(2,1)S(1)}, bf16[960,256]{1,0:T(8,128)(2,1)S(1)}, u32[]{:S(2)}, u32[]{:S(2)}) collective-permute-start(bf16[960,256]{1,0:T(8,128)(2,1)S(1)} %copy-done.6), channel_id=1, source_target_pairs={{0,1},{1,0},{2,3},{3,2},{4,5},{5,4},{6,7},{7,6},{8,9},{9,8},{10,11... | collective-permute-start | bytes 1474568 | tf_op jit(solution)/shard_map/ppermute | solution.py:754
  173.9 2.6 copy-start.10
  173.9 4.1 %collective-permute-start.7 = (bf16[960,256]{1,0:T(8,128)(2,1)S(1)}, bf16[960,256]{1,0:T(8,128)(2,1)S(1)}, u32[]{:S(2)}, u32[]{:S(2)}) collective-permute-start(bf16[960,256]{1,0:T(8,128)(2,1)S(1)} %copy-done.5), channel_id=1, source_target_pairs={{0,1},{1,0},{2,3},{3,2},{4,5},{5,4},{6,7},{7,6},{8,9},{9,8},{10,11... | collective-permute-start | bytes 1474568 | tf_op jit(solution)/shard_map/ppermute | solution.py:754
  174.1 3.9 %collective-permute-start.9 = (bf16[960,256]{1,0:T(8,128)(2,1)S(1)}, bf16[960,256]{1,0:T(8,128)(2,1)S(1)}, u32[]{:S(2)}, u32[]{:S(2)}) collective-permute-start(bf16[960,256]{1,0:T(8,128)(2,1)S(1)} %copy-done.8), channel_id=1, source_target_pairs={{0,1},{1,0},{2,3},{3,2},{4,5},{5,4},{6,7},{7,6},{8,9},{9,8},{10,11... | collective-permute-start | bytes 1474568 | tf_op jit(solution)/shard_map/ppermute | solution.py:754
  174.5 2.1 copy-start.20
  174.5 2.1 copy-start.21
  174.5 2.1 copy-start.22
  178.0 1.1 copy-start.11
  178.0 0.8 copy-start.12
  178.0 1.1 copy-start.13
  178.8 1.3 copy-start.3
  293.2 6.9 %copy-start.4 = (f32[960,256]{1,0:T(8,128)S(1)}, f32[960,256]{1,0:T(8,128)}, u32[]{:S(2)}) copy-start(f32[960,256]{1,0:T(8,128)} %get-tuple-element.100) | copy-start | bytes 2949124
  293.2 7.9 %copy-start.14 = (f32[120,960]{1,0:T(8,128)S(1)}, f32[120,960]{1,0:T(8,128)}, u32[]{:S(2)}) copy-start(f32[120,960]{1,0:T(8,128)} %get-tuple-element.147) | copy-start | bytes 1382404
  295.4 6.5 %copy-start.19 = (f32[120,640]{1,0:T(8,128)S(1)}, f32[120,640]{1,0:T(8,128)}, u32[]{:S(2)}) copy-start(f32[120,640]{1,0:T(8,128)} %get-tuple-element.152) | copy-start | bytes 921604
  297.1 5.5 %copy-start.18 = (f32[120,640]{1,0:T(8,128)S(1)}, f32[120,640]{1,0:T(8,128)}, u32[]{:S(2)}) copy-start(f32[120,640]{1,0:T(8,128)} %get-tuple-element.153) | copy-start | bytes 921604
  300.1 3.2 %copy-start.17 = (f32[120,640]{1,0:T(8,128)S(1)}, f32[120,640]{1,0:T(8,128)}, u32[]{:S(2)}) copy-start(f32[120,640]{1,0:T(8,128)} %get-tuple-element.108) | copy-start | bytes 921604

commit v4 on v3

--- a/solution.py
+++ b/solution.py
@@ -225,10 +225,6 @@
         self.beyond_half = move(1, BEYOND, 0, cut)
         self.asides = [aside(which) for which in range(4)]
 
-    def start(self):
-        self.cross.start()
-        self.near.start()
-
     def first(self):
         self.cross.wait_recv()
         self.side.start()
@@ -272,25 +268,33 @@
     spreads = [Spread(links, own, all_ref) for own, all_ref in zip(owns, held)]
     shares = [Share(links, ref) for ref in (kv_ref, next_kv)]
     greet((SIBLING, ACROSS, SIDE, BEYOND))
+    gate_way, up_way, down_way = spreads
+    gate_way.cross.start()
     for spread, copy in zip(spreads, loads):
-        spread.start()
+        spread.near.start()
         copy.start()
     cosine, sine = cos_ref[...], sin_ref[...]
     gain_one = gain_one_ref[...].astype(HIGH)
     project(hidden, gain_one, wq_ref, wk_ref, wv_ref, cosine, sine, a_ref, q_ref, kv_ref.at[0], shares[0].start)
-    spreads[0].first()
     fill_bias(where_ref, bias, rows, blocks)
+    gate_way.first()
+    up_way.cross.start()
     shares[0].pass_on()
-    spreads[1].first()
     shares[0].finish()
     lay_keys(kv_ref, k_sc, vt_sc, blocks, rows)
-    events = {0: spreads[2].first, 2: spreads[0].second, 3: spreads[1].second, 4: spreads[2].second}
 
     def event(group):
-        for when, action in events.items():
-            pl.when(group == when)(action)
+        @pl.when(group == 2)
+        def _():
+            up_way.first()
+            down_way.cross.start()
+
+        pl.when(group == 3)(gate_way.second)
 
     attend(bias, k_sc, vt_sc, q_ref, o_ref, lse_ref, event)
+    down_way.first()
+    up_way.second()
+    gate_way.third()
     middle, normed = after_attention(hidden, o_ref, wo_ref, gain_two_ref, m_ref, b_ref)
     saves = []
 
@@ -303,11 +307,13 @@
     for copy in loads:
         copy.wait()
     total = middle + hidden_part(normed, wg, wu, wd, g_ref, u_ref, 0)
+    up_way.third()
     for spread in spreads:
-        spread.third()
         spread.near.wait_recv()
     keep(1)
     total = total + hidden_part(normed, wg, wu, wd, g_ref, u_ref, 1)
+    down_way.second()
+    down_way.third()
     keep(2)
     total = total + hidden_part(normed, wg, wu, wd, g_ref, u_ref, 2)
     for spread in spreads:
@@ -323,32 +329,11 @@
     links.drain()
 
 
-def forward_last_kernel(blocks, *refs):
-    where_ref, h_ref, q_ref, kv_ref, wo_ref, gain_two_ref = refs[:6]
-    sources = refs[6:12]
-    o_ref, lse_ref, m_ref, b_ref, g_ref, u_ref, out_ref = refs[12:19]
-    bias, k_sc, vt_sc, wg, wu, wd, sems = refs[19:]
-    rows = h_ref.shape[0]
-    copies = weights_in(sources, (wg, wu, wd), sems, (0, 1, 2))
-    fill_bias(where_ref, bias, rows, blocks)
-    lay_keys(kv_ref, k_sc, vt_sc, blocks, rows)
-    attend(bias, k_sc, vt_sc, q_ref, o_ref, lse_ref, lambda group: None)
-    total, normed = after_attention(h_ref[...], o_ref, wo_ref, gain_two_ref, m_ref, b_ref)
-    for step in range(blocks):
-        if step < 2:
-            for which in range(3):
-                copies[step, which].wait()
-        total = total + hidden_part(normed, wg, wu, wd, g_ref, u_ref, step)
-    out_ref[...] = total.T.astype(LOW)
-
-
-def ffn_back(grad, copies, g_ref, u_ref, m_ref, gain_ref, wg, wu, wd, outs):
-    f_ref, mine_ref, theirs_ref, c_ref, dm_ref, gain_part_ref = outs
-    f_ref[...] = grad.T.astype(LOW)
+def ffn_back(grad, copies, g_ref, u_ref, m_ref, gain, wg, wu, wd, mine_ref, theirs_ref):
     low_grad = grad.astype(LOW)
     grad_normed = jnp.zeros(m_ref.shape, HIGH)
     for step in range(wg.shape[0]):
-        if step < 2:
+        if copies and step < 2:
             copies[step, 2].wait()
         grad_active = nn(low_grad, wd[step])
         gate = g_ref[step].astype(HIGH)
@@ -361,61 +346,98 @@
         kept[step // 2] = grad_gate
         kept[2 + step // 2] = grad_up
         kept[4 + step // 2] = (silu * up).astype(LOW)
-        if step < 2:
+        if copies and step < 2:
             copies[step, 0].wait()
             copies[step, 1].wait()
         grad_normed = grad_normed + nt(grad_gate, wg[step]) + nt(grad_up, wu[step])
-    gain_part, grad_middle = norm_back(m_ref[...], gain_ref[...].astype(HIGH), grad_normed, grad)
-    gain_part_ref[...] = gain_part
-    dm_ref[...] = grad_middle
-    c_ref[...] = grad_middle.T.astype(LOW)
-    return grad_middle
-
-
-def attend_back(where_ref, kv_ref, wo_ref, q_ref, o_ref, lse_ref, cosine, sine, grad_middle, dq_ref, dkv_ref, room):
-    bias, k_sc, v_sc, kt_sc, do_sc, delta = room
-    blocks, rows = kv_ref.shape[:2]
-    fill_bias(where_ref, bias, rows, blocks)
+    return norm_back(m_ref[...], gain, grad_normed, grad)
+
+
+def lay_back(kv_ref, k_sc, v_sc, kt_sc, blocks, rows, keys_laid):
     for step in range(blocks):
         at = slice(step * rows, (step + 1) * rows)
-        held = kv_ref[step]
         for group in range(KVH):
-            k_sc[group, at] = held[:, group * HD : (group + 1) * HD]
-            v_sc[group, at] = held[:, KV_WIDTH + group * HD : KV_WIDTH + (group + 1) * HD]
-        kt_sc[:, at] = held[:, :KV_WIDTH].T
+            if not keys_laid:
+                k_sc[group, at] = kv_ref[step, :, group * HD : (group + 1) * HD]
+            v_sc[group, at] = kv_ref[step, :, KV_WIDTH + group * HD : KV_WIDTH + (group + 1) * HD]
+        kt_sc[:, at] = kv_ref[step, :, :KV_WIDTH].T
+
+
+def attend_back(grad_middle, wo_ref, q_ref, o_ref, lse_ref, cosine, sine, dq_ref, dkv_ref, room, between):
+    bias, k_sc, v_sc, kt_sc, do_sc, delta, dq_sc = room
+    keys, rows = bias.shape
+    blocks = keys // rows
+    half = keys // 2
     do_sc[...] = nt(wo_ref[...], grad_middle.astype(LOW)).astype(LOW)
     for head in range(HQ):
         at = slice(head * HD, (head + 1) * HD)
         product = do_sc[at].astype(HIGH) * o_ref[at].astype(HIGH)
         delta[head : head + 1] = jnp.sum(product, axis=0, keepdims=True)
 
-    def group_body(group, carry):
-        keys = k_sc[group]
-        values = v_sc[group]
-        keys_t = kt_sc[pl.ds(pl.multiple_of(group * HD, HD), HD), :]
-        grad_keys = jnp.zeros((HD, blocks * rows), HIGH)
-        grad_values = jnp.zeros((HD, blocks * rows), HIGH)
-        for member in range(PER_GROUP):
-            head = group * PER_GROUP + member
-            at = pl.ds(pl.multiple_of(head * HD, HD), HD)
-            query = q_ref[at, :]
-            grad_out = do_sc[at, :]
-            scores = nn(keys, query) + bias[...]
-            prob = jnp.exp(scores - lse_ref[pl.ds(head, 1), :])
-            grad_prob = nn(values, grad_out)
-            grad_score = (prob * (grad_prob - delta[pl.ds(head, 1), :])).astype(LOW)
-            dq_ref[at, :] = turned(nn(keys_t, grad_score), cosine, sine, -1.0, SCALE).astype(LOW)
-            grad_keys = grad_keys + nt(query, grad_score)
-            grad_values = grad_values + nt(grad_out, prob.astype(LOW))
-        at = pl.ds(pl.multiple_of(group * HD, HD), HD)
-        after = pl.ds(pl.multiple_of(KV_WIDTH + group * HD, HD), HD)
-        for step in range(blocks):
-            cut = slice(step * rows, (step + 1) * rows)
-            dkv_ref[step, at, :] = grad_keys[:, cut].astype(LOW)
-            dkv_ref[step, after, :] = grad_values[:, cut].astype(LOW)
-        return carry
-
-    lax.fori_loop(0, KVH, group_body, 0)
+    def one_pass(start, last, event):
+        cut = slice(start, start + half)
+
+        def group_body(group, carry):
+            event(group)
+            group_keys = k_sc[group, cut]
+            values = v_sc[group, cut]
+            at = pl.ds(pl.multiple_of(group * HD, HD), HD)
+            after = pl.ds(pl.multiple_of(KV_WIDTH + group * HD, HD), HD)
+            keys_t = kt_sc[at, cut]
+            grad_keys = jnp.zeros((HD, half), HIGH)
+            grad_values = jnp.zeros((HD, half), HIGH)
+            for member in range(PER_GROUP):
+                head = group * PER_GROUP + member
+                head_at = pl.ds(pl.multiple_of(head * HD, HD), HD)
+                query = q_ref[head_at, :]
+                grad_out = do_sc[head_at, :]
+                scores = nn(group_keys, query) + bias[cut]
+                prob = jnp.exp(scores - lse_ref[pl.ds(head, 1), :])
+                grad_prob = nn(values, grad_out)
+                grad_score = (prob * (grad_prob - delta[pl.ds(head, 1), :])).astype(LOW)
+                grad_query = nn(keys_t, grad_score)
+                if last:
+                    grad_query = grad_query + dq_sc[head_at, :]
+                    dq_ref[head_at, :] = turned(grad_query, cosine, sine, -1.0, SCALE).astype(LOW)
+                else:
+                    dq_sc[head_at, :] = grad_query
+                grad_keys = grad_keys + nt(query, grad_score)
+                grad_values = grad_values + nt(grad_out, prob.astype(LOW))
+            for step in range(blocks // 2):
+                part = slice(step * rows, (step + 1) * rows)
+                dkv_ref[start // rows + step, at, :] = grad_keys[:, part].astype(LOW)
+                dkv_ref[start // rows + step, after, :] = grad_values[:, part].astype(LOW)
+            return carry
+
+        lax.fori_loop(0, KVH, group_body, 0)
+
+    one_pass(half, False, lambda group: None)
+    one_pass(0, True, between)
+
+
+class Settle:
+    def __init__(self, links, dkv_ref, near_ref, sum_ref, far_ref):
+        self.refs = dkv_ref, near_ref, sum_ref, far_ref
+        self.aside = links.push(dkv_ref.at[3], near_ref.at[1], SIBLING)
+        self.near = links.push(dkv_ref.at[1], near_ref.at[0], SIBLING)
+        self.far = links.push(sum_ref, far_ref, ACROSS)
+
+    def between(self, group):
+        dkv_ref, near_ref, sum_ref, _ = self.refs
+        pl.when(group == 0)(self.aside.start)
+
+        @pl.when(group == 1)
+        def _():
+            self.aside.wait_recv()
+            sum_ref[...] = (dkv_ref[2].astype(HIGH) + near_ref[1].astype(HIGH)).astype(LOW)
+            self.far.start()
+
+    def finish(self):
+        dkv_ref, near_ref, _, far_ref = self.refs
+        self.near.start()
+        self.near.wait_recv()
+        self.far.wait_recv()
+        return dkv_ref[0].astype(HIGH) + near_ref[0].astype(HIGH) + far_ref[...].astype(HIGH)
 
 
 def attention_room(blocks, rows, width):
@@ -427,37 +449,174 @@
         pltpu.VMEM((KV_WIDTH, keys), LOW),
         pltpu.VMEM((width, rows), LOW),
         pltpu.VMEM((16, rows), HIGH),
+        pltpu.VMEM((width, rows), HIGH),
     ]
 
 
-def backward_last_kernel(*refs):
-    where_ref, e_ref, g_ref, u_ref, m_ref, gain_ref, wo_ref, q_ref, kv_ref = refs[:9]
-    o_ref, lse_ref, cos_ref, sin_ref = refs[9:13]
-    sources = refs[13:19]
-    f_ref, mine_ref, theirs_ref, c_ref, dm_ref, dq_ref, dkv_ref, gain_part_ref = refs[19:27]
-    room, (wg, wu, wd, sems) = refs[27:33], refs[33:]
-    rows = m_ref.shape[0]
-    copies = weights_in(sources, (wg, wu, wd), sems, (2, 0, 1))
+class Local:
+    def __init__(self, sems):
+        self.sems, self.used, self.flying = sems, 0, []
+
+    def move(self, source, target, start=True):
+        copy = pltpu.make_async_copy(source, target, self.sems.at[self.used])
+        self.used += 1
+        self.flying.append(copy)
+        if start:
+            copy.start()
+        return copy
+
+    def drain(self):
+        for copy in self.flying:
+            copy.wait()
+
+
+def share_out(local, links, core, zero, one, target, own_at, got_at):
+    if zero is one:
+        keep = local.move(zero, target.at[own_at])
+        send = links.push(zero, target.at[got_at], SIBLING)
+        send.start()
+        return keep, send
+    keep = local.move(zero, target.at[own_at], False)
+    keep_one = pltpu.make_async_copy(one, target.at[own_at], local.sems.at[local.used - 1])
+    send = links.push(one, target.at[got_at], SIBLING)
+    links.used -= 1
+    links.flying.pop()
+    send_zero = links.push(zero, target.at[got_at], SIBLING)
+
+    @pl.when(core == 0)
+    def _():
+        keep.start()
+        send.start()
+
+    @pl.when(core == 1)
+    def _():
+        keep_one.start()
+        send_zero.start()
+
+    return keep, send
+
+
+COPIES_MIDDLE = 16
+LOCALS_MIDDLE = 24
+
+
+def middle_kernel(blocks, *refs):
+    where_ref, h_ref, q_ref, kv_ref, wo_ref, gain_one_ref, gain_two_ref, cos_ref, sin_ref = refs[:9]
+    cot_any, wq_any, wk_any, wv_any, g_any, u_any, m_any, a_any, b_any = refs[9:18]
+    sources = refs[18:24]
+    out_ref, c_ref, dm_ref, gains_ref = refs[24:28]
+    b_all, f_all, rhs_all, left_two, long_two, short_two, side_two = refs[28:35]
+    room = refs[35:42]
+    bias, k_sc, v_sc, kt_sc = room[:4]
+    vt_sc, o_sc, lse_sc, m_sc, b_sc, f_sc, c_sc, g_sc, u_sc = refs[42:51]
+    mine, theirs, dq_sc, dkv_sc, dkv_near, dkv_sum, dkv_far, dkv_low = refs[51:59]
+    cot, wq, wk, wv = refs[59:63]
+    wg, wu, wd, sems, load, send, receive = refs[63:]
+    rows = h_ref.shape[0]
+    core = lax.axis_index("head") % 2
+    copies = weights_in(sources, (wg, wu, wd), sems, (0, 1, 2))
+    local = Local(load)
+    links = Links(send, receive)
+    late = [local.move(source, target) for source, target in ((cot_any, cot), (wq_any, wq), (wk_any, wk), (wv_any, wv))]
+    settle = Settle(links, dkv_sc, dkv_near, dkv_sum, dkv_far)
+    spans = [pl.ds(i * rows, rows) for i in range(4)]
+    everything = slice(None)
+
+    def both(source, target, place):
+        keep = local.move(source, target.at[(*place, spans[both.layer])])
+        copy = links.push(source, target.at[(*place, spans[both.layer + 1])], SIBLING)
+        copy.start()
+        return keep, copy
+
+    greet((SIBLING, ACROSS))
+    both.layer = 2
+    posted = [both(b_any, b_all, (everything,))]
+    both.layer = 0
+    fill_bias(where_ref, bias, rows, blocks)
+    lay_keys(kv_ref, k_sc, vt_sc, blocks, rows)
+    attend(bias, k_sc, vt_sc, q_ref, o_sc, lse_sc, lambda group: None)
+    total, normed = after_attention(h_ref[...], o_sc, wo_ref, gain_two_ref, m_sc, b_sc)
+    posted.append(both(b_sc, b_all, (everything,)))
+    for step in range(blocks):
+        if step < 2:
+            for which in range(3):
+                copies[step, which].wait()
+        total = total + hidden_part(normed, wg, wu, wd, g_sc, u_sc, step)
+    out_ref[...] = total.T.astype(LOW)
+    lay_back(kv_ref, k_sc, v_sc, kt_sc, blocks, rows, True)
+
+    late[0].wait()
     row = where_ref[0] * rows + lax.broadcasted_iota(jnp.int32, (rows, 1), 0)
-    grad = jnp.where(row < where_ref[1], e_ref[...].astype(HIGH).T, 0.0)
-    outs = (f_ref, mine_ref, theirs_ref, c_ref, dm_ref, gain_part_ref)
-    grad_middle = ffn_back(grad, copies, g_ref, u_ref, m_ref, gain_ref, wg, wu, wd, outs)
+    grad = jnp.where(row < where_ref[1], cot[...].astype(HIGH).T, 0.0)
+    f_sc[...] = grad.T.astype(LOW)
+    first_f = both(f_sc, f_all, (everything,))
+    gain_two = gain_two_ref[...].astype(HIGH)
+    gain_part, grad_middle = ffn_back(grad, None, g_sc, u_sc, m_sc, gain_two, wg, wu, wd, mine, theirs)
+    first_loads = [local.move(source, target) for source, target in ((g_any, g_sc), (u_any, u_sc), (m_any, m_sc))]
+    keep_mine = local.move(mine, rhs_all.at[:, spans[0]])
+    send_theirs = links.push(theirs, rhs_all.at[:, spans[1]], SIBLING)
+    send_theirs.start()
+    gains_ref[...] = jnp.zeros(gains_ref.shape, HIGH)
+    gains_ref[1:2] = gain_part
+    c_sc[...] = grad_middle.T.astype(LOW)
+    cosine, sine = cos_ref[...], sin_ref[...]
     attend_back(
-        where_ref, kv_ref, wo_ref, q_ref, o_ref, lse_ref, cos_ref[...], sin_ref[...], grad_middle, dq_ref, dkv_ref, room
+        grad_middle, wo_ref, q_ref, o_sc, lse_sc, cosine, sine, dq_sc, dkv_sc, room, settle.between
     )
-
-
-def ffn_back_kernel(*refs):
-    e_ref, g_ref, u_ref, m_ref, gain_ref = refs[:5]
-    sources, outs, (wg, wu, wd, sems) = refs[5:11], refs[11:17], refs[17:]
-    copies = weights_in(sources, (wg, wu, wd), sems, (2, 0, 1))
-    ffn_back(e_ref[...], copies, g_ref, u_ref, m_ref, gain_ref, wg, wu, wd, outs)
+    grad_keys, grad_values = close_keys(settle.finish(), cosine, sine, dkv_low)
+    low_rows, high_rows = pl.ds(0, KV_WIDTH), pl.ds(KV_WIDTH, KV_WIDTH)
+    for zero, one, target in (
+        (a_any, c_sc, left_two),
+        (dq_sc, o_sc, long_two),
+        (dkv_low.at[low_rows], dkv_low.at[high_rows], short_two),
+        (a_any, a_any, side_two),
+    ):
+        posted.append(
+            share_out(local, links, core, zero, one, target, (everything, spans[0]), (everything, spans[1]))
+        )
+    for copy in late[1:]:
+        copy.wait()
+    gain_one = gain_one_ref[...].astype(HIGH)
+    gain_part, grad = close_rows(h_ref[...], gain_one, grad_middle, dq_sc, grad_keys, grad_values, wq, wk, wv)
+    gains_ref[0:1] = gain_part
+
+    first_f[0].wait()
+    first_f[1].wait_send()
+    keep_mine.wait()
+    send_theirs.wait_send()
+    for copy in first_loads:
+        copy.wait()
+    f_sc[...] = grad.T.astype(LOW)
+    both.layer = 2
+    posted.append(both(f_sc, f_all, (everything,)))
+    gain_part, grad_middle = ffn_back(grad, None, g_sc, u_sc, m_sc, gain_two, wg, wu, wd, mine, theirs)
+    keep_last = local.move(mine, rhs_all.at[:, spans[2]])
+    send_last = links.push(theirs, rhs_all.at[:, spans[3]], SIBLING)
+    send_last.start()
+    gains_ref[1:2] = gains_ref[1:2] + gain_part
+    dm_ref[...] = grad_middle
+    c_ref[...] = grad_middle.T.astype(LOW)
+    for keep, copy in posted:
+        keep.wait()
+        copy.wait()
+    first_f[1].wait_recv()
+    send_theirs.wait_recv()
+    keep_last.wait()
+    send_last.wait()
+    settle.aside.wait_send()
+    settle.near.wait_send()
+    settle.far.wait_send()
 
 
 def attend_back_kernel(*refs):
     where_ref, dm_ref, wo_ref, q_ref, kv_ref, o_ref, lse_ref, cos_ref, sin_ref, dq_ref, dkv_ref = refs[:11]
+    room = refs[11:]
+    bias, k_sc, v_sc, kt_sc = room[:4]
+    blocks, rows = kv_ref.shape[:2]
+    fill_bias(where_ref, bias, rows, blocks)
+    lay_back(kv_ref, k_sc, v_sc, kt_sc, blocks, rows, False)
     attend_back(
-        where_ref, kv_ref, wo_ref, q_ref, o_ref, lse_ref, cos_ref[...], sin_ref[...], dm_ref[...], dq_ref, dkv_ref, refs[11:]
+        dm_ref[...], wo_ref, q_ref, o_ref, lse_ref, cos_ref[...], sin_ref[...], dq_ref, dkv_ref, room, lambda group: None
     )
 
 
@@ -468,23 +627,22 @@
     return turned_keys.T.astype(LOW), total[KV_WIDTH:].T.astype(LOW)
 
 
-def close_rows(hidden, gain, dm_ref, dq_ref, grad_keys, grad_values, wq_ref, wk_ref, wv_ref):
+def close_rows(hidden, gain, grad_middle, dq_ref, grad_keys, grad_values, wq_ref, wk_ref, wv_ref):
     grad_normed = nn(wq_ref[...], dq_ref[...]).T
     grad_normed = grad_normed + nn(grad_keys, wk_ref[...]) + nn(grad_values, wv_ref[...])
-    return norm_back(hidden, gain, grad_normed, dm_ref[...])
-
-
-def close_kernel(last, *refs):
+    return norm_back(hidden, gain, grad_normed, grad_middle)
+
+
+def close_kernel(*refs):
     h_ref, gain_ref, dm_ref, dq_ref, wq_ref, wk_ref, wv_ref, cos_ref, sin_ref = refs[:9]
     own, near, far, dh_ref, dkv_ref, gain_part_ref = refs[9:]
     total = own[...].astype(HIGH) + near[...].astype(HIGH) + far[...].astype(HIGH)
     grad_keys, grad_values = close_keys(total, cos_ref[...], sin_ref[...], dkv_ref)
-    hidden = h_ref[...].astype(HIGH)
-    hidden = hidden if last else hidden.T
+    hidden = h_ref[...].astype(HIGH).T
     gain = gain_ref[...].astype(HIGH)
-    gain_part, grad_in = close_rows(hidden, gain, dm_ref, dq_ref, grad_keys, grad_values, wq_ref, wk_ref, wv_ref)
+    gain_part, grad_in = close_rows(hidden, gain, dm_ref[...], dq_ref, grad_keys, grad_values, wq_ref, wk_ref, wv_ref)
     gain_part_ref[...] = gain_part
-    dh_ref[...] = grad_in if last else grad_in.T
+    dh_ref[...] = grad_in.T
 
 
 class Halving:
@@ -537,23 +695,23 @@
 COPIES_FINISH = 3 * 4 + 2 * 4 + 4 + 5 + 3 + 4
 
 
-def finish_kernel(layers, *refs):
+def finish_kernel(*refs):
     where_ref, h_ref, gain_ref, dm_ref, wo_ref, q_ref, kv_ref, o_ref, lse_ref = refs[:9]
     wq_ref, wk_ref, wv_ref, cos_ref, sin_ref, a_ref, c_ref = refs[9:16]
     left_two, long_two, short_two, side_two = refs[16:20]
     gains_ref = refs[20]
     count = 4
-    b_any, f_any, rhs_any = refs[21:25], refs[25:29], refs[29:33]
-    dh_ref, gate_out, up_out, down_out = refs[33:37]
-    query_out, key_out, value_out, output_out, gain_out = refs[37:42]
-    room = refs[42:48]
-    dq_ref, dkv_ref, dkv_near, dkv_sum, dkv_far, dkv_low = refs[48:54]
-    b_all, f_all, rhs, left_all, long_all, short_all, side_all = refs[54:61]
-    wholes, rooms = refs[61:64], (refs[64:68], refs[68:72], refs[72:76])
-    attn_wholes, attn_rooms = refs[76:78], (refs[78:82], refs[82:86])
-    attn_alls = refs[86:88]
-    gain_whole, gain_got, gain_side = refs[88:91]
-    load, send, receive = refs[91:]
+    b_any, f_any, rhs_any = refs[21:24]
+    dh_ref, gate_out, up_out, down_out = refs[24:28]
+    query_out, key_out, value_out, output_out, gain_out = refs[28:33]
+    room = refs[33:40]
+    dq_ref, dkv_ref, dkv_near, dkv_sum, dkv_far, dkv_low = refs[40:46]
+    b_all, f_all, rhs, left_all, long_all, short_all, side_all = refs[46:53]
+    wholes, rooms = refs[53:56], (refs[56:60], refs[60:64], refs[64:68])
+    attn_wholes, attn_rooms = refs[68:70], (refs[70:74], refs[74:78])
+    attn_alls = refs[78:80]
+    gain_whole, gain_got, gain_side = refs[80:83]
+    load, send, receive = refs[83:]
     rows = h_ref.shape[1]
     block = gate_out.shape[0]
     place = lax.axis_index("dp")
@@ -563,28 +721,19 @@
     reduces = [halved(links, whole, got, order) for whole, got, order in zip(wholes, rooms, ORDERS)]
     attn = [halved(links, whole, got, order) for whole, got, order in zip(attn_wholes, attn_rooms, ATTN_ORDERS)]
 
-    loads = []
-
-    def load_in(source, target):
-        copy = pltpu.make_async_copy(source, target, load.at[len(loads)])
-        loads.append(copy)
-        copy.start()
-        return copy
-
-    columns = [pl.ds(i * rows, rows) for i in range(count)]
+    local = Local(load)
     wanted = (1, 2, 3, 4, 5, 0)
 
     def fetch(turn):
-        return [load_in(rhs_any[i].at[wanted[turn]], rhs.at[turn % 2, columns[i]]) for i in range(count)]
-
-    b_loads = [load_in(b_any[i], b_all.at[:, columns[i]]) for i in range(count)]
+        return local.move(rhs_any.at[wanted[turn]], rhs.at[turn % 2])
+
+    b_load = local.move(b_any, b_all)
     coming = fetch(0)
-    f_loads = [load_in(f_any[i], f_all.at[:, columns[i]]) for i in range(count)]
+    f_load = local.move(f_any, f_all)
     two = ((left_two, left_all), (long_two, long_all), (short_two, short_all), (side_two, side_all))
-    two_loads = [load_in(source, target.at[:, pl.ds(0, 2 * rows)]) for source, target in two]
+    two_loads = [local.move(source, target.at[:, pl.ds(0, 2 * rows)]) for source, target in two]
     greet((SIBLING, ACROSS, SIDE, BEYOND, FAR_SIDE))
-    for copy in b_loads:
-        copy.wait()
+    b_load.wait()
 
     def lay(product, whole, first):
         for index in range(8):
@@ -594,13 +743,11 @@
             ].astype(LOW)
 
     for turn, which in enumerate(wanted):
-        for copy in coming:
-            copy.wait()
+        coming.wait()
         if turn < 5:
             coming = fetch(turn + 1)
         if which == 4:
-            for copy in f_loads:
-                copy.wait()
+            f_load.wait()
         lay(nn((b_all if which < 4 else f_all)[...], rhs[turn % 2]), wholes[which // 2], which % 2)
         if which == 1:
             reduces[0].start(0)
@@ -610,51 +757,31 @@
             reduces[2].start(0)
 
     cosine, sine = cos_ref[...], sin_ref[...]
-    attend_back(where_ref, kv_ref, wo_ref, q_ref, o_ref, lse_ref, cosine, sine, dm_ref[...], dq_ref, dkv_ref, room)
-    near = [links.push(dkv_ref.at[3], dkv_near.at[1], SIBLING), links.push(dkv_ref.at[1], dkv_near.at[0], SIBLING)]
-    far = links.push(dkv_sum, dkv_far, ACROSS)
-    for copy in near:
-        copy.start()
-    near[0].wait_recv()
-    dkv_sum[...] = (dkv_ref[2].astype(HIGH) + dkv_near[1].astype(HIGH)).astype(LOW)
-    far.start()
+    bias, k_sc, v_sc, kt_sc = room[:4]
+    settle = Settle(links, dkv_ref, dkv_near, dkv_sum, dkv_far)
+    fill_bias(where_ref, bias, rows, count)
+    lay_back(kv_ref, k_sc, v_sc, kt_sc, count, rows, False)
+    attend_back(
+        dm_ref[...], wo_ref, q_ref, o_ref, lse_ref, cosine, sine, dq_ref, dkv_ref, room, settle.between
+    )
+    total = settle.finish()
     for reduce in reduces:
         reduce.fold(0)
-    near[1].wait_recv()
-    far.wait_recv()
-    total = dkv_ref[0].astype(HIGH) + dkv_near[0].astype(HIGH) + dkv_far[...].astype(HIGH)
     grad_keys, grad_values = close_keys(total, cosine, sine, dkv_low)
 
     low_rows, own_at, got_at = pl.ds(0, KV_WIDTH), pl.ds(2 * rows, rows), pl.ds(3 * rows, rows)
-    high_rows = pl.ds(KV_WIDTH, KV_WIDTH)
-    pairs = (
+    high_rows, everything = pl.ds(KV_WIDTH, KV_WIDTH), slice(None)
+    swaps = []
+    for zero, one, target in (
         (a_ref, c_ref, left_all),
         (dq_ref, o_ref, long_all),
         (dkv_low.at[low_rows], dkv_low.at[high_rows], short_all),
         (a_ref, a_ref, side_all),
-    )
-    swaps, first_used = [], links.used
-    for index, (zero, one, target) in enumerate(pairs):
-        keep_zero = load_in(zero, target.at[:, own_at]) if zero is one else None
-        if keep_zero is None:
-            keep_zero = pltpu.make_async_copy(zero, target.at[:, own_at], load.at[len(loads)])
-            keep_one = pltpu.make_async_copy(one, target.at[:, own_at], load.at[len(loads)])
-            loads.append(keep_zero)
-            pl.when(core == 0)(keep_zero.start)
-            pl.when(core == 1)(keep_one.start)
-        send_one = links.push(one, target.at[:, got_at], SIBLING)
-        if zero is one:
-            send_one.start()
-        else:
-            links.used -= 1
-            links.flying.pop()
-            send_zero = links.push(zero, target.at[:, got_at], SIBLING)
-            pl.when(core == 0)(send_one.start)
-            pl.when(core == 1)(send_zero.start)
-        swaps.append((keep_zero, send_one))
+    ):
+        swaps.append(share_out(local, links, core, zero, one, target, (everything, own_at), (everything, got_at)))
     hidden = h_ref[...].astype(HIGH).T
     gain = gain_ref[...].astype(HIGH)
-    gain_part, grad_in = close_rows(hidden, gain, dm_ref, dq_ref, grad_keys, grad_values, wq_ref, wk_ref, wv_ref)
+    gain_part, grad_in = close_rows(hidden, gain, dm_ref[...], dq_ref, grad_keys, grad_values, wq_ref, wk_ref, wv_ref)
     dh_ref[...] = grad_in.T
     for copy in two_loads:
         copy.wait()
@@ -834,48 +961,40 @@
     outs = forward_first()
     a_one, q_one, kv_one, o_one, lse_one, m_one, b_one, g_one, u_one, h_one, a_two, q_two, kv_two = outs[:13]
     weights = [w_gate, outs[13], w_up, outs[14], w_down, outs[15]]
-    weight_scratch = weight_room + [pltpu.SemaphoreType.DMA((3, 2))]
-
-    def forward_last():
-        specs = [SMEM] + [VMEM] * 5 + [ANY] * 6
-        body = functools.partial(forward_last_kernel, blocks)
-        outs = layer_outs + [(feature_rows, LOW)]
-        return call(body, outs, specs, attend_room + weight_scratch, "forward_last")(
-            where, h_one, q_two, kv_two, w_output, gain_two, *weights
-        )
-
-    o_two, lse_two, m_two, b_two, g_two, u_two, block_out = forward_last()
-    ffn_outs = [
-        (feature_rows, LOW),
-        ((6, rows, hidden), LOW),
-        ((6, rows, hidden), LOW),
-        (feature_rows, LOW),
-        ((rows, width), HIGH),
-    ]
     attend_outs = [(feature_rows, LOW), ((blocks, 2 * KV_WIDTH, rows), LOW)]
-    gain_outs = [((1, width), HIGH)]
     room = attention_room(blocks, rows, width)
-
-    def backward_last():
-        given = [where, cotangent, g_two, u_two, m_two, gain_two, w_output, q_two, kv_two, o_two, lse_two]
-        specs = [SMEM] + [VMEM] * 12 + [ANY] * 6
-        return call(
-            backward_last_kernel, ffn_outs + attend_outs + gain_outs, specs, room + weight_scratch, "backward_last"
-        )(*given, cosine, sine, *weights)
-
-    def close(h, grad_middle, grad_query, partial, last):
+    key_room = [(blocks, 2 * KV_WIDTH, rows), (2, 2 * KV_WIDTH, rows)] + [(2 * KV_WIDTH, rows)] * 3
+
+    def middle():
+        outs = [(feature_rows, LOW), (feature_rows, LOW), ((rows, width), HIGH), ((8, width), HIGH)]
+        outs += [((width, 4 * rows), LOW)] * 2 + [((6, 4 * rows, hidden), LOW)]
+        outs += [((n, 2 * rows), LOW) for n in (width, HQ * HD, KV_WIDTH, width)]
+        scratch = room + [
+            pltpu.VMEM((KV_WIDTH, keys), LOW),
+            pltpu.VMEM(feature_rows, LOW),
+            pltpu.VMEM((16, rows), HIGH),
+            pltpu.VMEM((rows, width), HIGH),
+        ]
+        scratch += [pltpu.VMEM(feature_rows, LOW)] * 3 + [pltpu.VMEM((blocks, rows, hidden), LOW)] * 2
+        scratch += [pltpu.VMEM((6, rows, hidden), LOW)] * 2 + [pltpu.VMEM(feature_rows, LOW)]
+        scratch += [pltpu.VMEM(shape, LOW) for shape in key_room]
+        scratch += [pltpu.VMEM(v.shape, LOW) for v in (cotangent, w_query, w_key, w_value)]
+        scratch += weight_room + [pltpu.SemaphoreType.DMA((3, 2)), pltpu.SemaphoreType.DMA((LOCALS_MIDDLE,))]
+        scratch += [pltpu.SemaphoreType.DMA((COPIES_MIDDLE,)), pltpu.SemaphoreType.DMA((COPIES_MIDDLE,))]
+        given = [where, h_one, q_two, kv_two, w_output, gain_one, gain_two, cosine, sine]
+        given += [cotangent, w_query, w_key, w_value, g_one, u_one, m_one, a_two, b_one, *weights]
+        specs = [SMEM] + [VMEM] * 8 + [ANY] * 15
+        return call(functools.partial(middle_kernel, blocks), outs, specs, scratch, "middle", 7, 3)(*given)
+
+    block_out, c_one, dm_one, gains, b_all, f_all, rhs_all, *halves_two = middle()
+
+    def close(h, grad_middle, grad_query, partial):
         sent = swap(jnp.stack([partial[1], partial[3]]), 1)
         far = swap((partial[2].astype(HIGH) + sent[1].astype(HIGH)).astype(LOW), 2)
-        outs = [((rows, width) if last else feature_rows, HIGH), ((2 * KV_WIDTH, rows), LOW), ((1, width), HIGH)]
+        outs = [(feature_rows, HIGH), ((2 * KV_WIDTH, rows), LOW), ((1, width), HIGH)]
         given = [h, gain_one, grad_middle, grad_query, w_query, w_key, w_value, cosine, sine]
         given += [partial[0], sent[0], far]
-        return call(functools.partial(close_kernel, last), outs, [VMEM] * 12, [], "close")(*given)
-
-    f_two, mine_two, theirs_two, c_two, dm_two, dq_two, part_two, gain_two_b = backward_last()
-    e_one, dkv_two, gain_one_b = close(h_one, dm_two, dq_two, part_two, True)
-    f_one, mine_one, theirs_one, c_one, dm_one, gain_two_a = call(
-        ffn_back_kernel, ffn_outs + gain_outs, [VMEM] * 5 + [ANY] * 6, weight_scratch, "ffn_back"
-    )(e_one, g_one, u_one, m_one, gain_two, *weights)
+        return call(close_kernel, outs, [VMEM] * 12, [], "close")(*given)
 
     def beside(parts):
         return jnp.concatenate(parts, axis=-1)
@@ -890,19 +1009,13 @@
         short = [choose(dk, dv), swap(choose(dv, dk), 1)]
         return beside(left), beside(long), beside(short), beside([a, swap(a, 1)])
 
-    halves_two = halves(a_two, c_two, o_two, dq_two, dkv_two)
-    b_all = [b_two, swap(b_two, 1), b_one, swap(b_one, 1)]
-    f_all = [f_two, swap(f_two, 1), f_one, swap(f_one, 1)]
-    sides = [mine_two, swap(theirs_two, 1), mine_one, swap(theirs_one, 1)]
     places = lax.axis_size("dp")
     block = width // places
 
     def finish():
-        gains = jnp.concatenate([gain_one_b, gain_two_a + gain_two_b, jnp.zeros((6, width), HIGH)], axis=0)
         outs = [(feature_rows, HIGH)] + [((block, hidden), HIGH)] * 3
         outs += [((block, n), HIGH) for n in (HQ * HD, KV_WIDTH, KV_WIDTH, HQ * HD)] + [((8, 128), HIGH)]
-        low_room = [feature_rows, (blocks, 2 * KV_WIDTH, rows), (2, 2 * KV_WIDTH, rows)]
-        low_room += [(2 * KV_WIDTH, rows)] * 3
+        low_room = [feature_rows] + key_room
         low_room += [(width, 4 * rows), (width, 4 * rows), (2, 4 * rows, hidden)]
         low_room += [(width, 4 * rows), (width, 4 * rows), (KV_WIDTH, 4 * rows), (width, 4 * rows)]
         low_room += [(2, 2, 2, 2, block, hidden)] * 3
@@ -918,10 +1031,8 @@
         scratch += [pltpu.SemaphoreType.DMA((COPIES_FINISH,))]
         given = [where, tokens, gain_one, dm_one, w_output, q_one, kv_one, o_one, lse_one]
         given += [w_query, w_key, w_value, cosine, sine, a_one, c_one, *halves_two, gains]
-        specs = [SMEM] + [VMEM] * 15 + [ANY] * 4 + [VMEM] + [ANY] * 12
-        return call(functools.partial(finish_kernel, 2), outs, specs, scratch, "finish", 0, 2)(
-            *given, *b_all, *f_all, *sides
-        )
+        specs = [SMEM] + [VMEM] * 15 + [ANY] * 4 + [VMEM] + [ANY] * 3
+        return call(finish_kernel, outs, specs, scratch, "finish", 0, 2)(*given, b_all, f_all, rhs_all)
 
     if places == 8 and blocks == 4:
         outs = finish()
@@ -930,11 +1041,10 @@
     else:
         given = [where, dm_one, w_output, q_one, kv_one, o_one, lse_one, cosine, sine]
         dq_one, part_one = call(attend_back_kernel, attend_outs, [SMEM] + [VMEM] * 8, room, "attend_back")(*given)
-        input_grad, dkv_one, gain_one_a = close(tokens, dm_one, dq_one, part_one, False)
+        input_grad, dkv_one, gain_one_a = close(tokens, dm_one, dq_one, part_one)
         kept, sent = [], []
         for which in range(6):
-            side = jnp.concatenate([each[which] for each in sides], 0)
-            product = nn(beside(b_all if which < 4 else f_all), side).astype(LOW)
+            product = nn(b_all if which < 4 else f_all, rhs_all[which]).astype(LOW)
             (sent if which % 2 else kept).append(product)
         got = swap(beside(sent), 2)
         ffn = scatter_rows((beside(kept).astype(HIGH) + got.astype(HIGH)).astype(LOW), "dp")
@@ -944,7 +1054,7 @@
         attn = (attn.astype(HIGH) + swap(attn, 2).astype(HIGH)).astype(LOW)
         other = swap(attn, 1)
         zero, one = choose(attn, other).astype(HIGH), choose(other, attn).astype(HIGH)
-        gains = jnp.concatenate([gain_one_a + gain_one_b, gain_two_a + gain_two_b], axis=0)
+        gains = jnp.concatenate([gains[:1] + gain_one_a, gains[1:2]], axis=0)
         gains = lax.psum_scatter(lax.psum(gains, "head"), "dp", scatter_dimension=1, tiled=True)
         query_grad, key_grad = zero[:, : HQ * HD], zero[:, HQ * HD :]
         output_grad, value_grad = one[:, : HQ * HD], one[:, HQ * HD :]

time: 310 us -> 291 us (0.939)
  waiting for transfers between devices: 12.9 us -> 0 us
  Pallas kernels: 258 us -> 270 us
  other arithmetic: 7.28 us -> 1.43 us
  local copies, waits for them, and re-layouts: 19.4 us -> 14 us
  starting transfers between devices: 4.44 us -> 0 us
    pallas_call x5 -> x2, Pallas kernels: 180 us -> 194 us  [the longest x1 114 us: finish(): call(finish_kernel, outs, specs, scratch, 'finish', 0, 2)]
    ppermute x12 -> x0, waiting for transfers between devices: 12.9 us -> none  [swap(): lax.ppermute(value, 'head', [(i, i ^ distance) for i in range(count)])]
    concatenate x5 -> x0, other arithmetic: 4.56 us -> none  [the longest x4 3.87 us: beside(): return jnp.concatenate(parts, axis=-1)]
    ppermute x12 -> x0, starting transfers between devices: 4.44 us -> none  [swap(): lax.ppermute(value, 'head', [(i, i ^ distance) for i in range(count)])]
    unnamed x54 -> x21, local copies, waits for them, and re-layouts: 12.8 us -> 10.2 us
  transfers between devices with their start and end apart: 12 -> 0, of which waited for: 4 -> 0; matrix products, arithmetic and copies ran while one was open for 2% -> 0% of each run, Pallas kernels for 6% -> 0%
where the time goes in v4:
time: 291 us; the launch traced here: 287 us
  Pallas kernels  270 us (93%)
  local copies, waits for them, and re-layouts  14 us (5%)
    pallas_call x1, Pallas kernels, finish(): call(finish_kernel, outs, specs, scratch, 'finish', 0, 2)  114 us
    pallas_call x1, Pallas kernels, middle(): call(functools.partial(middle_kernel, blocks), outs, specs, scratch, 'mid...  79.2 us
    pallas_call x1, Pallas kernels, forward_first(): call(body, outs, specs, scratch, 'forward_first', 3, 1)  76.3 us
    unnamed x21, local copies, waits for them, and re-layouts  10.2 us

profile of v4, /device:TPU:0, one launch (start us, length us, event | category | flops | bytes accessed | tf_op | source)
XLA Modules:
  0.0 286.9 jit_solution(10668181334258634966)
XLA Ops:
  1.3 0.6 pad_add_fusion.refs_0_
  1.9 1.3 broadcast_in_dim.8.refs_2_.refs_5_
  3.2 1.3 broadcast_in_dim.9.refs_9_.refs_6_
  4.5 0.8 multiply_sine_fusion
  5.3 76.3 %forward_first.1 = (bf16[960,256]{1,0:T(8,128)(2,1)}, bf16[960,256]{1,0:T(8,128)(2,1)}, bf16[4,256,640]{2,1,0:T(8,128)(2,1)}, bf16[960,256]{1,0:T(8,128)(2,1)}, ...) custom-call(s32[2]{0:T(128)} %pad_add_fusion.refs_0_, ...), custom_call_target="tpu_custom_call" | custom-call | tf_op jit(solution)/shard_map/forward_first/pallas_call | solution.py:957
  81.6 79.2 %middle.1 = (bf16[960,256]{1,0:T(8,128)(2,1)}, bf16[960,256]{1,0:T(8,128)(2,1)}, f32[256,960]{1,0:T(8,128)}, f32[8,960]{1,0:T(8,128)}, bf16[960,1024]{1,0:T(8,12...) custom-call(s32[2]{0:T(128)} %pad_add_fusion.refs_0_, ...), custom_call_target="tpu_custom_call" | custom-call | tf_op jit(solution)/shard_map/middle/pallas_call | solution.py:987
  160.8 114.4 %finish.1 = (f32[960,256]{1,0:T(8,128)}, f32[120,640]{1,0:T(8,128)}, f32[120,640]{1,0:T(8,128)}, f32[120,640]{1,0:T(8,128)}, f32[120,960]{1,0:T(8,128)}, /*index...) custom-call(s32[2]{0:T(128)} %pad_add_fusion.refs_0_, bf16[960,256]{1,0:T(8,128)(2,1)} %bitcast.23, ...), custom_call_target="tpu_custom_call" | custom-call | tf_op jit(solution)/shard_map/finish/pallas_call | solution.py:1035
  275.2 0.0 copy-start.1
  275.2 0.0 copy-start
  275.2 1.3 slice_bitcast_fusion
  276.6 1.7 copy.23
  278.3 1.7 copy.24
  280.0 0.0 copy-start.2
  280.0 2.1 copy.25
  282.0 0.0 copy-done.1
  282.0 0.0 copy-start.5
  282.1 0.8 copy.33
  282.8 0.0 copy-done
  282.8 0.0 copy-start.4
  282.8 0.0 copy-start.3
  282.8 0.9 copy.34
  283.8 0.0 copy-done.2
  283.8 0.8 copy.35
  284.6 0.0 copy-done.5
  284.6 0.7 copy.36
  285.3 0.0 copy-done.4
  285.3 0.7 copy.37
  286.0 0.0 copy-done.3
  286.0 0.7 copy.38
  (2 shorter events, 0.0 us)
Async XLA Ops:
  275.2 6.8 %copy-start.1 = (bf16[960,256]{1,0:T(8,128)(2,1)S(1)}, bf16[960,256]{1,0:T(8,128)(2,1)}, u32[]{:S(2)}) copy-start(bf16[960,256]{1,0:T(8,128)(2,1)} %get-tuple-element.58) | copy-start | bytes 1474564
  275.2 7.6 %copy-start = (f32[960,256]{1,0:T(8,128)S(1)}, f32[960,256]{1,0:T(8,128)}, u32[]{:S(2)}) copy-start(f32[960,256]{1,0:T(8,128)} %get-tuple-element.74) | copy-start | bytes 2949124
  280.0 3.8 %copy-start.2 = (f32[120,960]{1,0:T(8,128)S(1)}, f32[120,960]{1,0:T(8,128)}, u32[]{:S(2)}) copy-start(f32[120,960]{1,0:T(8,128)} %get-tuple-element.112) | copy-start | bytes 1382404
  282.0 2.5 copy-start.5
  282.8 2.5 copy-start.4
  282.8 3.2 %copy-start.3 = (f32[120,640]{1,0:T(8,128)S(1)}, f32[120,640]{1,0:T(8,128)}, u32[]{:S(2)}) copy-start(f32[120,640]{1,0:T(8,128)} %get-tuple-element.82) | copy-start | bytes 921604

commit v5 on v4

--- a/solution.py
+++ b/solution.py
@@ -73,8 +73,8 @@
 
 
 def fill_bias(where_ref, bias, rows, blocks):
-    me = where_ref[0]
-    length = where_ref[1]
+    me = lax.axis_index("head")
+    length = where_ref[0]
     key = lax.broadcasted_iota(jnp.int32, (rows, rows), 0)
     query = lax.broadcasted_iota(jnp.int32, (rows, rows), 1)
     for step in range(blocks):
@@ -118,18 +118,57 @@
     lax.fori_loop(0, KVH, group_body, 0)
 
 
-def lay_keys(kv_ref, k_sc, vt_sc, blocks, rows):
-    for step in range(blocks):
+def attend_first(bias, k_sc, vt_sc, q_ref, top_ref, total_ref, part_ref, half):
+    def group_body(group, carry):
+        keys = k_sc[group, :half]
+        values = vt_sc[pl.ds(pl.multiple_of(group * HD, HD), HD), :half]
+        for member in range(PER_GROUP):
+            head = group * PER_GROUP + member
+            at = pl.ds(pl.multiple_of(head * HD, HD), HD)
+            scores = nn(keys, q_ref[at, :]) + bias[:half]
+            top = jnp.max(scores, axis=0, keepdims=True)
+            exponent = jnp.exp(scores - top)
+            top_ref[pl.ds(head, 1), :] = top
+            total_ref[pl.ds(head, 1), :] = jnp.sum(exponent, axis=0, keepdims=True)
+            part_ref[at, :] = nn(values, exponent.astype(LOW))
+        return carry
+
+    lax.fori_loop(0, KVH, group_body, 0)
+
+
+def attend_rest(bias, k_sc, vt_sc, q_ref, top_ref, total_ref, part_ref, half, o_ref, lse_ref):
+    def group_body(group, carry):
+        keys = k_sc[group, half:]
+        values = vt_sc[pl.ds(pl.multiple_of(group * HD, HD), HD), half:]
+        for member in range(PER_GROUP):
+            head = group * PER_GROUP + member
+            at = pl.ds(pl.multiple_of(head * HD, HD), HD)
+            scores = nn(keys, q_ref[at, :]) + bias[half:]
+            before = top_ref[pl.ds(head, 1), :]
+            top = jnp.maximum(before, jnp.max(scores, axis=0, keepdims=True))
+            exponent = jnp.exp(scores - top)
+            rescale = jnp.exp(before - top)
+            total = total_ref[pl.ds(head, 1), :] * rescale + jnp.sum(exponent, axis=0, keepdims=True)
+            attended = (part_ref[at, :] * rescale + nn(values, exponent.astype(LOW))) * (1.0 / total)
+            o_ref[at, :] = attended.astype(LOW)
+            lse_ref[pl.ds(head, 1), :] = top + jnp.log(total)
+        return carry
+
+    lax.fori_loop(0, KVH, group_body, 0)
+
+
+def lay_keys(kv_ref, k_sc, vt_sc, steps, rows):
+    for step in steps:
         at = slice(step * rows, (step + 1) * rows)
         for group in range(KVH):
             k_sc[group, at] = kv_ref[step, :, group * HD : (group + 1) * HD]
         vt_sc[:, at] = kv_ref[step, :, KV_WIDTH:].T
 
 
-def after_attention(hidden, o_ref, wo_ref, gain_ref, m_ref, b_ref):
+def after_attention(hidden, o_ref, wo_ref, gain, m_ref, b_ref):
     middle = hidden + nn(o_ref[...].T, wo_ref[...])
     m_ref[...] = middle
-    normed = middle * inverse_rms(middle) * gain_ref[...].astype(HIGH)
+    normed = middle * inverse_rms(middle) * gain
     b_ref[...] = normed.T.astype(LOW)
     return middle, normed.astype(LOW)
 
@@ -177,6 +216,23 @@
             copy.wait_send()
 
 
+class Local:
+    def __init__(self, sems):
+        self.sems, self.used, self.flying = sems, 0, []
+
+    def move(self, source, target, start=True):
+        copy = pltpu.make_async_copy(source, target, self.sems.at[self.used])
+        self.used += 1
+        self.flying.append(copy)
+        if start:
+            copy.start()
+        return copy
+
+    def drain(self):
+        for copy in self.flying:
+            copy.wait()
+
+
 SIBLING, ACROSS, SIDE, BEYOND = ("head", 1), ("head", 2), ("dp", 1), ("dp", 2)
 
 
@@ -254,65 +310,68 @@
 
 
 def forward_first_kernel(blocks, *refs):
-    where_ref, h_ref, gain_one_ref, wq_ref, wk_ref, wv_ref, cos_ref, sin_ref, wo_ref, gain_two_ref = refs[:10]
-    owns = refs[10:13]
-    a_ref, q_ref, kv_ref, o_ref, lse_ref, m_ref, b_ref, g_ref, u_ref, out_ref = refs[13:23]
-    next_a, next_q, next_kv = refs[23:26]
-    kept = refs[26:29]
-    bias, k_sc, vt_sc, wg, wu, wd, load, save, send, receive = refs[29:]
+    where_ref, h_ref, gain_ref, cos_ref, sin_ref = refs[:5]
+    late_refs, owns = refs[5:9], refs[9:12]
+    a_ref, q_ref, kv_ref, o_ref, lse_ref, m_ref, b_ref, g_ref, u_ref, out_ref = refs[12:22]
+    kept = refs[22:25]
+    bias, k_sc, vt_sc, wg, wu, wd = refs[25:31]
+    late, (load, send, receive) = refs[31:35], refs[35:]
+    wk_ref, wv_ref, wq_ref, wo_ref = late
     rows = h_ref.shape[1]
-    hidden = h_ref[...].astype(HIGH).T
-    links = Links(send, receive)
+    links, local = Links(send, receive), Local(load)
     held = (wg, wu, wd)
-    loads = [pltpu.make_async_copy(own, all_ref.at[0], load.at[i]) for i, (own, all_ref) in enumerate(zip(owns, held))]
-    spreads = [Spread(links, own, all_ref) for own, all_ref in zip(owns, held)]
-    shares = [Share(links, ref) for ref in (kv_ref, next_kv)]
+    lates = [local.move(source, target) for source, target in zip(late_refs, late)]
+    loads = [local.move(own, all_ref.at[0], False) for own, all_ref in zip(owns, held)]
+    gate_way, up_way, down_way = spreads = [Spread(links, own, all_ref) for own, all_ref in zip(owns, held)]
+    share = Share(links, kv_ref)
     greet((SIBLING, ACROSS, SIDE, BEYOND))
-    gate_way, up_way, down_way = spreads
     gate_way.cross.start()
+    up_way.cross.start()
     for spread, copy in zip(spreads, loads):
         spread.near.start()
         copy.start()
-    cosine, sine = cos_ref[...], sin_ref[...]
-    gain_one = gain_one_ref[...].astype(HIGH)
-    project(hidden, gain_one, wq_ref, wk_ref, wv_ref, cosine, sine, a_ref, q_ref, kv_ref.at[0], shares[0].start)
+    hidden = h_ref[...].astype(HIGH).T
+
+    def queue():
+        share.start()
+        down_way.cross.start()
+        lates[2].wait()
+
+    lates[0].wait()
+    lates[1].wait()
+    gain_one = gain_ref[0:1].astype(HIGH)
+    project(hidden, gain_one, wq_ref, wk_ref, wv_ref, cos_ref[...], sin_ref[...], a_ref, q_ref, kv_ref.at[0], queue)
+    gate_way.first()
     fill_bias(where_ref, bias, rows, blocks)
-    gate_way.first()
-    up_way.cross.start()
-    shares[0].pass_on()
-    shares[0].finish()
-    lay_keys(kv_ref, k_sc, vt_sc, blocks, rows)
+    up_way.first()
+    gate_way.second()
+    share.pass_on()
+    share.finish()
+    lay_keys(kv_ref, k_sc, vt_sc, range(blocks), rows)
 
     def event(group):
-        @pl.when(group == 2)
-        def _():
-            up_way.first()
-            down_way.cross.start()
-
-        pl.when(group == 3)(gate_way.second)
+        pl.when(group == 1)(up_way.second)
+        pl.when(group == 2)(gate_way.third)
+        pl.when(group == 3)(down_way.first)
 
     attend(bias, k_sc, vt_sc, q_ref, o_ref, lse_ref, event)
-    down_way.first()
-    up_way.second()
-    gate_way.third()
-    middle, normed = after_attention(hidden, o_ref, wo_ref, gain_two_ref, m_ref, b_ref)
+    lates[3].wait()
+    middle, normed = after_attention(hidden, o_ref, wo_ref, gain_ref[1:2].astype(HIGH), m_ref, b_ref)
     saves = []
 
     def keep(step):
         for which in range(3):
-            copy = pltpu.make_async_copy(held[which].at[step], kept[which].at[step - 1], save.at[which, step - 1])
-            copy.start()
-            saves.append(copy)
+            saves.append(local.move(held[which].at[step], kept[which].at[step - 1]))
 
     for copy in loads:
         copy.wait()
     total = middle + hidden_part(normed, wg, wu, wd, g_ref, u_ref, 0)
     up_way.third()
+    down_way.second()
     for spread in spreads:
         spread.near.wait_recv()
     keep(1)
     total = total + hidden_part(normed, wg, wu, wd, g_ref, u_ref, 1)
-    down_way.second()
     down_way.third()
     keep(2)
     total = total + hidden_part(normed, wg, wu, wd, g_ref, u_ref, 2)
@@ -321,9 +380,6 @@
     keep(3)
     total = total + hidden_part(normed, wg, wu, wd, g_ref, u_ref, 3)
     out_ref[...] = total
-    project(total, gain_one, wq_ref, wk_ref, wv_ref, cosine, sine, next_a, next_q, next_kv.at[0], shares[1].start)
-    shares[1].pass_on()
-    shares[1].finish()
     for copy in saves:
         copy.wait()
     links.drain()
@@ -363,7 +419,7 @@
         kt_sc[:, at] = kv_ref[step, :, :KV_WIDTH].T
 
 
-def attend_back(grad_middle, wo_ref, q_ref, o_ref, lse_ref, cosine, sine, dq_ref, dkv_ref, room, between):
+def attend_back(grad_middle, wo_ref, q_ref, o_ref, lse_ref, cosine, sine, dq_ref, dkv_ref, room, before, between):
     bias, k_sc, v_sc, kt_sc, do_sc, delta, dq_sc = room
     keys, rows = bias.shape
     blocks = keys // rows
@@ -411,7 +467,7 @@
 
         lax.fori_loop(0, KVH, group_body, 0)
 
-    one_pass(half, False, lambda group: None)
+    one_pass(half, False, before)
     one_pass(0, True, between)
 
 
@@ -451,23 +507,6 @@
         pltpu.VMEM((16, rows), HIGH),
         pltpu.VMEM((width, rows), HIGH),
     ]
-
-
-class Local:
-    def __init__(self, sems):
-        self.sems, self.used, self.flying = sems, 0, []
-
-    def move(self, source, target, start=True):
-        copy = pltpu.make_async_copy(source, target, self.sems.at[self.used])
-        self.used += 1
-        self.flying.append(copy)
-        if start:
-            copy.start()
-        return copy
-
-    def drain(self):
-        for copy in self.flying:
-            copy.wait()
 
 
 def share_out(local, links, core, zero, one, target, own_at, got_at):
@@ -496,28 +535,33 @@
     return keep, send
 
 
-COPIES_MIDDLE = 16
+COPIES_MIDDLE = 20
 LOCALS_MIDDLE = 24
 
 
 def middle_kernel(blocks, *refs):
-    where_ref, h_ref, q_ref, kv_ref, wo_ref, gain_one_ref, gain_two_ref, cos_ref, sin_ref = refs[:9]
-    cot_any, wq_any, wk_any, wv_any, g_any, u_any, m_any, a_any, b_any = refs[9:18]
-    sources = refs[18:24]
-    out_ref, c_ref, dm_ref, gains_ref = refs[24:28]
-    b_all, f_all, rhs_all, left_two, long_two, short_two, side_two = refs[28:35]
-    room = refs[35:42]
+    where_ref, h_ref, gain_ref, cos_ref, sin_ref = refs[:5]
+    late_refs = refs[5:10]
+    g_any, u_any, m_any, b_any = refs[10:14]
+    sources = refs[14:20]
+    out_ref, c_ref, dm_ref, gains_ref = refs[20:24]
+    b_all, f_all, rhs_all, left_two, long_two, short_two, side_two = refs[24:31]
+    room = refs[31:38]
     bias, k_sc, v_sc, kt_sc = room[:4]
-    vt_sc, o_sc, lse_sc, m_sc, b_sc, f_sc, c_sc, g_sc, u_sc = refs[42:51]
-    mine, theirs, dq_sc, dkv_sc, dkv_near, dkv_sum, dkv_far, dkv_low = refs[51:59]
-    cot, wq, wk, wv = refs[59:63]
-    wg, wu, wd, sems, load, send, receive = refs[63:]
+    part_sc = room[6]
+    vt_sc, o_sc, lse_sc, m_sc, b_sc, f_sc, c_sc, g_sc, u_sc = refs[38:47]
+    mine, theirs, dq_sc, dkv_sc, dkv_near, dkv_sum, dkv_far, dkv_low = refs[47:55]
+    late = refs[55:60]
+    a_sc, q_ref, kv_ref, top_sc, total_sc = refs[60:65]
+    wk, wv, wq, wo_ref, cot = late
+    wg, wu, wd, sems, load, send, receive = refs[65:]
     rows = h_ref.shape[0]
     core = lax.axis_index("head") % 2
-    copies = weights_in(sources, (wg, wu, wd), sems, (0, 1, 2))
     local = Local(load)
     links = Links(send, receive)
-    late = [local.move(source, target) for source, target in ((cot_any, cot), (wq_any, wq), (wk_any, wk), (wv_any, wv))]
+    lates = [local.move(source, target) for source, target in zip(late_refs, late)]
+    copies = weights_in(sources, (wg, wu, wd), sems, (0, 1, 2))
+    share = Share(links, kv_ref)
     settle = Settle(links, dkv_sc, dkv_near, dkv_sum, dkv_far)
     spans = [pl.ds(i * rows, rows) for i in range(4)]
     everything = slice(None)
@@ -532,10 +576,27 @@
     both.layer = 2
     posted = [both(b_any, b_all, (everything,))]
     both.layer = 0
+    cosine, sine = cos_ref[...], sin_ref[...]
+    half = blocks * rows // 2
+
+    def ready():
+        share.start()
+        lates[2].wait()
+
+    lates[0].wait()
+    lates[1].wait()
+    gain_one = gain_ref[0:1].astype(HIGH)
+    project(h_ref[...], gain_one, wq, wk, wv, cosine, sine, a_sc, q_ref, kv_ref.at[0], ready)
     fill_bias(where_ref, bias, rows, blocks)
-    lay_keys(kv_ref, k_sc, vt_sc, blocks, rows)
-    attend(bias, k_sc, vt_sc, q_ref, o_sc, lse_sc, lambda group: None)
-    total, normed = after_attention(h_ref[...], o_sc, wo_ref, gain_two_ref, m_sc, b_sc)
+    share.near.wait_recv()
+    lay_keys(kv_ref, k_sc, vt_sc, range(blocks // 2), rows)
+    attend_first(bias, k_sc, vt_sc, q_ref, top_sc, total_sc, part_sc, half)
+    share.pass_on()
+    share.forth.wait_recv()
+    lay_keys(kv_ref, k_sc, vt_sc, range(blocks // 2, blocks), rows)
+    attend_rest(bias, k_sc, vt_sc, q_ref, top_sc, total_sc, part_sc, half, o_sc, lse_sc)
+    lates[3].wait()
+    total, normed = after_attention(h_ref[...], o_sc, wo_ref, gain_ref[1:2].astype(HIGH), m_sc, b_sc)
     posted.append(both(b_sc, b_all, (everything,)))
     for step in range(blocks):
         if step < 2:
@@ -545,12 +606,12 @@
     out_ref[...] = total.T.astype(LOW)
     lay_back(kv_ref, k_sc, v_sc, kt_sc, blocks, rows, True)
 
-    late[0].wait()
-    row = where_ref[0] * rows + lax.broadcasted_iota(jnp.int32, (rows, 1), 0)
-    grad = jnp.where(row < where_ref[1], cot[...].astype(HIGH).T, 0.0)
+    lates[4].wait()
+    row = lax.axis_index("head") * rows + lax.broadcasted_iota(jnp.int32, (rows, 1), 0)
+    grad = jnp.where(row < where_ref[0], cot[...].astype(HIGH).T, 0.0)
     f_sc[...] = grad.T.astype(LOW)
     first_f = both(f_sc, f_all, (everything,))
-    gain_two = gain_two_ref[...].astype(HIGH)
+    gain_two = gain_ref[1:2].astype(HIGH)
     gain_part, grad_middle = ffn_back(grad, None, g_sc, u_sc, m_sc, gain_two, wg, wu, wd, mine, theirs)
     first_loads = [local.move(source, target) for source, target in ((g_any, g_sc), (u_any, u_sc), (m_any, m_sc))]
     keep_mine = local.move(mine, rhs_all.at[:, spans[0]])
@@ -559,24 +620,20 @@
     gains_ref[...] = jnp.zeros(gains_ref.shape, HIGH)
     gains_ref[1:2] = gain_part
     c_sc[...] = grad_middle.T.astype(LOW)
-    cosine, sine = cos_ref[...], sin_ref[...]
     attend_back(
-        grad_middle, wo_ref, q_ref, o_sc, lse_sc, cosine, sine, dq_sc, dkv_sc, room, settle.between
+        grad_middle, wo_ref, q_ref, o_sc, lse_sc, cosine, sine, dq_sc, dkv_sc, room, lambda group: None, settle.between
     )
     grad_keys, grad_values = close_keys(settle.finish(), cosine, sine, dkv_low)
     low_rows, high_rows = pl.ds(0, KV_WIDTH), pl.ds(KV_WIDTH, KV_WIDTH)
     for zero, one, target in (
-        (a_any, c_sc, left_two),
+        (a_sc, c_sc, left_two),
         (dq_sc, o_sc, long_two),
         (dkv_low.at[low_rows], dkv_low.at[high_rows], short_two),
-        (a_any, a_any, side_two),
+        (a_sc, a_sc, side_two),
     ):
         posted.append(
             share_out(local, links, core, zero, one, target, (everything, spans[0]), (everything, spans[1]))
         )
-    for copy in late[1:]:
-        copy.wait()
-    gain_one = gain_one_ref[...].astype(HIGH)
     gain_part, grad = close_rows(h_ref[...], gain_one, grad_middle, dq_sc, grad_keys, grad_values, wq, wk, wv)
     gains_ref[0:1] = gain_part
 
@@ -603,9 +660,8 @@
     send_theirs.wait_recv()
     keep_last.wait()
     send_last.wait()
-    settle.aside.wait_send()
-    settle.near.wait_send()
-    settle.far.wait_send()
+    for copy in (settle.aside, settle.near, settle.far, share.near, share.far, share.forth):
+        copy.wait_send()
 
 
 def attend_back_kernel(*refs):
@@ -616,7 +672,7 @@
     fill_bias(where_ref, bias, rows, blocks)
     lay_back(kv_ref, k_sc, v_sc, kt_sc, blocks, rows, False)
     attend_back(
-        dm_ref[...], wo_ref, q_ref, o_ref, lse_ref, cos_ref[...], sin_ref[...], dq_ref, dkv_ref, room, lambda group: None
+        dm_ref[...], wo_ref, q_ref, o_ref, lse_ref, cos_ref[...], sin_ref[...], dq_ref, dkv_ref, room, lambda group: None, lambda group: None
     )
 
 
@@ -639,7 +695,7 @@
     total = own[...].astype(HIGH) + near[...].astype(HIGH) + far[...].astype(HIGH)
     grad_keys, grad_values = close_keys(total, cos_ref[...], sin_ref[...], dkv_ref)
     hidden = h_ref[...].astype(HIGH).T
-    gain = gain_ref[...].astype(HIGH)
+    gain = gain_ref[0:1].astype(HIGH)
     gain_part, grad_in = close_rows(hidden, gain, dm_ref[...], dq_ref, grad_keys, grad_values, wq_ref, wk_ref, wv_ref)
     gain_part_ref[...] = gain_part
     dh_ref[...] = grad_in.T
@@ -649,24 +705,72 @@
     def __init__(self, links, steps):
         self.steps = [(links.push(sent, got, to), kept, got) for sent, kept, got, to in steps]
 
-    def start(self, which):
-        self.steps[which][0].start()
+    def start(self):
+        self.steps[0][0].start()
 
     def fold(self, which):
         copy, kept, got = self.steps[which]
         copy.wait_recv()
+        total = kept[...].astype(HIGH) + got[...].astype(HIGH)
         if which == len(self.steps) - 1:
-            return kept[...].astype(HIGH) + got[...].astype(HIGH)
-        total = kept[...].astype(HIGH) + got[...].astype(HIGH)
-        kept[...] = total.astype(kept.dtype)
-        self.steps[which + 1][0].start()
-        return None
+            self.done(total)
+        else:
+            kept[...] = total.astype(kept.dtype)
+            self.steps[which + 1][0].start()
+
+
+class Regather(Halving):
+    def share(self, links, held):
+        self.held = held
+        self.across = links.push(held.at[0, 0], held.at[0, 1], ACROSS)
+        self.aside = links.push(held.at[0], held.at[1], SIBLING)
+
+    def done(self, total):
+        self.held[0, 0] = total.astype(LOW)
+        self.across.start()
+
+    def fold(self, which):
+        if which < len(self.steps):
+            Halving.fold(self, which)
+        elif which == len(self.steps):
+            self.across.wait_recv()
+            self.aside.start()
+        else:
+            self.aside.wait_recv()
+
+
+class Rows:
+    def __init__(self, links, whole, side, got, out):
+        self.steps = (
+            (whole.at[:, :, 1], side, whole.at[:, :, 0], SIDE),
+            (whole.at[:, 1, 0], got.at[pl.ds(0, 2)], whole.at[:, 0, 0], BEYOND),
+            (whole.at[1, 0, 0], got.at[2], whole.at[0, 0, 0], FAR_SIDE),
+            (whole.at[0, 0, 0], got.at[3], None, ACROSS),
+            (got.at[4], got.at[5], None, SIBLING),
+        )
+        self.copies = [links.push(source, target, to) for source, target, _, to in self.steps]
+        self.whole, self.got, self.out = whole, got, out
+
+    def start(self):
+        self.copies[0].start()
+
+    def fold(self, which):
+        self.copies[which].wait_recv()
+        if which < 3:
+            _, target, kept, _ = self.steps[which]
+            kept[...] = kept[...] + target[...]
+        elif which == 3:
+            self.got[4] = self.whole[0, 0, 0] + self.got[3]
+        else:
+            self.out[...] = self.got[4] + self.got[5]
+        if which < 4:
+            self.copies[which + 1].start()
 
 
 FAR_SIDE = ("dp", 4)
 
 
-def halved(links, whole, rooms, order):
+def halved(kind, links, whole, rooms, order):
     where = {"X": 0, "Z1": 1, "Z0": 2, "Y": 3}
     to = {"X": ACROSS, "Z1": FAR_SIDE, "Z0": BEYOND, "Y": SIDE}
     chosen = [slice(None)] * 4
@@ -676,7 +780,7 @@
         sent[where[axis]], kept[where[axis]] = 1, 0
         steps.append((whole.at[tuple(sent)], whole.at[tuple(kept)], room, to[axis]))
         chosen = kept
-    return Halving(links, steps)
+    return kind(links, steps)
 
 
 def halving_rooms(block, columns, order):
@@ -689,47 +793,125 @@
     return rooms
 
 
-ORDERS = (("X", "Y", "Z0", "Z1"), ("Y", "Z0", "X", "Z1"), ("Z0", "X", "Y", "Z1"))
-ATTN_ORDERS = (("X", "Y", "Z0", "Z1"), ("Y", "X", "Z0", "Z1"))
-ATTN_CUTS = (256, 384)
-COPIES_FINISH = 3 * 4 + 2 * 4 + 4 + 5 + 3 + 4
+FFN_CUTS = ((0, 256), (256, 384))
+ORDERS = (
+    ("Y", "X", "Z0", "Z1"),
+    ("Z0", "Y", "Z1", "X"),
+    ("Z0", "Z1", "X", "Y"),
+    ("Y", "Z0", "X", "Z1"),
+    ("X", "Y", "Z0", "Z1"),
+    ("X", "Y", "Z0", "Z1"),
+)
+ATTN_ORDERS = (
+    ("Z0", "X", "Z1", "Y"),
+    ("Y", "Z0", "X", "Z1"),
+    ("X", "Z0", "Y", "Z1"),
+)
+ATTN_CUTS = (128, 256, 256)
+PLAN = (
+    (("begin",), ()),
+    (("w", 1, 1), ()),
+    (("w", 1, 0), ()),
+    (("w", 3, 1), ()),
+    (("w", 3, 0), ()),
+    (("w", 4, 1), ()),
+    (("w", 4, 0), ()),
+    (("w", 2, 1), ()),
+    (("w", 2, 0), ()),
+    (("prep",), ()),
+    (("p", 0), ()),
+    (("p", 1), ()),
+    (("p", 2), ()),
+    (("p", 3), ()),
+    (("p", 4), ()),
+    (("q", 0), ()),
+    (("q", 1), ("f4",)),
+    (("q", 2), ("f1",)),
+    (("q", 3), ("f3",)),
+    (("q", 4), ()),
+    (("w", 5, 1), ()),
+    (("w", 5, 0), ()),
+    (("w", 0, 1), ("f4",)),
+    (("w", 0, 0), ()),
+    (("kf",), ("f2",)),
+    (("close",), ()),
+    (("attn",), ("f1",)),
+    (("tail",), ("f2", "f3", "f5", "f0", "f4", "f1", "f4", "a2", "a1", "g0", "a0", "f2", "f3", "a2", "f5", "f2", "f0", "f3", "a2", "f1", "a1", "g0", "a0", "a2", "g0", "a1", "a0", "f5", "a2", "g0", "a0", "a2", "g0", "a1", "f0", "a0", "f5", "a1", "a0", "a1", "f0")),
+)
+PARTS = len(FFN_CUTS)
+COPIES_FINISH = 4 * len(ORDERS) + 6 * len(ATTN_ORDERS) + 5 + 3 + 4
 
 
 def finish_kernel(*refs):
-    where_ref, h_ref, gain_ref, dm_ref, wo_ref, q_ref, kv_ref, o_ref, lse_ref = refs[:9]
-    wq_ref, wk_ref, wv_ref, cos_ref, sin_ref, a_ref, c_ref = refs[9:16]
-    left_two, long_two, short_two, side_two = refs[16:20]
-    gains_ref = refs[20]
+    where_ref, gain_ref, cos_ref, sin_ref, gains_ref = refs[:5]
+    late_refs, lse_any = refs[5:14], refs[14]
+    a_ref, c_ref, left_two, long_two, short_two, side_two, b_any, f_any, rhs_any = refs[15:24]
     count = 4
-    b_any, f_any, rhs_any = refs[21:24]
     dh_ref, gate_out, up_out, down_out = refs[24:28]
     query_out, key_out, value_out, output_out, gain_out = refs[28:33]
-    room = refs[33:40]
-    dq_ref, dkv_ref, dkv_near, dkv_sum, dkv_far, dkv_low = refs[40:46]
-    b_all, f_all, rhs, left_all, long_all, short_all, side_all = refs[46:53]
-    wholes, rooms = refs[53:56], (refs[56:60], refs[60:64], refs[64:68])
-    attn_wholes, attn_rooms = refs[68:70], (refs[70:74], refs[74:78])
-    attn_alls = refs[78:80]
-    gain_whole, gain_got, gain_side = refs[80:83]
-    load, send, receive = refs[83:]
+    refs = refs[33:]
+
+    def taken(count):
+        nonlocal refs
+        first, refs = refs[:count], refs[count:]
+        return first
+
+    room = taken(7)
+    dq_ref, dkv_ref, dkv_near, dkv_sum, dkv_far, dkv_low = taken(6)
+    late = taken(9)
+    q_ref, kv_ref, o_ref, wo_ref, dm_ref, h_ref, wq_ref, wk_ref, wv_ref = late
+    lse_ref = taken(1)[0]
+    b_all, f_all, rhs, left_all, long_all, short_all, side_all = taken(7)
+    wholes = taken(len(ORDERS))
+    rooms = [taken(4) for _ in ORDERS]
+    attn_wholes = taken(len(ATTN_ORDERS))
+    attn_rooms = [taken(4) for _ in ATTN_ORDERS]
+    attn_alls = taken(len(ATTN_ORDERS))
+    gain_whole, gain_got, gain_side, load, send, receive = refs
     rows = h_ref.shape[1]
     block = gate_out.shape[0]
     place = lax.axis_index("dp")
     head_at = lax.axis_index("head")
     core, across = head_at % 2, head_at // 2
-    links = Links(send, receive)
-    reduces = [halved(links, whole, got, order) for whole, got, order in zip(wholes, rooms, ORDERS)]
-    attn = [halved(links, whole, got, order) for whole, got, order in zip(attn_wholes, attn_rooms, ATTN_ORDERS)]
-
-    local = Local(load)
-    wanted = (1, 2, 3, 4, 5, 0)
+    links, local = Links(send, receive), Local(load)
+    sums = {}
+    for index, (whole, got, order) in enumerate(zip(wholes, rooms, ORDERS)):
+        start, cut = FFN_CUTS[index % PARTS]
+        out = (gate_out, up_out, down_out)[index // PARTS].at[:, start : start + cut]
+        reduce = halved(Halving, links, whole, got, order)
+        reduce.done = functools.partial(out.__setitem__, Ellipsis)
+        sums["f%d" % index] = reduce
+    for index, (whole, got, order) in enumerate(zip(attn_wholes, attn_rooms, ATTN_ORDERS)):
+        reduce = halved(Regather, links, whole, got, order)
+        reduce.share(links, attn_alls[index])
+        sums["a%d" % index] = reduce
+    sums["g0"] = Rows(links, gain_whole, gain_side, gain_got, gain_out)
+    seen = {name: 0 for name in sums}
+    plan = []
+    for step, names in PLAN:
+        folds = []
+        for name in names:
+            folds.append((name, seen[name]))
+            seen[name] += 1
+        plan.append((step, folds))
+
+    def take(folds):
+        for name, which in folds:
+            sums[name].fold(which)
+
+    products = [step for step, _ in plan if step[0] == "w"]
 
     def fetch(turn):
-        return local.move(rhs_any.at[wanted[turn]], rhs.at[turn % 2])
+        _, index, half = products[turn]
+        start, cut = FFN_CUTS[index % PARTS]
+        source = rhs_any.at[2 * (index // PARTS) + half, :, pl.ds(start, cut)]
+        return local.move(source, rhs.at[turn % 2, :, pl.ds(0, cut)])
 
     b_load = local.move(b_any, b_all)
-    coming = fetch(0)
+    coming = {0: fetch(0)}
     f_load = local.move(f_any, f_all)
+    lates = [local.move(source, target) for source, target in zip(late_refs, late)]
+    lates.append(local.move(lse_any, lse_ref))
     two = ((left_two, left_all), (long_two, long_all), (short_two, short_all), (side_two, side_all))
     two_loads = [local.move(source, target.at[:, pl.ds(0, 2 * rows)]) for source, target in two]
     greet((SIBLING, ACROSS, SIDE, BEYOND, FAR_SIDE))
@@ -742,116 +924,104 @@
                 index * block : (index + 1) * block
             ].astype(LOW)
 
-    for turn, which in enumerate(wanted):
-        coming.wait()
-        if turn < 5:
-            coming = fetch(turn + 1)
-        if which == 4:
+    f_ready = []
+
+    def multiply(index, half):
+        turn = products.index(("w", index, half))
+        coming[turn].wait()
+        if turn + 1 < len(products):
+            coming[turn + 1] = fetch(turn + 1)
+        if index >= 2 * PARTS and not f_ready:
             f_load.wait()
-        lay(nn((b_all if which < 4 else f_all)[...], rhs[turn % 2]), wholes[which // 2], which % 2)
-        if which == 1:
-            reduces[0].start(0)
-        if which == 3:
-            reduces[1].start(0)
-        if which == 5:
-            reduces[2].start(0)
+            f_ready.append(True)
+        cut = FFN_CUTS[index % PARTS][1]
+        lay(nn((b_all if index < 2 * PARTS else f_all)[...], rhs[turn % 2, :, :cut]), wholes[index], half)
+        if half == (1 if ORDERS[index][0] == "X" else 0):
+            sums["f%d" % index].start()
 
     cosine, sine = cos_ref[...], sin_ref[...]
-    bias, k_sc, v_sc, kt_sc = room[:4]
     settle = Settle(links, dkv_ref, dkv_near, dkv_sum, dkv_far)
-    fill_bias(where_ref, bias, rows, count)
-    lay_back(kv_ref, k_sc, v_sc, kt_sc, count, rows, False)
-    attend_back(
-        dm_ref[...], wo_ref, q_ref, o_ref, lse_ref, cosine, sine, dq_ref, dkv_ref, room, settle.between
-    )
-    total = settle.finish()
-    for reduce in reduces:
-        reduce.fold(0)
-    grad_keys, grad_values = close_keys(total, cosine, sine, dkv_low)
-
     low_rows, own_at, got_at = pl.ds(0, KV_WIDTH), pl.ds(2 * rows, rows), pl.ds(3 * rows, rows)
     high_rows, everything = pl.ds(KV_WIDTH, KV_WIDTH), slice(None)
-    swaps = []
-    for zero, one, target in (
-        (a_ref, c_ref, left_all),
-        (dq_ref, o_ref, long_all),
-        (dkv_low.at[low_rows], dkv_low.at[high_rows], short_all),
-        (a_ref, a_ref, side_all),
-    ):
-        swaps.append(share_out(local, links, core, zero, one, target, (everything, own_at), (everything, got_at)))
-    hidden = h_ref[...].astype(HIGH).T
-    gain = gain_ref[...].astype(HIGH)
-    gain_part, grad_in = close_rows(hidden, gain, dm_ref[...], dq_ref, grad_keys, grad_values, wq_ref, wk_ref, wv_ref)
-    dh_ref[...] = grad_in.T
-    for copy in two_loads:
-        copy.wait()
-    for keep, swap_copy in swaps:
-        keep.wait()
-        swap_copy.wait_recv()
-    long_part = nt(left_all[...], long_all[...])
-    short_part = nt(side_all[...], short_all[...])
-    product = jnp.concatenate([long_part, short_part], axis=1)
-    start = 0
-    for whole, cut in zip(attn_wholes, ATTN_CUTS):
-        for half in range(2):
-            lay(product[:, start : start + cut], whole, jnp.bitwise_xor(half, across))
-            start += cut
-    for reduce in attn:
-        reduce.start(0)
-
-    summed = gains_ref[...] + jnp.concatenate([gain_part, jnp.zeros((7, gain_part.shape[1]), HIGH)], axis=0)
-    for index in range(8):
-        relative = jnp.bitwise_xor(index, place)
-        gain_whole[relative // 4, relative // 2 % 2, relative % 2, :, :block] = summed[
-            :, index * block : (index + 1) * block
-        ]
-        gain_whole[relative // 4, relative // 2 % 2, relative % 2, :, block:] = jnp.zeros((8, 128 - block), HIGH)
-    gain_y = links.push(gain_whole.at[:, :, 1], gain_side, SIDE)
-    gain_y.start()
-    for reduce in reduces:
-        reduce.fold(1)
-    gain_y.wait_recv()
-    gain_whole[:, :, 0] = gain_whole[:, :, 0] + gain_side[...]
-    gain_z = links.push(gain_whole.at[:, 1, 0], gain_got.at[pl.ds(0, 2)], BEYOND)
-    gain_z.start()
-    attn[0].fold(0)
-    gain_z.wait_recv()
-    gain_whole[:, 0, 0] = gain_whole[:, 0, 0] + gain_got[0:2]
-    gain_f = links.push(gain_whole.at[1, 0, 0], gain_got.at[2], FAR_SIDE)
-    gain_f.start()
-    attn[1].fold(0)
-    for reduce in reduces:
-        reduce.fold(2)
-    gain_f.wait_recv()
-    gain_whole[0, 0, 0] = gain_whole[0, 0, 0] + gain_got[2]
-    gain_x = links.push(gain_whole.at[0, 0, 0], gain_got.at[3], ACROSS)
-    gain_x.start()
-    attn[0].fold(1)
-    attn[1].fold(1)
-    gain_x.wait_recv()
-    gain_got[4] = gain_whole[0, 0, 0] + gain_got[3]
-    gain_c = links.push(gain_got.at[4], gain_got.at[5], SIBLING)
-    gain_c.start()
-    attn[0].fold(2)
-    attn[1].fold(2)
-    gain_c.wait_recv()
-    gain_out[...] = gain_got[4] + gain_got[5]
-    for reduce, out in zip(reduces, (gate_out, up_out, down_out)):
-        out[...] = reduce.fold(3)
-    shared = []
-    for reduce, held in zip(attn, attn_alls):
-        held[0, 0] = reduce.fold(3).astype(LOW)
-        copy = links.push(held.at[0, 0], held.at[0, 1], ACROSS)
-        copy.start()
-        shared.append((copy, held))
-    last = []
-    for copy, held in shared:
-        copy.wait_recv()
-        copy = links.push(held.at[0], held.at[1], SIBLING)
-        copy.start()
-        last.append(copy)
-    for copy in last:
-        copy.wait_recv()
+    passes = {"p": {}, "q": {}}
+    for step, folds in plan:
+        if step[0] in passes:
+            passes[step[0]][step[1]] = folds
+
+    def at_group(which, group):
+        for when, folds in passes[which].items():
+            if folds:
+                pl.when(group == when)(functools.partial(take, folds))
+        if which == "q":
+            settle.between(group)
+
+    for step, folds in plan:
+        if step[0] in passes:
+            continue
+        take(folds)
+        if step[0] == "w":
+            multiply(step[1], step[2])
+        elif step[0] == "prep":
+            for copy in lates:
+                copy.wait()
+            bias, k_sc, v_sc, kt_sc = room[:4]
+            fill_bias(where_ref, bias, rows, count)
+            lay_back(kv_ref, k_sc, v_sc, kt_sc, count, rows, False)
+            attend_back(
+                dm_ref[...],
+                wo_ref,
+                q_ref,
+                o_ref,
+                lse_ref,
+                cosine,
+                sine,
+                dq_ref,
+                dkv_ref,
+                room,
+                functools.partial(at_group, "p"),
+                functools.partial(at_group, "q"),
+            )
+        elif step[0] == "kf":
+            grad_keys, grad_values = close_keys(settle.finish(), cosine, sine, dkv_low)
+            swaps = []
+            for zero, one, target in (
+                (a_ref, c_ref, left_all),
+                (dq_ref, o_ref, long_all),
+                (dkv_low.at[low_rows], dkv_low.at[high_rows], short_all),
+                (a_ref, a_ref, side_all),
+            ):
+                swaps.append(
+                    share_out(local, links, core, zero, one, target, (everything, own_at), (everything, got_at))
+                )
+        elif step[0] == "close":
+            hidden = h_ref[...].astype(HIGH).T
+            gain = gain_ref[0:1].astype(HIGH)
+            gain_part, grad_in = close_rows(
+                hidden, gain, dm_ref[...], dq_ref, grad_keys, grad_values, wq_ref, wk_ref, wv_ref
+            )
+            dh_ref[...] = grad_in.T
+            summed = gains_ref[...] + jnp.concatenate([gain_part, jnp.zeros((7, gain_part.shape[1]), HIGH)], axis=0)
+            for index in range(8):
+                relative = jnp.bitwise_xor(index, place)
+                spot = relative // 4, relative // 2 % 2, relative % 2
+                gain_whole[(*spot, slice(None), slice(0, block))] = summed[:, index * block : (index + 1) * block]
+                gain_whole[(*spot, slice(None), slice(block, 128))] = jnp.zeros((8, 128 - block), HIGH)
+            sums["g0"].start()
+        elif step[0] == "attn":
+            for copy in two_loads:
+                copy.wait()
+            for keep, swap_copy in swaps:
+                keep.wait()
+                swap_copy.wait_recv()
+            long_part = nt(left_all[...], long_all[...])
+            short_part = nt(side_all[...], short_all[...])
+            product = jnp.concatenate([long_part, short_part], axis=1)
+            start = 0
+            for index, (whole, cut) in enumerate(zip(attn_wholes, ATTN_CUTS)):
+                for half in range(2):
+                    lay(product[:, start : start + cut], whole, jnp.bitwise_xor(half, across))
+                    start += cut
+                sums["a%d" % index].start()
     for kind, (long_out, short_out) in enumerate(((query_out, key_out), (output_out, value_out))):
         from_core = jnp.bitwise_xor(kind, core)
         parts = [held[from_core, jnp.bitwise_xor(half, across)] for held in attn_alls for half in range(2)]
@@ -859,6 +1029,12 @@
         long_out[...] = both[:, : long_out.shape[1]]
         short_out[...] = both[:, long_out.shape[1] :]
     links.drain()
+
+
+def emit_kernel(*refs):
+    count = len(refs) // 2
+    for source, target in zip(refs[:count], refs[count:]):
+        target[...] = source[...] if source.shape == target.shape else source[...].T
 
 
 def call(body, outs, specs, scratch, name, spots=0, collective=None):
@@ -919,13 +1095,12 @@
     rows, width = tokens.shape
     hidden = w_gate.shape[1]
     keys = blocks * rows
-    where = jnp.stack([me, lengths[0]])
+    where = lengths
     frequency = 10000.0 ** (-(jnp.arange(HALF, dtype=HIGH) * 2.0 / HD))
     position = (me * rows + jnp.arange(rows, dtype=jnp.int32)).astype(HIGH)
     angles = frequency[:, None] * position[None, :]
     cosine, sine = jnp.cos(angles), jnp.sin(angles)
-    gain_one = attn_gain[None, :]
-    gain_two = ffn_gain[None, :]
+    gain_rows = jnp.stack([attn_gain, ffn_gain])
 
     feature_rows = (width, rows)
     project_outs = [(feature_rows, LOW), (feature_rows, LOW), ((blocks, rows, 2 * KV_WIDTH), LOW)]
@@ -946,21 +1121,22 @@
     ]
 
     def forward_first():
-        outs = project_outs + layer_outs + [((rows, width), HIGH)] + project_outs
+        outs = project_outs + layer_outs + [((rows, width), HIGH)]
         outs += [((blocks - 1, width, hidden), LOW)] * 3
-        copies = 3 * COPIES_SPREAD + 2 * COPIES_SHARE
-        scratch = attend_room + weight_room
-        scratch += [pltpu.SemaphoreType.DMA((3,)), pltpu.SemaphoreType.DMA((3, blocks - 1))]
+        copies = 3 * COPIES_SPREAD + COPIES_SHARE
+        late = (w_key, w_value, w_query, w_output)
+        scratch = attend_room + weight_room + [pltpu.VMEM(v.shape, LOW) for v in late]
+        scratch += [pltpu.SemaphoreType.DMA((7 + 3 * (blocks - 1),))]
         scratch += [pltpu.SemaphoreType.DMA((copies,)), pltpu.SemaphoreType.DMA((copies,))]
         body = functools.partial(forward_first_kernel, blocks)
-        specs = [SMEM] + [VMEM] * 9 + [ANY] * 3
+        specs = [SMEM] + [VMEM] * 4 + [ANY] * 7
         return call(body, outs, specs, scratch, "forward_first", 3, 1)(
-            where, tokens, gain_one, w_query, w_key, w_value, cosine, sine, w_output, gain_two, w_gate, w_up, w_down
+            where, tokens, gain_rows, cosine, sine, *late, w_gate, w_up, w_down
         )
 
     outs = forward_first()
-    a_one, q_one, kv_one, o_one, lse_one, m_one, b_one, g_one, u_one, h_one, a_two, q_two, kv_two = outs[:13]
-    weights = [w_gate, outs[13], w_up, outs[14], w_down, outs[15]]
+    a_one, q_one, kv_one, o_one, lse_one, m_one, b_one, g_one, u_one, h_one = outs[:10]
+    weights = [w_gate, outs[10], w_up, outs[11], w_down, outs[12]]
     attend_outs = [(feature_rows, LOW), ((blocks, 2 * KV_WIDTH, rows), LOW)]
     room = attention_room(blocks, rows, width)
     key_room = [(blocks, 2 * KV_WIDTH, rows), (2, 2 * KV_WIDTH, rows)] + [(2 * KV_WIDTH, rows)] * 3
@@ -978,12 +1154,14 @@
         scratch += [pltpu.VMEM(feature_rows, LOW)] * 3 + [pltpu.VMEM((blocks, rows, hidden), LOW)] * 2
         scratch += [pltpu.VMEM((6, rows, hidden), LOW)] * 2 + [pltpu.VMEM(feature_rows, LOW)]
         scratch += [pltpu.VMEM(shape, LOW) for shape in key_room]
-        scratch += [pltpu.VMEM(v.shape, LOW) for v in (cotangent, w_query, w_key, w_value)]
+        late = (w_key, w_value, w_query, w_output, cotangent)
+        scratch += [pltpu.VMEM(v.shape, LOW) for v in late]
+        scratch += [pltpu.VMEM(shape, LOW) for shape in (feature_rows, feature_rows, (blocks, rows, 2 * KV_WIDTH))]
+        scratch += [pltpu.VMEM((16, rows), HIGH)] * 2
         scratch += weight_room + [pltpu.SemaphoreType.DMA((3, 2)), pltpu.SemaphoreType.DMA((LOCALS_MIDDLE,))]
         scratch += [pltpu.SemaphoreType.DMA((COPIES_MIDDLE,)), pltpu.SemaphoreType.DMA((COPIES_MIDDLE,))]
-        given = [where, h_one, q_two, kv_two, w_output, gain_one, gain_two, cosine, sine]
-        given += [cotangent, w_query, w_key, w_value, g_one, u_one, m_one, a_two, b_one, *weights]
-        specs = [SMEM] + [VMEM] * 8 + [ANY] * 15
+        given = [where, h_one, gain_rows, cosine, sine, *late, g_one, u_one, m_one, b_one, *weights]
+        specs = [SMEM] + [VMEM] * 4 + [ANY] * 15
         return call(functools.partial(middle_kernel, blocks), outs, specs, scratch, "middle", 7, 3)(*given)
 
     block_out, c_one, dm_one, gains, b_all, f_all, rhs_all, *halves_two = middle()
@@ -992,7 +1170,7 @@
         sent = swap(jnp.stack([partial[1], partial[3]]), 1)
         far = swap((partial[2].astype(HIGH) + sent[1].astype(HIGH)).astype(LOW), 2)
         outs = [(feature_rows, HIGH), ((2 * KV_WIDTH, rows), LOW), ((1, width), HIGH)]
-        given = [h, gain_one, grad_middle, grad_query, w_query, w_key, w_value, cosine, sine]
+        given = [h, gain_rows, grad_middle, grad_query, w_query, w_key, w_value, cosine, sine]
         given += [partial[0], sent[0], far]
         return call(close_kernel, outs, [VMEM] * 12, [], "close")(*given)
 
@@ -1015,29 +1193,37 @@
     def finish():
         outs = [(feature_rows, HIGH)] + [((block, hidden), HIGH)] * 3
         outs += [((block, n), HIGH) for n in (HQ * HD, KV_WIDTH, KV_WIDTH, HQ * HD)] + [((8, 128), HIGH)]
-        low_room = [feature_rows] + key_room
-        low_room += [(width, 4 * rows), (width, 4 * rows), (2, 4 * rows, hidden)]
+        late = (q_one, kv_one, o_one, w_output, dm_one, tokens, w_query, w_key, w_value)
+        scratch = room + [pltpu.VMEM(shape, LOW) for shape in [feature_rows] + key_room]
+        scratch += [pltpu.VMEM(v.shape, v.dtype) for v in late] + [pltpu.VMEM(lse_one.shape, HIGH)]
+        low_room = []
+        low_room += [(width, 4 * rows), (width, 4 * rows), (2, 4 * rows, max(n for _, n in FFN_CUTS))]
         low_room += [(width, 4 * rows), (width, 4 * rows), (KV_WIDTH, 4 * rows), (width, 4 * rows)]
-        low_room += [(2, 2, 2, 2, block, hidden)] * 3
-        scratch = room + [pltpu.VMEM(shape, LOW) for shape in low_room]
-        for order in ORDERS:
-            scratch += halving_rooms(block, hidden, order)
+        low_room += [(2, 2, 2, 2, block, FFN_CUTS[i % PARTS][1]) for i in range(len(ORDERS))]
+        scratch += [pltpu.VMEM(shape, LOW) for shape in low_room]
+        for index, order in enumerate(ORDERS):
+            scratch += halving_rooms(block, FFN_CUTS[index % PARTS][1], order)
         scratch += [pltpu.VMEM((2, 2, 2, 2, block, cut), LOW) for cut in ATTN_CUTS]
         for order, cut in zip(ATTN_ORDERS, ATTN_CUTS):
             scratch += halving_rooms(block, cut, order)
         scratch += [pltpu.VMEM((2, 2, block, cut), LOW) for cut in ATTN_CUTS]
         scratch += [pltpu.VMEM(shape, HIGH) for shape in ((2, 2, 2, 8, 128), (8, 8, 128), (2, 2, 8, 128))]
-        scratch += [pltpu.SemaphoreType.DMA((40,)), pltpu.SemaphoreType.DMA((COPIES_FINISH,))]
+        scratch += [pltpu.SemaphoreType.DMA((48,)), pltpu.SemaphoreType.DMA((COPIES_FINISH,))]
         scratch += [pltpu.SemaphoreType.DMA((COPIES_FINISH,))]
-        given = [where, tokens, gain_one, dm_one, w_output, q_one, kv_one, o_one, lse_one]
-        given += [w_query, w_key, w_value, cosine, sine, a_one, c_one, *halves_two, gains]
-        specs = [SMEM] + [VMEM] * 15 + [ANY] * 4 + [VMEM] + [ANY] * 3
+        given = [where, gain_rows, cosine, sine, gains, *late, lse_one, a_one, c_one, *halves_two]
+        specs = [SMEM] + [VMEM] * 4 + [ANY] * 19
         return call(finish_kernel, outs, specs, scratch, "finish", 0, 2)(*given, b_all, f_all, rhs_all)
 
     if places == 8 and blocks == 4:
         outs = finish()
         input_grad, gate_grad, up_grad, down_grad, query_grad, key_grad, value_grad, output_grad, gains = outs
         gains = gains[:2, :block]
+        results = [block_out, input_grad, query_grad, key_grad, value_grad, output_grad, gate_grad, up_grad, down_grad]
+        turned_over = (3, 4, 5)
+        outs = [(v.shape[::-1] if i in turned_over else v.shape, v.dtype) for i, v in enumerate(results)]
+        results = call(emit_kernel, outs, [VMEM] * len(outs), [], "emit")(*results)
+        block_out, input_grad, query_grad, key_grad, value_grad, output_grad, gate_grad, up_grad, down_grad = results
+        key_grad, value_grad, output_grad = key_grad.T, value_grad.T, output_grad.T
     else:
         given = [where, dm_one, w_output, q_one, kv_one, o_one, lse_one, cosine, sine]
         dq_one, part_one = call(attend_back_kernel, attend_outs, [SMEM] + [VMEM] * 8, room, "attend_back")(*given)

time: 291 us -> 237 us (0.81)
  Pallas kernels: 270 us -> 228 us
  local copies, waits for them, and re-layouts: 14 us -> 2.63 us
    pallas_call x1, Pallas kernels: 76.3 us -> 56.7 us  [forward_first(): call(body, outs, specs, scratch, 'forward_first', 3, 1)]
    pallas_call x1, Pallas kernels: 79.2 us -> 66.2 us  [middle(): call(functools.partial(middle_kernel, blocks), outs, specs, scratch, 'mid...]
    pallas_call x1, Pallas kernels: 114 us -> 101 us  [finish(): call(finish_kernel, outs, specs, scratch, 'finish', 0, 2)]
    unnamed x21 -> x0, local copies, waits for them, and re-layouts: 10.2 us -> none
    pallas_call x0 -> x1, Pallas kernels: none -> 4.07 us  [shards(): results = call(emit_kernel, outs, [VMEM] * len(outs), [], 'emit')(*results)]
where the time goes in v5:
time: 237 us; the launch traced here: 234 us
  Pallas kernels  228 us (96%)
  local copies, waits for them, and re-layouts  2.63 us (1%)
    pallas_call x1, Pallas kernels, finish(): call(finish_kernel, outs, specs, scratch, 'finish', 0, 2)  101 us
    pallas_call x1, Pallas kernels, middle(): call(functools.partial(middle_kernel, blocks), outs, specs, scratch, 'mid...  66.2 us
    pallas_call x1, Pallas kernels, forward_first(): call(body, outs, specs, scratch, 'forward_first', 3, 1)  56.7 us

profile of v5, /device:TPU:0, one launch (start us, length us, event | category | flops | bytes accessed | tf_op | source)
XLA Modules:
  0.0 233.8 jit_solution(8577669338483557495)
XLA Ops:
  1.3 0.7 stack.9
  2.0 0.7 stack.10
  2.7 0.6 pad_maximum_fusion.refs_2_.refs_1_
  3.3 0.8 multiply_sine_fusion
  4.1 56.7 %forward_first.1 = (bf16[960,256]{1,0:T(8,128)(2,1)}, bf16[960,256]{1,0:T(8,128)(2,1)}, bf16[4,256,640]{2,1,0:T(8,128)(2,1)}, bf16[960,256]{1,0:T(8,128)(2,1)}, ...) custom-call(s32[1]{0:T(128)S(6)} %copy.23.refs_0_, ...), custom_call_target="tpu_custom_call" | custom-call | tf_op jit(solution)/shard_map/forward_first/pallas_call | solution.py:1133
  60.8 66.2 %middle.1 = (bf16[960,256]{1,0:T(8,128)(2,1)}, bf16[960,256]{1,0:T(8,128)(2,1)}, f32[256,960]{1,0:T(8,128)}, f32[8,960]{1,0:T(8,128)}, bf16[960,1024]{1,0:T(8,12...) custom-call(s32[1]{0:T(128)S(6)} %copy.23.refs_0_, ...), custom_call_target="tpu_custom_call" | custom-call | tf_op jit(solution)/shard_map/middle/pallas_call | solution.py:1165
  127.0 101.4 %finish.1 = (f32[960,256]{1,0:T(8,128)}, f32[120,640]{1,0:T(8,128)}, f32[120,640]{1,0:T(8,128)}, f32[120,640]{1,0:T(8,128)}, f32[120,960]{1,0:T(8,128)}, /*index...) custom-call(s32[1]{0:T(128)S(6)} %copy.23.refs_0_, ...), custom_call_target="tpu_custom_call" | custom-call | tf_op jit(solution)/shard_map/finish/pallas_call | solution.py:1215
  228.3 4.1 %emit.1 = (bf16[960,256]{1,0:T(8,128)(2,1)}, f32[960,256]{1,0:T(8,128)}, f32[120,960]{1,0:T(8,128)}, f32[320,120]{1,0:T(8,128)}, f32[320,120]{1,0:T(8,128)}, /*i...) custom-call(bf16[960,256]{1,0:T(8,128)(2,1)} %get-tuple-element.61.refs_0_, ...), custom_call_target="tpu_custom_call" | custom-call | tf_op jit(solution)/shard_map/emit/pallas_call | solution.py:1224
  232.4 1.3 slice_bitcast_fusion
  (2 shorter events, 0.0 us)

commit v6 on v5

--- a/solution.py
+++ b/solution.py
@@ -87,15 +87,21 @@
         bias[step * rows : (step + 1) * rows] = jnp.where(allowed, 0.0, BLOCKED)
 
 
-def weights_in(sources, holders, sems, order):
-    copies = {}
-    for step in range(2):
-        for which in order:
-            holder = holders[which]
-            target = holder.at[0] if step == 0 else holder.at[pl.ds(1, holder.shape[0] - 1)]
-            copies[step, which] = pltpu.make_async_copy(sources[2 * which + step], target, sems.at[which, step])
-            copies[step, which].start()
-    return copies
+def side_by_side(ref, group):
+    first = group * PER_GROUP
+    heads = [ref[pl.ds(pl.multiple_of((first + i) * HD, HD), HD), :] for i in range(PER_GROUP)]
+    return jnp.concatenate(heads, axis=1)
+
+
+def one_below_other(ref, group, value):
+    rows = value.shape[1] // PER_GROUP
+    for member in range(PER_GROUP):
+        at = pl.ds(pl.multiple_of((group * PER_GROUP + member) * HD, HD), HD)
+        ref[at, :] = value[:, member * rows : (member + 1) * rows].astype(ref.dtype)
+
+
+def scored(keys, queries, bias):
+    return nn(keys, queries) + jnp.concatenate([bias] * PER_GROUP, axis=1)
 
 
 def attend(bias, k_sc, vt_sc, q_ref, o_ref, lse_ref, event):
@@ -103,16 +109,12 @@
         keys = k_sc[group]
         values = vt_sc[pl.ds(pl.multiple_of(group * HD, HD), HD), :]
         event(group)
-        for member in range(PER_GROUP):
-            head = group * PER_GROUP + member
-            at = pl.ds(pl.multiple_of(head * HD, HD), HD)
-            scores = nn(keys, q_ref[at, :]) + bias[...]
-            top = jnp.max(scores, axis=0, keepdims=True)
-            exponent = jnp.exp(scores - top)
-            total = jnp.sum(exponent, axis=0, keepdims=True)
-            attended = nn(values, exponent.astype(LOW)) * (1.0 / total)
-            o_ref[at, :] = attended.astype(LOW)
-            lse_ref[pl.ds(head, 1), :] = top + jnp.log(total)
+        scores = scored(keys, side_by_side(q_ref, group), bias[...])
+        top = jnp.max(scores, axis=0, keepdims=True)
+        exponent = jnp.exp(scores - top)
+        total = jnp.sum(exponent, axis=0, keepdims=True)
+        one_below_other(o_ref, group, nn(values, exponent.astype(LOW)) * (1.0 / total))
+        lse_ref[pl.ds(group, 1), :] = top + jnp.log(total)
         return carry
 
     lax.fori_loop(0, KVH, group_body, 0)
@@ -122,15 +124,12 @@
     def group_body(group, carry):
         keys = k_sc[group, :half]
         values = vt_sc[pl.ds(pl.multiple_of(group * HD, HD), HD), :half]
-        for member in range(PER_GROUP):
-            head = group * PER_GROUP + member
-            at = pl.ds(pl.multiple_of(head * HD, HD), HD)
-            scores = nn(keys, q_ref[at, :]) + bias[:half]
-            top = jnp.max(scores, axis=0, keepdims=True)
-            exponent = jnp.exp(scores - top)
-            top_ref[pl.ds(head, 1), :] = top
-            total_ref[pl.ds(head, 1), :] = jnp.sum(exponent, axis=0, keepdims=True)
-            part_ref[at, :] = nn(values, exponent.astype(LOW))
+        scores = scored(keys, side_by_side(q_ref, group), bias[:half])
+        top = jnp.max(scores, axis=0, keepdims=True)
+        exponent = jnp.exp(scores - top)
+        top_ref[pl.ds(group, 1), :] = top
+        total_ref[pl.ds(group, 1), :] = jnp.sum(exponent, axis=0, keepdims=True)
+        one_below_other(part_ref, group, nn(values, exponent.astype(LOW)))
         return carry
 
     lax.fori_loop(0, KVH, group_body, 0)
@@ -140,18 +139,15 @@
     def group_body(group, carry):
         keys = k_sc[group, half:]
         values = vt_sc[pl.ds(pl.multiple_of(group * HD, HD), HD), half:]
-        for member in range(PER_GROUP):
-            head = group * PER_GROUP + member
-            at = pl.ds(pl.multiple_of(head * HD, HD), HD)
-            scores = nn(keys, q_ref[at, :]) + bias[half:]
-            before = top_ref[pl.ds(head, 1), :]
-            top = jnp.maximum(before, jnp.max(scores, axis=0, keepdims=True))
-            exponent = jnp.exp(scores - top)
-            rescale = jnp.exp(before - top)
-            total = total_ref[pl.ds(head, 1), :] * rescale + jnp.sum(exponent, axis=0, keepdims=True)
-            attended = (part_ref[at, :] * rescale + nn(values, exponent.astype(LOW))) * (1.0 / total)
-            o_ref[at, :] = attended.astype(LOW)
-            lse_ref[pl.ds(head, 1), :] = top + jnp.log(total)
+        scores = scored(keys, side_by_side(q_ref, group), bias[half:])
+        before = top_ref[pl.ds(group, 1), :]
+        top = jnp.maximum(before, jnp.max(scores, axis=0, keepdims=True))
+        exponent = jnp.exp(scores - top)
+        rescale = jnp.exp(before - top)
+        total = total_ref[pl.ds(group, 1), :] * rescale + jnp.sum(exponent, axis=0, keepdims=True)
+        attended = side_by_side(part_ref, group) * rescale + nn(values, exponent.astype(LOW))
+        one_below_other(o_ref, group, attended * (1.0 / total))
+        lse_ref[pl.ds(group, 1), :] = top + jnp.log(total)
         return carry
 
     lax.fori_loop(0, KVH, group_body, 0)
@@ -173,13 +169,16 @@
     return middle, normed.astype(LOW)
 
 
-def hidden_part(normed, wg, wu, wd, g_ref, u_ref, step):
+def active_part(normed, wg, wu, g_ref, u_ref, step):
     gate = nn(normed, wg[step])
     up = nn(normed, wu[step])
     g_ref[step] = gate.astype(LOW)
     u_ref[step] = up.astype(LOW)
-    active = (gate * sigmoid(gate) * up).astype(LOW)
-    return nt(active, wd[step])
+    return (gate * sigmoid(gate) * up).astype(LOW)
+
+
+def hidden_part(normed, wg, wu, wd, g_ref, u_ref, step):
+    return nt(active_part(normed, wg, wu, g_ref, u_ref, step), wd[step])
 
 
 def partner(axis, distance):
@@ -256,26 +255,25 @@
 
 
 class Spread:
-    def __init__(self, links, own, all_ref):
-        rows = own.shape[0]
-        quarter = rows // 4
+    def __init__(self, links, own, all_ref, start, count):
+        quarter = count // 4
         cut = quarter // 32 * 16
         place = lax.axis_index("dp") % 4
 
-        def part(ref, which, start=0, size=quarter):
-            first = jnp.bitwise_xor(place, which) * quarter + start
-            return ref.at[pl.ds(pl.multiple_of(first, 16), size)]
-
-        far, diag = all_ref.at[2], all_ref.at[3]
+        def rows(which, first=0, size=quarter):
+            at = start + jnp.bitwise_xor(place, which) * quarter + first
+            return pl.ds(pl.multiple_of(at, 16), size)
 
         def move(which, to, *piece):
-            return links.push(part(far, which, *piece), part(far, which, *piece), to)
+            ref = all_ref.at[2, rows(which, *piece)]
+            return links.push(ref, ref, to)
 
         def aside(which):
-            return links.push(part(far, which), part(diag, which), SIBLING)
-
-        self.near = links.push(own, all_ref.at[1], SIBLING)
-        self.cross = links.push(part(own, 0), part(far, 0), ACROSS)
+            return links.push(all_ref.at[2, rows(which)], all_ref.at[3, rows(which)], SIBLING)
+
+        span = pl.ds(start, count)
+        self.near = links.push(own.at[span], all_ref.at[1, span], SIBLING)
+        self.cross = links.push(own.at[rows(0)], all_ref.at[2, rows(0)], ACROSS)
         self.side, self.beyond = move(0, SIDE), move(0, BEYOND)
         self.side_half = move(2, SIDE, cut, quarter - cut)
         self.beyond_half = move(1, BEYOND, 0, cut)
@@ -309,88 +307,97 @@
 COPIES_SPREAD = 10
 
 
-def forward_first_kernel(blocks, *refs):
-    where_ref, h_ref, gain_ref, cos_ref, sin_ref = refs[:5]
-    late_refs, owns = refs[5:9], refs[9:12]
-    a_ref, q_ref, kv_ref, o_ref, lse_ref, m_ref, b_ref, g_ref, u_ref, out_ref = refs[12:22]
-    kept = refs[22:25]
-    bias, k_sc, vt_sc, wg, wu, wd = refs[25:31]
-    late, (load, send, receive) = refs[31:35], refs[35:]
-    wk_ref, wv_ref, wq_ref, wo_ref = late
-    rows = h_ref.shape[1]
-    links, local = Links(send, receive), Local(load)
-    held = (wg, wu, wd)
-    lates = [local.move(source, target) for source, target in zip(late_refs, late)]
+def first_forward(where_ref, h_ref, gain_ref, cos_ref, sin_ref, late, lates, owns, parts, results, attn, held, links, local):
+    a_ref, q_ref, kv_ref, o_ref, lse_ref, m_ref, b_ref, g_ref, u_ref = parts
+    bias, k_sc, vt_sc = attn
+    wk_ref, wv_ref, wq_ref, wo_ref, _ = late
+    wg, wu, wd = held
+    blocks, rows = wg.shape[0], h_ref.shape[1]
     loads = [local.move(own, all_ref.at[0], False) for own, all_ref in zip(owns, held)]
-    gate_way, up_way, down_way = spreads = [Spread(links, own, all_ref) for own, all_ref in zip(owns, held)]
+    whole = owns[0].shape[0]
+    middle_row = (whole // 128 + 1) * 64
+    cuts = ((0, middle_row), (middle_row, whole - middle_row))
+    spreads = [[Spread(links, own, all_ref, *cut) for cut in cuts] for own, all_ref in zip(owns, held)]
+    (g1, g2), (u1, u2), (d1, d2) = spreads
     share = Share(links, kv_ref)
     greet((SIBLING, ACROSS, SIDE, BEYOND))
-    gate_way.cross.start()
-    up_way.cross.start()
-    for spread, copy in zip(spreads, loads):
-        spread.near.start()
+    for piece in (g1, g2):
+        piece.cross.start()
+    for pair, copy in zip(spreads, loads):
+        for piece in pair:
+            piece.near.start()
         copy.start()
     hidden = h_ref[...].astype(HIGH).T
 
     def queue():
         share.start()
-        down_way.cross.start()
+        for piece in (u1, u2, d1, d2):
+            piece.cross.start()
         lates[2].wait()
 
     lates[0].wait()
     lates[1].wait()
     gain_one = gain_ref[0:1].astype(HIGH)
     project(hidden, gain_one, wq_ref, wk_ref, wv_ref, cos_ref[...], sin_ref[...], a_ref, q_ref, kv_ref.at[0], queue)
-    gate_way.first()
+    g1.first()
+    g2.first()
     fill_bias(where_ref, bias, rows, blocks)
-    up_way.first()
-    gate_way.second()
+    g1.second()
+    g2.second()
     share.pass_on()
+    g1.third()
     share.finish()
     lay_keys(kv_ref, k_sc, vt_sc, range(blocks), rows)
+    events = ((g2.third, u1.first), (), (u2.first,), (u1.second,), (d1.first, u2.second))
 
     def event(group):
-        pl.when(group == 1)(up_way.second)
-        pl.when(group == 2)(gate_way.third)
-        pl.when(group == 3)(down_way.first)
+        for when, actions in enumerate(events):
+
+            @pl.when(group == when)
+            def _():
+                for action in actions:
+                    action()
 
     attend(bias, k_sc, vt_sc, q_ref, o_ref, lse_ref, event)
+    d2.first()
+    u1.third()
     lates[3].wait()
     middle, normed = after_attention(hidden, o_ref, wo_ref, gain_ref[1:2].astype(HIGH), m_ref, b_ref)
-    saves = []
-
-    def keep(step):
-        for which in range(3):
-            saves.append(local.move(held[which].at[step], kept[which].at[step - 1]))
-
+    early = [local.move(source, target) for source, target in zip(parts[:7], results[:7])]
+    u2.third()
     for copy in loads:
         copy.wait()
-    total = middle + hidden_part(normed, wg, wu, wd, g_ref, u_ref, 0)
-    up_way.third()
-    down_way.second()
-    for spread in spreads:
-        spread.near.wait_recv()
-    keep(1)
-    total = total + hidden_part(normed, wg, wu, wd, g_ref, u_ref, 1)
-    down_way.third()
-    keep(2)
-    total = total + hidden_part(normed, wg, wu, wd, g_ref, u_ref, 2)
-    for spread in spreads:
-        spread.last()
-    keep(3)
-    total = total + hidden_part(normed, wg, wu, wd, g_ref, u_ref, 3)
-    out_ref[...] = total
-    for copy in saves:
+    active = [active_part(normed, wg, wu, g_ref, u_ref, 0)]
+    d1.second()
+    for pair in spreads:
+        for piece in pair:
+            piece.near.wait_recv()
+    active.append(active_part(normed, wg, wu, g_ref, u_ref, 1))
+    d2.second()
+    d1.third()
+    for step in range(2, 4):
+        active.append(active_part(normed, wg, wu, g_ref, u_ref, step))
+        if step == 2:
+            for piece in (g1, g2, u1, u2):
+                piece.last()
+    early += [local.move(source, target) for source, target in zip(parts[7:], results[7:])]
+    total = middle
+    for step in range(blocks):
+        if step == 2:
+            d2.third()
+        if step == 3:
+            d1.last()
+            d2.last()
+        total = total + nt(active[step], wd[step])
+    for copy in early:
         copy.wait()
-    links.drain()
-
-
-def ffn_back(grad, copies, g_ref, u_ref, m_ref, gain, wg, wu, wd, mine_ref, theirs_ref):
+    return total
+
+
+def ffn_back(grad, g_ref, u_ref, m_ref, gain, wg, wu, wd, mine_ref, theirs_ref):
     low_grad = grad.astype(LOW)
     grad_normed = jnp.zeros(m_ref.shape, HIGH)
     for step in range(wg.shape[0]):
-        if copies and step < 2:
-            copies[step, 2].wait()
         grad_active = nn(low_grad, wd[step])
         gate = g_ref[step].astype(HIGH)
         up = u_ref[step].astype(HIGH)
@@ -402,9 +409,6 @@
         kept[step // 2] = grad_gate
         kept[2 + step // 2] = grad_up
         kept[4 + step // 2] = (silu * up).astype(LOW)
-        if copies and step < 2:
-            copies[step, 0].wait()
-            copies[step, 1].wait()
         grad_normed = grad_normed + nt(grad_gate, wg[step]) + nt(grad_up, wu[step])
     return norm_back(m_ref[...], gain, grad_normed, grad)
 
@@ -428,7 +432,10 @@
     for head in range(HQ):
         at = slice(head * HD, (head + 1) * HD)
         product = do_sc[at].astype(HIGH) * o_ref[at].astype(HIGH)
-        delta[head : head + 1] = jnp.sum(product, axis=0, keepdims=True)
+        group, member = divmod(head, PER_GROUP)
+        spot = slice(member * rows, (member + 1) * rows)
+        delta[group : group + 1, spot] = jnp.sum(product, axis=0, keepdims=True)
+    cosines, sines = (jnp.concatenate([table] * PER_GROUP, axis=1) for table in (cosine, sine))
 
     def one_pass(start, last, event):
         cut = slice(start, start + half)
@@ -440,25 +447,19 @@
             at = pl.ds(pl.multiple_of(group * HD, HD), HD)
             after = pl.ds(pl.multiple_of(KV_WIDTH + group * HD, HD), HD)
             keys_t = kt_sc[at, cut]
-            grad_keys = jnp.zeros((HD, half), HIGH)
-            grad_values = jnp.zeros((HD, half), HIGH)
-            for member in range(PER_GROUP):
-                head = group * PER_GROUP + member
-                head_at = pl.ds(pl.multiple_of(head * HD, HD), HD)
-                query = q_ref[head_at, :]
-                grad_out = do_sc[head_at, :]
-                scores = nn(group_keys, query) + bias[cut]
-                prob = jnp.exp(scores - lse_ref[pl.ds(head, 1), :])
-                grad_prob = nn(values, grad_out)
-                grad_score = (prob * (grad_prob - delta[pl.ds(head, 1), :])).astype(LOW)
-                grad_query = nn(keys_t, grad_score)
-                if last:
-                    grad_query = grad_query + dq_sc[head_at, :]
-                    dq_ref[head_at, :] = turned(grad_query, cosine, sine, -1.0, SCALE).astype(LOW)
-                else:
-                    dq_sc[head_at, :] = grad_query
-                grad_keys = grad_keys + nt(query, grad_score)
-                grad_values = grad_values + nt(grad_out, prob.astype(LOW))
+            query, grad_out = side_by_side(q_ref, group), side_by_side(do_sc, group)
+            scores = scored(group_keys, query, bias[cut])
+            prob = jnp.exp(scores - lse_ref[pl.ds(group, 1), :])
+            grad_prob = nn(values, grad_out)
+            grad_score = (prob * (grad_prob - delta[pl.ds(group, 1), :])).astype(LOW)
+            grad_query = nn(keys_t, grad_score)
+            if last:
+                grad_query = grad_query + side_by_side(dq_sc, group)
+                one_below_other(dq_ref, group, turned(grad_query, cosines, sines, -1.0, SCALE))
+            else:
+                one_below_other(dq_sc, group, grad_query)
+            grad_keys = nt(query, grad_score)
+            grad_values = nt(grad_out, prob.astype(LOW))
             for step in range(blocks // 2):
                 part = slice(step * rows, (step + 1) * rows)
                 dkv_ref[start // rows + step, at, :] = grad_keys[:, part].astype(LOW)
@@ -490,7 +491,6 @@
 
     def finish(self):
         dkv_ref, near_ref, _, far_ref = self.refs
-        self.near.start()
         self.near.wait_recv()
         self.far.wait_recv()
         return dkv_ref[0].astype(HIGH) + near_ref[0].astype(HIGH) + far_ref[...].astype(HIGH)
@@ -504,7 +504,7 @@
         pltpu.VMEM((KVH, keys, HD), LOW),
         pltpu.VMEM((KV_WIDTH, keys), LOW),
         pltpu.VMEM((width, rows), LOW),
-        pltpu.VMEM((16, rows), HIGH),
+        pltpu.VMEM((8, PER_GROUP * rows), HIGH),
         pltpu.VMEM((width, rows), HIGH),
     ]
 
@@ -535,32 +535,49 @@
     return keep, send
 
 
-COPIES_MIDDLE = 20
-LOCALS_MIDDLE = 24
-
-
-def middle_kernel(blocks, *refs):
-    where_ref, h_ref, gain_ref, cos_ref, sin_ref = refs[:5]
-    late_refs = refs[5:10]
-    g_any, u_any, m_any, b_any = refs[10:14]
-    sources = refs[14:20]
-    out_ref, c_ref, dm_ref, gains_ref = refs[20:24]
-    b_all, f_all, rhs_all, left_two, long_two, short_two, side_two = refs[24:31]
-    room = refs[31:38]
+COPIES_MIDDLE = 6 * COPIES_SPREAD + COPIES_SHARE + 20
+LOCALS_MIDDLE = 40
+
+
+def layers_kernel(blocks, *refs):
+    where_ref, tokens_ref, gain_ref, cos_ref, sin_ref = refs[:5]
+    late_refs, owns = refs[5:10], refs[10:13]
+    out_ref, c_ref, dm_ref, gains_ref = refs[13:17]
+    results = refs[17:26]
+    m_any, b_any, g_any, u_any = results[5:]
+    b_all, f_all, rhs_all, left_two, long_two, short_two, side_two = refs[26:33]
+    room = refs[33:40]
     bias, k_sc, v_sc, kt_sc = room[:4]
     part_sc = room[6]
-    vt_sc, o_sc, lse_sc, m_sc, b_sc, f_sc, c_sc, g_sc, u_sc = refs[38:47]
-    mine, theirs, dq_sc, dkv_sc, dkv_near, dkv_sum, dkv_far, dkv_low = refs[47:55]
-    late = refs[55:60]
-    a_sc, q_ref, kv_ref, top_sc, total_sc = refs[60:65]
+    vt_sc, o_sc, lse_sc, m_sc, b_sc, f_sc, c_sc, g_sc, u_sc = refs[40:49]
+    mine, theirs, dq_sc, dkv_sc, dkv_near, dkv_sum, dkv_far, dkv_low = refs[49:57]
+    late = refs[57:62]
+    a_sc, q_ref, kv_first, kv_ref, top_sc, total_sc, h_ref = refs[62:69]
     wk, wv, wq, wo_ref, cot = late
-    wg, wu, wd, sems, load, send, receive = refs[65:]
+    wg, wu, wd, load, send, receive = refs[69:]
     rows = h_ref.shape[0]
     core = lax.axis_index("head") % 2
     local = Local(load)
     links = Links(send, receive)
     lates = [local.move(source, target) for source, target in zip(late_refs, late)]
-    copies = weights_in(sources, (wg, wu, wd), sems, (0, 1, 2))
+    parts = (a_sc, q_ref, kv_first, o_sc, lse_sc, m_sc, b_sc, g_sc, u_sc)
+    h_ref[...] = first_forward(
+        where_ref,
+        tokens_ref,
+        gain_ref,
+        cos_ref,
+        sin_ref,
+        late,
+        lates,
+        owns,
+        parts,
+        results,
+        (bias, k_sc, vt_sc),
+        (wg, wu, wd),
+        links,
+        local,
+    )
+    waited = list(links.flying)
     share = Share(links, kv_ref)
     settle = Settle(links, dkv_sc, dkv_near, dkv_sum, dkv_far)
     spans = [pl.ds(i * rows, rows) for i in range(4)]
@@ -572,22 +589,14 @@
         copy.start()
         return keep, copy
 
-    greet((SIBLING, ACROSS))
     both.layer = 2
     posted = [both(b_any, b_all, (everything,))]
     both.layer = 0
     cosine, sine = cos_ref[...], sin_ref[...]
     half = blocks * rows // 2
 
-    def ready():
-        share.start()
-        lates[2].wait()
-
-    lates[0].wait()
-    lates[1].wait()
     gain_one = gain_ref[0:1].astype(HIGH)
-    project(h_ref[...], gain_one, wq, wk, wv, cosine, sine, a_sc, q_ref, kv_ref.at[0], ready)
-    fill_bias(where_ref, bias, rows, blocks)
+    project(h_ref[...], gain_one, wq, wk, wv, cosine, sine, a_sc, q_ref, kv_ref.at[0], share.start)
     share.near.wait_recv()
     lay_keys(kv_ref, k_sc, vt_sc, range(blocks // 2), rows)
     attend_first(bias, k_sc, vt_sc, q_ref, top_sc, total_sc, part_sc, half)
@@ -595,13 +604,9 @@
     share.forth.wait_recv()
     lay_keys(kv_ref, k_sc, vt_sc, range(blocks // 2, blocks), rows)
     attend_rest(bias, k_sc, vt_sc, q_ref, top_sc, total_sc, part_sc, half, o_sc, lse_sc)
-    lates[3].wait()
     total, normed = after_attention(h_ref[...], o_sc, wo_ref, gain_ref[1:2].astype(HIGH), m_sc, b_sc)
     posted.append(both(b_sc, b_all, (everything,)))
     for step in range(blocks):
-        if step < 2:
-            for which in range(3):
-                copies[step, which].wait()
         total = total + hidden_part(normed, wg, wu, wd, g_sc, u_sc, step)
     out_ref[...] = total.T.astype(LOW)
     lay_back(kv_ref, k_sc, v_sc, kt_sc, blocks, rows, True)
@@ -612,7 +617,7 @@
     f_sc[...] = grad.T.astype(LOW)
     first_f = both(f_sc, f_all, (everything,))
     gain_two = gain_ref[1:2].astype(HIGH)
-    gain_part, grad_middle = ffn_back(grad, None, g_sc, u_sc, m_sc, gain_two, wg, wu, wd, mine, theirs)
+    gain_part, grad_middle = ffn_back(grad, g_sc, u_sc, m_sc, gain_two, wg, wu, wd, mine, theirs)
     first_loads = [local.move(source, target) for source, target in ((g_any, g_sc), (u_any, u_sc), (m_any, m_sc))]
     keep_mine = local.move(mine, rhs_all.at[:, spans[0]])
     send_theirs = links.push(theirs, rhs_all.at[:, spans[1]], SIBLING)
@@ -623,6 +628,8 @@
     attend_back(
         grad_middle, wo_ref, q_ref, o_sc, lse_sc, cosine, sine, dq_sc, dkv_sc, room, lambda group: None, settle.between
     )
+    settle.near.start()
+    from_query = nn(wq[...], dq_sc[...]).T
     grad_keys, grad_values = close_keys(settle.finish(), cosine, sine, dkv_low)
     low_rows, high_rows = pl.ds(0, KV_WIDTH), pl.ds(KV_WIDTH, KV_WIDTH)
     for zero, one, target in (
@@ -634,7 +641,7 @@
         posted.append(
             share_out(local, links, core, zero, one, target, (everything, spans[0]), (everything, spans[1]))
         )
-    gain_part, grad = close_rows(h_ref[...], gain_one, grad_middle, dq_sc, grad_keys, grad_values, wq, wk, wv)
+    gain_part, grad = close_rows(h_ref[...], gain_one, grad_middle, from_query, grad_keys, grad_values, wk, wv)
     gains_ref[0:1] = gain_part
 
     first_f[0].wait()
@@ -646,7 +653,7 @@
     f_sc[...] = grad.T.astype(LOW)
     both.layer = 2
     posted.append(both(f_sc, f_all, (everything,)))
-    gain_part, grad_middle = ffn_back(grad, None, g_sc, u_sc, m_sc, gain_two, wg, wu, wd, mine, theirs)
+    gain_part, grad_middle = ffn_back(grad, g_sc, u_sc, m_sc, gain_two, wg, wu, wd, mine, theirs)
     keep_last = local.move(mine, rhs_all.at[:, spans[2]])
     send_last = links.push(theirs, rhs_all.at[:, spans[3]], SIBLING)
     send_last.start()
@@ -660,7 +667,7 @@
     send_theirs.wait_recv()
     keep_last.wait()
     send_last.wait()
-    for copy in (settle.aside, settle.near, settle.far, share.near, share.far, share.forth):
+    for copy in (settle.aside, settle.near, settle.far, share.near, share.far, share.forth, *waited):
         copy.wait_send()
 
 
@@ -683,9 +690,8 @@
     return turned_keys.T.astype(LOW), total[KV_WIDTH:].T.astype(LOW)
 
 
-def close_rows(hidden, gain, grad_middle, dq_ref, grad_keys, grad_values, wq_ref, wk_ref, wv_ref):
-    grad_normed = nn(wq_ref[...], dq_ref[...]).T
-    grad_normed = grad_normed + nn(grad_keys, wk_ref[...]) + nn(grad_values, wv_ref[...])
+def close_rows(hidden, gain, grad_middle, from_query, grad_keys, grad_values, wk_ref, wv_ref):
+    grad_normed = from_query + nn(grad_keys, wk_ref[...]) + nn(grad_values, wv_ref[...])
     return norm_back(hidden, gain, grad_normed, grad_middle)
 
 
@@ -696,7 +702,8 @@
     grad_keys, grad_values = close_keys(total, cos_ref[...], sin_ref[...], dkv_ref)
     hidden = h_ref[...].astype(HIGH).T
     gain = gain_ref[0:1].astype(HIGH)
-    gain_part, grad_in = close_rows(hidden, gain, dm_ref[...], dq_ref, grad_keys, grad_values, wq_ref, wk_ref, wv_ref)
+    from_query = nn(wq_ref[...], dq_ref[...]).T
+    gain_part, grad_in = close_rows(hidden, gain, dm_ref[...], from_query, grad_keys, grad_values, wk_ref, wv_ref)
     gain_part_ref[...] = gain_part
     dh_ref[...] = grad_in.T
 
@@ -982,6 +989,8 @@
                 functools.partial(at_group, "q"),
             )
         elif step[0] == "kf":
+            settle.near.start()
+            from_query = nn(wq_ref[...], dq_ref[...]).T
             grad_keys, grad_values = close_keys(settle.finish(), cosine, sine, dkv_low)
             swaps = []
             for zero, one, target in (
@@ -997,7 +1006,7 @@
             hidden = h_ref[...].astype(HIGH).T
             gain = gain_ref[0:1].astype(HIGH)
             gain_part, grad_in = close_rows(
-                hidden, gain, dm_ref[...], dq_ref, grad_keys, grad_values, wq_ref, wk_ref, wv_ref
+                hidden, gain, dm_ref[...], from_query, grad_keys, grad_values, wk_ref, wv_ref
             )
             dh_ref[...] = grad_in.T
             summed = gains_ref[...] + jnp.concatenate([gain_part, jnp.zeros((7, gain_part.shape[1]), HIGH)], axis=0)
@@ -1031,7 +1040,10 @@
     links.drain()
 
 
-def emit_kernel(*refs):
+def emit_kernel(gains, *refs):
+    refs, rows = refs[:-2], refs[-2:]
+    for index, row in enumerate(rows):
+        row[...] = gains[index : index + 1, : row.shape[1]]
     count = len(refs) // 2
     for source, target in zip(refs[:count], refs[count:]):
         target[...] = source[...] if source.shape == target.shape else source[...].T
@@ -1106,65 +1118,44 @@
     project_outs = [(feature_rows, LOW), (feature_rows, LOW), ((blocks, rows, 2 * KV_WIDTH), LOW)]
     tokens, cotangent, w_key, w_value, w_down = (v.T for v in (tokens, cotangent, w_key, w_value, w_down))
     weight_room = [pltpu.VMEM((blocks, width, hidden), LOW)] * 3
-    attend_room = [
-        pltpu.VMEM((keys, rows), HIGH),
-        pltpu.VMEM((KVH, keys, HD), LOW),
-        pltpu.VMEM((KV_WIDTH, keys), LOW),
-    ]
     layer_outs = [
         (feature_rows, LOW),
-        ((16, rows), HIGH),
+        ((8, PER_GROUP * rows), HIGH),
         ((rows, width), HIGH),
         (feature_rows, LOW),
         ((blocks, rows, hidden), LOW),
         ((blocks, rows, hidden), LOW),
     ]
 
-    def forward_first():
-        outs = project_outs + layer_outs + [((rows, width), HIGH)]
-        outs += [((blocks - 1, width, hidden), LOW)] * 3
-        copies = 3 * COPIES_SPREAD + COPIES_SHARE
-        late = (w_key, w_value, w_query, w_output)
-        scratch = attend_room + weight_room + [pltpu.VMEM(v.shape, LOW) for v in late]
-        scratch += [pltpu.SemaphoreType.DMA((7 + 3 * (blocks - 1),))]
-        scratch += [pltpu.SemaphoreType.DMA((copies,)), pltpu.SemaphoreType.DMA((copies,))]
-        body = functools.partial(forward_first_kernel, blocks)
-        specs = [SMEM] + [VMEM] * 4 + [ANY] * 7
-        return call(body, outs, specs, scratch, "forward_first", 3, 1)(
-            where, tokens, gain_rows, cosine, sine, *late, w_gate, w_up, w_down
-        )
-
-    outs = forward_first()
-    a_one, q_one, kv_one, o_one, lse_one, m_one, b_one, g_one, u_one, h_one = outs[:10]
-    weights = [w_gate, outs[10], w_up, outs[11], w_down, outs[12]]
     attend_outs = [(feature_rows, LOW), ((blocks, 2 * KV_WIDTH, rows), LOW)]
     room = attention_room(blocks, rows, width)
     key_room = [(blocks, 2 * KV_WIDTH, rows), (2, 2 * KV_WIDTH, rows)] + [(2 * KV_WIDTH, rows)] * 3
 
-    def middle():
+    def layers():
         outs = [(feature_rows, LOW), (feature_rows, LOW), ((rows, width), HIGH), ((8, width), HIGH)]
+        outs += project_outs + layer_outs
         outs += [((width, 4 * rows), LOW)] * 2 + [((6, 4 * rows, hidden), LOW)]
         outs += [((n, 2 * rows), LOW) for n in (width, HQ * HD, KV_WIDTH, width)]
-        scratch = room + [
-            pltpu.VMEM((KV_WIDTH, keys), LOW),
-            pltpu.VMEM(feature_rows, LOW),
-            pltpu.VMEM((16, rows), HIGH),
-            pltpu.VMEM((rows, width), HIGH),
-        ]
+        statistics = pltpu.VMEM((8, PER_GROUP * rows), HIGH)
+        scratch = room + [pltpu.VMEM((KV_WIDTH, keys), LOW), pltpu.VMEM(feature_rows, LOW)]
+        scratch += [statistics, pltpu.VMEM((rows, width), HIGH)]
         scratch += [pltpu.VMEM(feature_rows, LOW)] * 3 + [pltpu.VMEM((blocks, rows, hidden), LOW)] * 2
         scratch += [pltpu.VMEM((6, rows, hidden), LOW)] * 2 + [pltpu.VMEM(feature_rows, LOW)]
         scratch += [pltpu.VMEM(shape, LOW) for shape in key_room]
         late = (w_key, w_value, w_query, w_output, cotangent)
         scratch += [pltpu.VMEM(v.shape, LOW) for v in late]
-        scratch += [pltpu.VMEM(shape, LOW) for shape in (feature_rows, feature_rows, (blocks, rows, 2 * KV_WIDTH))]
-        scratch += [pltpu.VMEM((16, rows), HIGH)] * 2
-        scratch += weight_room + [pltpu.SemaphoreType.DMA((3, 2)), pltpu.SemaphoreType.DMA((LOCALS_MIDDLE,))]
+        kv_shape = (blocks, rows, 2 * KV_WIDTH)
+        scratch += [pltpu.VMEM(shape, LOW) for shape in (feature_rows, feature_rows, kv_shape, kv_shape)]
+        scratch += [statistics, statistics, pltpu.VMEM((rows, width), HIGH)]
+        scratch += weight_room + [pltpu.SemaphoreType.DMA((LOCALS_MIDDLE,))]
         scratch += [pltpu.SemaphoreType.DMA((COPIES_MIDDLE,)), pltpu.SemaphoreType.DMA((COPIES_MIDDLE,))]
-        given = [where, h_one, gain_rows, cosine, sine, *late, g_one, u_one, m_one, b_one, *weights]
-        specs = [SMEM] + [VMEM] * 4 + [ANY] * 15
-        return call(functools.partial(middle_kernel, blocks), outs, specs, scratch, "middle", 7, 3)(*given)
-
-    block_out, c_one, dm_one, gains, b_all, f_all, rhs_all, *halves_two = middle()
+        given = [where, tokens, gain_rows, cosine, sine, *late, w_gate, w_up, w_down]
+        specs = [SMEM] + [VMEM] * 4 + [ANY] * 8
+        return call(functools.partial(layers_kernel, blocks), outs, specs, scratch, "layers", 16, 3)(*given)
+
+    outs = layers()
+    block_out, c_one, dm_one, gains, a_one, q_one, kv_one, o_one, lse_one = outs[:9]
+    b_all, f_all, rhs_all, *halves_two = outs[13:]
 
     def close(h, grad_middle, grad_query, partial):
         sent = swap(jnp.stack([partial[1], partial[3]]), 1)
@@ -1217,11 +1208,12 @@
     if places == 8 and blocks == 4:
         outs = finish()
         input_grad, gate_grad, up_grad, down_grad, query_grad, key_grad, value_grad, output_grad, gains = outs
-        gains = gains[:2, :block]
         results = [block_out, input_grad, query_grad, key_grad, value_grad, output_grad, gate_grad, up_grad, down_grad]
         turned_over = (3, 4, 5)
         outs = [(v.shape[::-1] if i in turned_over else v.shape, v.dtype) for i, v in enumerate(results)]
-        results = call(emit_kernel, outs, [VMEM] * len(outs), [], "emit")(*results)
+        outs += [((1, block), HIGH)] * 2
+        *results, one, two = call(emit_kernel, outs, [VMEM] * (len(results) + 1), [], "emit")(gains, *results)
+        gains = one[0], two[0]
         block_out, input_grad, query_grad, key_grad, value_grad, output_grad, gate_grad, up_grad, down_grad = results
         key_grad, value_grad, output_grad = key_grad.T, value_grad.T, output_grad.T
     else:

time: 237 us -> 222 us (0.937)
  Pallas kernels: 228 us -> 215 us
    pallas_call x3 -> x2, Pallas kernels: 127 us -> 115 us  [the longest x1 111 us: layers(): call(functools.partial(layers_kernel, blocks), outs, specs, scratch, 'lay...]
where the time goes in v6:
time: 222 us; the launch traced here: 219 us
  Pallas kernels  215 us (97%)
    pallas_call x1, Pallas kernels, layers(): call(functools.partial(layers_kernel, blocks), outs, specs, scratch, 'lay...  111 us
    pallas_call x1, Pallas kernels, finish(): call(finish_kernel, outs, specs, scratch, 'finish', 0, 2)  100 us

profile of v6, /device:TPU:0, one launch (start us, length us, event | category | flops | bytes accessed | tf_op | source)
XLA Modules:
  0.0 219.3 jit_solution(13714085722754229667)
XLA Ops:
  1.3 0.7 stack.9
  2.0 0.7 stack.10
  2.7 0.6 pad_maximum_fusion.refs_2_.refs_1_
  3.3 0.8 multiply_sine_fusion
  4.1 110.8 %layers.1 = (bf16[960,256]{1,0:T(8,128)(2,1)}, bf16[960,256]{1,0:T(8,128)(2,1)}, f32[256,960]{1,0:T(8,128)}, f32[8,960]{1,0:T(8,128)}, bf16[960,256]{1,0:T(8,128...) custom-call(s32[1]{0:T(128)S(6)} %copy.23.refs_0_, ...), custom_call_target="tpu_custom_call" | custom-call | tf_op jit(solution)/shard_map/layers/pallas_call | solution.py:1154
  114.9 100.2 %finish.1 = (f32[960,256]{1,0:T(8,128)}, f32[120,640]{1,0:T(8,128)}, f32[120,640]{1,0:T(8,128)}, f32[120,640]{1,0:T(8,128)}, f32[120,960]{1,0:T(8,128)}, /*index...) custom-call(s32[1]{0:T(128)S(6)} %copy.23.refs_0_, ...), custom_call_target="tpu_custom_call" | custom-call | tf_op jit(solution)/shard_map/finish/pallas_call | solution.py:1206
  215.1 4.0 %emit.1 = (bf16[960,256]{1,0:T(8,128)(2,1)}, f32[960,256]{1,0:T(8,128)}, f32[120,960]{1,0:T(8,128)}, f32[320,120]{1,0:T(8,128)}, f32[320,120]{1,0:T(8,128)}, /*i...) custom-call(f32[8,128]{1,0:T(8,128)} %get-tuple-element.62.gains, ...), custom_call_target="tpu_custom_call" | custom-call | tf_op jit(solution)/shard_map/emit/pallas_call | solution.py:1215
  (2 shorter events, 0.0 us)

commit v7 on v6

--- a/solution.py
+++ b/solution.py
@@ -37,6 +37,10 @@
     return 0.5 * (1.0 + jnp.tanh(0.5 * value))
 
 
+def wide(gain_ref):
+    return gain_ref[...].astype(HIGH).reshape(1, gain_ref.shape[0])
+
+
 def inverse_rms(rows):
     return lax.rsqrt(jnp.mean(rows * rows, axis=1, keepdims=True) + EPSILON)
 
@@ -307,7 +311,7 @@
 COPIES_SPREAD = 10
 
 
-def first_forward(where_ref, h_ref, gain_ref, cos_ref, sin_ref, late, lates, owns, parts, results, attn, held, links, local):
+def first_forward(where_ref, h_ref, gain_one_ref, gain_two_ref, cos_ref, sin_ref, late, lates, owns, parts, results, attn, held, links, local):
     a_ref, q_ref, kv_ref, o_ref, lse_ref, m_ref, b_ref, g_ref, u_ref = parts
     bias, k_sc, vt_sc = attn
     wk_ref, wv_ref, wq_ref, wo_ref, _ = late
@@ -337,7 +341,7 @@
 
     lates[0].wait()
     lates[1].wait()
-    gain_one = gain_ref[0:1].astype(HIGH)
+    gain_one = wide(gain_one_ref)
     project(hidden, gain_one, wq_ref, wk_ref, wv_ref, cos_ref[...], sin_ref[...], a_ref, q_ref, kv_ref.at[0], queue)
     g1.first()
     g2.first()
@@ -362,7 +366,7 @@
     d2.first()
     u1.third()
     lates[3].wait()
-    middle, normed = after_attention(hidden, o_ref, wo_ref, gain_ref[1:2].astype(HIGH), m_ref, b_ref)
+    middle, normed = after_attention(hidden, o_ref, wo_ref, wide(gain_two_ref), m_ref, b_ref)
     early = [local.move(source, target) for source, target in zip(parts[:7], results[:7])]
     u2.third()
     for copy in loads:
@@ -394,10 +398,10 @@
     return total
 
 
-def ffn_back(grad, g_ref, u_ref, m_ref, gain, wg, wu, wd, mine_ref, theirs_ref):
+def ffn_back(grad, g_ref, u_ref, m_ref, gain, wg, wu, wd, mine_ref, theirs_ref, ready):
     low_grad = grad.astype(LOW)
     grad_normed = jnp.zeros(m_ref.shape, HIGH)
-    for step in range(wg.shape[0]):
+    for step in (1, 3, 0, 2):
         grad_active = nn(low_grad, wd[step])
         gate = g_ref[step].astype(HIGH)
         up = u_ref[step].astype(HIGH)
@@ -409,6 +413,8 @@
         kept[step // 2] = grad_gate
         kept[2 + step // 2] = grad_up
         kept[4 + step // 2] = (silu * up).astype(LOW)
+        if step == 3:
+            ready()
         grad_normed = grad_normed + nt(grad_gate, wg[step]) + nt(grad_up, wu[step])
     return norm_back(m_ref[...], gain, grad_normed, grad)
 
@@ -445,7 +451,8 @@
             group_keys = k_sc[group, cut]
             values = v_sc[group, cut]
             at = pl.ds(pl.multiple_of(group * HD, HD), HD)
-            after = pl.ds(pl.multiple_of(KV_WIDTH + group * HD, HD), HD)
+            key_rows = pl.ds(pl.multiple_of(group * 2 * HD, HD), HD)
+            value_rows = pl.ds(pl.multiple_of(group * 2 * HD + HD, HD), HD)
             keys_t = kt_sc[at, cut]
             query, grad_out = side_by_side(q_ref, group), side_by_side(do_sc, group)
             scores = scored(group_keys, query, bias[cut])
@@ -462,8 +469,8 @@
             grad_values = nt(grad_out, prob.astype(LOW))
             for step in range(blocks // 2):
                 part = slice(step * rows, (step + 1) * rows)
-                dkv_ref[start // rows + step, at, :] = grad_keys[:, part].astype(LOW)
-                dkv_ref[start // rows + step, after, :] = grad_values[:, part].astype(LOW)
+                dkv_ref[start // rows + step, key_rows, :] = grad_keys[:, part].astype(LOW)
+                dkv_ref[start // rows + step, value_rows, :] = grad_values[:, part].astype(LOW)
             return carry
 
         lax.fori_loop(0, KVH, group_body, 0)
@@ -475,24 +482,33 @@
 class Settle:
     def __init__(self, links, dkv_ref, near_ref, sum_ref, far_ref):
         self.refs = dkv_ref, near_ref, sum_ref, far_ref
-        self.aside = links.push(dkv_ref.at[3], near_ref.at[1], SIBLING)
+        cut = 3 * 2 * HD
+        self.spans = [pl.ds(0, cut), pl.ds(cut, dkv_ref.shape[1] - cut)]
+        self.asides = [links.push(dkv_ref.at[3, span], near_ref.at[1, span], SIBLING) for span in self.spans]
         self.near = links.push(dkv_ref.at[1], near_ref.at[0], SIBLING)
-        self.far = links.push(sum_ref, far_ref, ACROSS)
+        self.fars = [links.push(sum_ref.at[span], far_ref.at[span], ACROSS) for span in self.spans]
+        self.copies = [*self.asides, self.near, *self.fars]
+
+    def across(self, which):
+        dkv_ref, near_ref, sum_ref, _ = self.refs
+        span = self.spans[which]
+        self.asides[which].wait_recv()
+        sum_ref[span] = (dkv_ref[2, span].astype(HIGH) + near_ref[1, span].astype(HIGH)).astype(LOW)
+        self.fars[which].start()
+
+    def before(self, group):
+        pl.when(group == 3)(self.asides[0].start)
+        pl.when(group == 4)(functools.partial(self.across, 0))
 
     def between(self, group):
-        dkv_ref, near_ref, sum_ref, _ = self.refs
-        pl.when(group == 0)(self.aside.start)
-
-        @pl.when(group == 1)
-        def _():
-            self.aside.wait_recv()
-            sum_ref[...] = (dkv_ref[2].astype(HIGH) + near_ref[1].astype(HIGH)).astype(LOW)
-            self.far.start()
+        pl.when(group == 0)(self.asides[1].start)
+        pl.when(group == 1)(functools.partial(self.across, 1))
 
     def finish(self):
         dkv_ref, near_ref, _, far_ref = self.refs
         self.near.wait_recv()
-        self.far.wait_recv()
+        for copy in self.fars:
+            copy.wait_recv()
         return dkv_ref[0].astype(HIGH) + near_ref[0].astype(HIGH) + far_ref[...].astype(HIGH)
 
 
@@ -535,12 +551,13 @@
     return keep, send
 
 
-COPIES_MIDDLE = 6 * COPIES_SPREAD + COPIES_SHARE + 20
+COPIES_MIDDLE = 6 * COPIES_SPREAD + COPIES_SHARE + 22
 LOCALS_MIDDLE = 40
 
 
 def layers_kernel(blocks, *refs):
-    where_ref, tokens_ref, gain_ref, cos_ref, sin_ref = refs[:5]
+    where_ref, tokens_ref, gain_one_ref, gain_two_ref, cos_ref, sin_ref = refs[:6]
+    refs = refs[1:]
     late_refs, owns = refs[5:10], refs[10:13]
     out_ref, c_ref, dm_ref, gains_ref = refs[13:17]
     results = refs[17:26]
@@ -564,7 +581,8 @@
     h_ref[...] = first_forward(
         where_ref,
         tokens_ref,
-        gain_ref,
+        gain_one_ref,
+        gain_two_ref,
         cos_ref,
         sin_ref,
         late,
@@ -595,7 +613,7 @@
     cosine, sine = cos_ref[...], sin_ref[...]
     half = blocks * rows // 2
 
-    gain_one = gain_ref[0:1].astype(HIGH)
+    gain_one = wide(gain_one_ref)
     project(h_ref[...], gain_one, wq, wk, wv, cosine, sine, a_sc, q_ref, kv_ref.at[0], share.start)
     share.near.wait_recv()
     lay_keys(kv_ref, k_sc, vt_sc, range(blocks // 2), rows)
@@ -604,7 +622,7 @@
     share.forth.wait_recv()
     lay_keys(kv_ref, k_sc, vt_sc, range(blocks // 2, blocks), rows)
     attend_rest(bias, k_sc, vt_sc, q_ref, top_sc, total_sc, part_sc, half, o_sc, lse_sc)
-    total, normed = after_attention(h_ref[...], o_sc, wo_ref, gain_ref[1:2].astype(HIGH), m_sc, b_sc)
+    total, normed = after_attention(h_ref[...], o_sc, wo_ref, wide(gain_two_ref), m_sc, b_sc)
     posted.append(both(b_sc, b_all, (everything,)))
     for step in range(blocks):
         total = total + hidden_part(normed, wg, wu, wd, g_sc, u_sc, step)
@@ -616,17 +634,18 @@
     grad = jnp.where(row < where_ref[0], cot[...].astype(HIGH).T, 0.0)
     f_sc[...] = grad.T.astype(LOW)
     first_f = both(f_sc, f_all, (everything,))
-    gain_two = gain_ref[1:2].astype(HIGH)
-    gain_part, grad_middle = ffn_back(grad, g_sc, u_sc, m_sc, gain_two, wg, wu, wd, mine, theirs)
+    gain_two = wide(gain_two_ref)
+    send_theirs = links.push(theirs, rhs_all.at[:, spans[1]], SIBLING)
+    gain_part, grad_middle = ffn_back(
+        grad, g_sc, u_sc, m_sc, gain_two, wg, wu, wd, mine, theirs, send_theirs.start
+    )
     first_loads = [local.move(source, target) for source, target in ((g_any, g_sc), (u_any, u_sc), (m_any, m_sc))]
     keep_mine = local.move(mine, rhs_all.at[:, spans[0]])
-    send_theirs = links.push(theirs, rhs_all.at[:, spans[1]], SIBLING)
-    send_theirs.start()
     gains_ref[...] = jnp.zeros(gains_ref.shape, HIGH)
     gains_ref[1:2] = gain_part
     c_sc[...] = grad_middle.T.astype(LOW)
     attend_back(
-        grad_middle, wo_ref, q_ref, o_sc, lse_sc, cosine, sine, dq_sc, dkv_sc, room, lambda group: None, settle.between
+        grad_middle, wo_ref, q_ref, o_sc, lse_sc, cosine, sine, dq_sc, dkv_sc, room, settle.before, settle.between
     )
     settle.near.start()
     from_query = nn(wq[...], dq_sc[...]).T
@@ -653,10 +672,11 @@
     f_sc[...] = grad.T.astype(LOW)
     both.layer = 2
     posted.append(both(f_sc, f_all, (everything,)))
-    gain_part, grad_middle = ffn_back(grad, g_sc, u_sc, m_sc, gain_two, wg, wu, wd, mine, theirs)
+    send_last = links.push(theirs, rhs_all.at[:, spans[3]], SIBLING)
+    gain_part, grad_middle = ffn_back(
+        grad, g_sc, u_sc, m_sc, gain_two, wg, wu, wd, mine, theirs, send_last.start
+    )
     keep_last = local.move(mine, rhs_all.at[:, spans[2]])
-    send_last = links.push(theirs, rhs_all.at[:, spans[3]], SIBLING)
-    send_last.start()
     gains_ref[1:2] = gains_ref[1:2] + gain_part
     dm_ref[...] = grad_middle
     c_ref[...] = grad_middle.T.astype(LOW)
@@ -667,7 +687,7 @@
     send_theirs.wait_recv()
     keep_last.wait()
     send_last.wait()
-    for copy in (settle.aside, settle.near, settle.far, share.near, share.far, share.forth, *waited):
+    for copy in (*settle.copies, share.near, share.far, share.forth, *waited):
         copy.wait_send()
 
 
@@ -684,6 +704,9 @@
 
 
 def close_keys(total, cosine, sine, dkv_ref):
+    starts = range(0, total.shape[0], 2 * HD)
+    parts = [total[start : start + HD] for start in starts] + [total[start + HD : start + 2 * HD] for start in starts]
+    total = jnp.concatenate(parts, axis=0)
     turned_keys = turned(total[:KV_WIDTH], cosine, sine, -1.0, 1.0)
     dkv_ref[:KV_WIDTH] = turned_keys.astype(LOW)
     dkv_ref[KV_WIDTH:] = total[KV_WIDTH:].astype(LOW)
@@ -696,12 +719,12 @@
 
 
 def close_kernel(*refs):
-    h_ref, gain_ref, dm_ref, dq_ref, wq_ref, wk_ref, wv_ref, cos_ref, sin_ref = refs[:9]
+    h_ref, gain_one_ref, dm_ref, dq_ref, wq_ref, wk_ref, wv_ref, cos_ref, sin_ref = refs[:9]
     own, near, far, dh_ref, dkv_ref, gain_part_ref = refs[9:]
     total = own[...].astype(HIGH) + near[...].astype(HIGH) + far[...].astype(HIGH)
     grad_keys, grad_values = close_keys(total, cos_ref[...], sin_ref[...], dkv_ref)
     hidden = h_ref[...].astype(HIGH).T
-    gain = gain_ref[0:1].astype(HIGH)
+    gain = wide(gain_one_ref)
     from_query = nn(wq_ref[...], dq_ref[...]).T
     gain_part, grad_in = close_rows(hidden, gain, dm_ref[...], from_query, grad_keys, grad_values, wk_ref, wv_ref)
     gain_part_ref[...] = gain_part
@@ -846,11 +869,11 @@
     (("tail",), ("f2", "f3", "f5", "f0", "f4", "f1", "f4", "a2", "a1", "g0", "a0", "f2", "f3", "a2", "f5", "f2", "f0", "f3", "a2", "f1", "a1", "g0", "a0", "a2", "g0", "a1", "a0", "f5", "a2", "g0", "a0", "a2", "g0", "a1", "f0", "a0", "f5", "a1", "a0", "a1", "f0")),
 )
 PARTS = len(FFN_CUTS)
-COPIES_FINISH = 4 * len(ORDERS) + 6 * len(ATTN_ORDERS) + 5 + 3 + 4
+COPIES_FINISH = 4 * len(ORDERS) + 6 * len(ATTN_ORDERS) + 5 + 5 + 4
 
 
 def finish_kernel(*refs):
-    where_ref, gain_ref, cos_ref, sin_ref, gains_ref = refs[:5]
+    where_ref, gain_one_ref, cos_ref, sin_ref, gains_ref = refs[:5]
     late_refs, lse_any = refs[5:14], refs[14]
     a_ref, c_ref, left_two, long_two, short_two, side_two, b_any, f_any, rhs_any = refs[15:24]
     count = 4
@@ -959,8 +982,7 @@
         for when, folds in passes[which].items():
             if folds:
                 pl.when(group == when)(functools.partial(take, folds))
-        if which == "q":
-            settle.between(group)
+        (settle.between if which == "q" else settle.before)(group)
 
     for step, folds in plan:
         if step[0] in passes:
@@ -1004,7 +1026,7 @@
                 )
         elif step[0] == "close":
             hidden = h_ref[...].astype(HIGH).T
-            gain = gain_ref[0:1].astype(HIGH)
+            gain = wide(gain_one_ref)
             gain_part, grad_in = close_rows(
                 hidden, gain, dm_ref[...], from_query, grad_keys, grad_values, wk_ref, wv_ref
             )
@@ -1112,7 +1134,6 @@
     position = (me * rows + jnp.arange(rows, dtype=jnp.int32)).astype(HIGH)
     angles = frequency[:, None] * position[None, :]
     cosine, sine = jnp.cos(angles), jnp.sin(angles)
-    gain_rows = jnp.stack([attn_gain, ffn_gain])
 
     feature_rows = (width, rows)
     project_outs = [(feature_rows, LOW), (feature_rows, LOW), ((blocks, rows, 2 * KV_WIDTH), LOW)]
@@ -1149,8 +1170,8 @@
         scratch += [statistics, statistics, pltpu.VMEM((rows, width), HIGH)]
         scratch += weight_room + [pltpu.SemaphoreType.DMA((LOCALS_MIDDLE,))]
         scratch += [pltpu.SemaphoreType.DMA((COPIES_MIDDLE,)), pltpu.SemaphoreType.DMA((COPIES_MIDDLE,))]
-        given = [where, tokens, gain_rows, cosine, sine, *late, w_gate, w_up, w_down]
-        specs = [SMEM] + [VMEM] * 4 + [ANY] * 8
+        given = [where, tokens, attn_gain, ffn_gain, cosine, sine, *late, w_gate, w_up, w_down]
+        specs = [SMEM] + [VMEM] * 5 + [ANY] * 8
         return call(functools.partial(layers_kernel, blocks), outs, specs, scratch, "layers", 16, 3)(*given)
 
     outs = layers()
@@ -1161,7 +1182,7 @@
         sent = swap(jnp.stack([partial[1], partial[3]]), 1)
         far = swap((partial[2].astype(HIGH) + sent[1].astype(HIGH)).astype(LOW), 2)
         outs = [(feature_rows, HIGH), ((2 * KV_WIDTH, rows), LOW), ((1, width), HIGH)]
-        given = [h, gain_rows, grad_middle, grad_query, w_query, w_key, w_value, cosine, sine]
+        given = [h, attn_gain, grad_middle, grad_query, w_query, w_key, w_value, cosine, sine]
         given += [partial[0], sent[0], far]
         return call(close_kernel, outs, [VMEM] * 12, [], "close")(*given)
 
@@ -1201,7 +1222,7 @@
         scratch += [pltpu.VMEM(shape, HIGH) for shape in ((2, 2, 2, 8, 128), (8, 8, 128), (2, 2, 8, 128))]
         scratch += [pltpu.SemaphoreType.DMA((48,)), pltpu.SemaphoreType.DMA((COPIES_FINISH,))]
         scratch += [pltpu.SemaphoreType.DMA((COPIES_FINISH,))]
-        given = [where, gain_rows, cosine, sine, gains, *late, lse_one, a_one, c_one, *halves_two]
+        given = [where, attn_gain, cosine, sine, gains, *late, lse_one, a_one, c_one, *halves_two]
         specs = [SMEM] + [VMEM] * 4 + [ANY] * 19
         return call(finish_kernel, outs, specs, scratch, "finish", 0, 2)(*given, b_all, f_all, rhs_all)
 

time: 222 us -> 215 us (0.968)
  Pallas kernels: 215 us -> 210 us
    pallas_call x1, Pallas kernels: 111 us -> 106 us  [layers(): call(functools.partial(layers_kernel, blocks), outs, specs, scratch, 'lay...]
where the time goes in v7:
time: 215 us; the launch traced here: 212 us
  Pallas kernels  210 us (98%)
    pallas_call x1, Pallas kernels, layers(): call(functools.partial(layers_kernel, blocks), outs, specs, scratch, 'lay...  106 us
    pallas_call x1, Pallas kernels, finish(): call(finish_kernel, outs, specs, scratch, 'finish', 0, 2)  99.9 us

profile of v7, /device:TPU:0, one launch (start us, length us, event | category | flops | bytes accessed | tf_op | source)
XLA Modules:
  0.0 212.0 jit_solution(6178560098976214551)
XLA Ops:
  1.3 0.8 multiply_sine_fusion
  2.1 105.7 %layers.1 = (bf16[960,256]{1,0:T(8,128)(2,1)}, bf16[960,256]{1,0:T(8,128)(2,1)}, f32[256,960]{1,0:T(8,128)}, f32[8,960]{1,0:T(8,128)}, bf16[960,256]{1,0:T(8,128...) custom-call(s32[1]{0:T(128)S(6)} %copy.23.refs_0_, ...), custom_call_target="tpu_custom_call" | custom-call | tf_op jit(solution)/shard_map/layers/pallas_call | solution.py:1175
  107.8 99.9 %finish.1 = (f32[960,256]{1,0:T(8,128)}, f32[120,640]{1,0:T(8,128)}, f32[120,640]{1,0:T(8,128)}, f32[120,640]{1,0:T(8,128)}, f32[120,960]{1,0:T(8,128)}, /*index...) custom-call(s32[1]{0:T(128)S(6)} %copy.23.refs_0_, bf16[960]{0:T(1024)(128)(2,1)} %refs_1_.1, ...), custom_call_target="tpu_custom_call" | custom-call | tf_op jit(solution)/shard_map/finish/pallas_call | solution.py:1227
  207.7 4.0 %emit.1 = (bf16[960,256]{1,0:T(8,128)(2,1)}, f32[960,256]{1,0:T(8,128)}, f32[120,960]{1,0:T(8,128)}, f32[320,120]{1,0:T(8,128)}, f32[320,120]{1,0:T(8,128)}, /*i...) custom-call(f32[8,128]{1,0:T(8,128)} %get-tuple-element.62.gains, ...), custom_call_target="tpu_custom_call" | custom-call | tf_op jit(solution)/shard_map/emit/pallas_call | solution.py:1236
  (2 shorter events, 0.0 us)

commit v8 on v7

--- a/solution.py
+++ b/solution.py
@@ -401,8 +401,12 @@
 def ffn_back(grad, g_ref, u_ref, m_ref, gain, wg, wu, wd, mine_ref, theirs_ref, ready):
     low_grad = grad.astype(LOW)
     grad_normed = jnp.zeros(m_ref.shape, HIGH)
-    for step in (1, 3, 0, 2):
-        grad_active = nn(low_grad, wd[step])
+    order, products = (1, 3, 0, 2), []
+    coming = nn(low_grad, wd[order[0]])
+    for turn, step in enumerate(order):
+        grad_active = coming
+        if turn < 3:
+            coming = nn(low_grad, wd[order[turn + 1]])
         gate = g_ref[step].astype(HIGH)
         up = u_ref[step].astype(HIGH)
         sig = sigmoid(gate)
@@ -415,7 +419,12 @@
         kept[4 + step // 2] = (silu * up).astype(LOW)
         if step == 3:
             ready()
-        grad_normed = grad_normed + nt(grad_gate, wg[step]) + nt(grad_up, wu[step])
+        products.append((step, grad_gate, grad_up))
+        if turn:
+            before, one, two = products[turn - 1]
+            grad_normed = grad_normed + nt(one, wg[before]) + nt(two, wu[before])
+    before, one, two = products[-1]
+    grad_normed = grad_normed + nt(one, wg[before]) + nt(two, wu[before])
     return norm_back(m_ref[...], gain, grad_normed, grad)
 
 
@@ -825,48 +834,48 @@
 
 FFN_CUTS = ((0, 256), (256, 384))
 ORDERS = (
+    ("Z0", "Z1", "Y", "X"),
     ("Y", "X", "Z0", "Z1"),
-    ("Z0", "Y", "Z1", "X"),
-    ("Z0", "Z1", "X", "Y"),
     ("Y", "Z0", "X", "Z1"),
-    ("X", "Y", "Z0", "Z1"),
-    ("X", "Y", "Z0", "Z1"),
+    ("Y", "X", "Z0", "Z1"),
+    ("Z0", "Y", "X", "Z1"),
+    ("X", "Z0", "Y", "Z1"),
 )
 ATTN_ORDERS = (
-    ("Z0", "X", "Z1", "Y"),
     ("Y", "Z0", "X", "Z1"),
     ("X", "Z0", "Y", "Z1"),
+    ("Z0", "X", "Y", "Z1"),
 )
 ATTN_CUTS = (128, 256, 256)
 PLAN = (
     (("begin",), ()),
+    (("w", 0, 1), ()),
+    (("w", 0, 0), ()),
     (("w", 1, 1), ()),
     (("w", 1, 0), ()),
-    (("w", 3, 1), ()),
-    (("w", 3, 0), ()),
+    (("w", 5, 1), ()),
+    (("w", 5, 0), ()),
+    (("w", 2, 1), ()),
+    (("w", 2, 0), ()),
     (("w", 4, 1), ()),
     (("w", 4, 0), ()),
-    (("w", 2, 1), ()),
-    (("w", 2, 0), ()),
     (("prep",), ()),
     (("p", 0), ()),
     (("p", 1), ()),
-    (("p", 2), ()),
+    (("p", 2), ("f0",)),
     (("p", 3), ()),
     (("p", 4), ()),
     (("q", 0), ()),
-    (("q", 1), ("f4",)),
-    (("q", 2), ("f1",)),
-    (("q", 3), ("f3",)),
+    (("q", 1), ()),
+    (("q", 2), ("f1", "f5")),
+    (("q", 3), ()),
     (("q", 4), ()),
-    (("w", 5, 1), ()),
-    (("w", 5, 0), ()),
-    (("w", 0, 1), ("f4",)),
-    (("w", 0, 0), ()),
-    (("kf",), ("f2",)),
+    (("kf",), ("f0", "f4")),
     (("close",), ()),
-    (("attn",), ("f1",)),
-    (("tail",), ("f2", "f3", "f5", "f0", "f4", "f1", "f4", "a2", "a1", "g0", "a0", "f2", "f3", "a2", "f5", "f2", "f0", "f3", "a2", "f1", "a1", "g0", "a0", "a2", "g0", "a1", "a0", "f5", "a2", "g0", "a0", "a2", "g0", "a1", "f0", "a0", "f5", "a1", "a0", "a1", "f0")),
+    (("w", 3, 1), ("f2",)),
+    (("w", 3, 0), ()),
+    (("attn",), ("f0",)),
+    (("tail",), ("f1", "f5", "f0", "f4", "f2", "a1", "a2", "f4", "f3", "f2", "f1", "f4", "a0", "g0", "f2", "a2", "f5", "f1", "a1", "a2", "f3", "f5", "a1", "a0", "g0", "a2", "a0", "a1", "g0", "a2", "f3", "a0", "a2", "a1", "g0", "a0", "a1", "g0", "f3", "a0")),
 )
 PARTS = len(FFN_CUTS)
 COPIES_FINISH = 4 * len(ORDERS) + 6 * len(ATTN_ORDERS) + 5 + 5 + 4

time: 215 us -> 210 us (0.977)
  Pallas kernels: 210 us -> 205 us
    pallas_call x1, Pallas kernels: 99.9 us -> 96 us  [finish(): call(finish_kernel, outs, specs, scratch, 'finish', 0, 2)]
where the time goes in v8:
time: 210 us; the launch traced here: 207 us
  Pallas kernels  205 us (98%)
    pallas_call x1, Pallas kernels, layers(): call(functools.partial(layers_kernel, blocks), outs, specs, scratch, 'lay...  105 us
    pallas_call x1, Pallas kernels, finish(): call(finish_kernel, outs, specs, scratch, 'finish', 0, 2)  96 us

profile of v8, /device:TPU:0, one launch (start us, length us, event | category | flops | bytes accessed | tf_op | source)
XLA Modules:
  0.0 207.1 jit_solution(7306114370730572696)
XLA Ops:
  1.3 0.8 multiply_sine_fusion
  2.1 104.7 %layers.1 = (bf16[960,256]{1,0:T(8,128)(2,1)}, bf16[960,256]{1,0:T(8,128)(2,1)}, f32[256,960]{1,0:T(8,128)}, f32[8,960]{1,0:T(8,128)}, bf16[960,256]{1,0:T(8,128...) custom-call(s32[1]{0:T(128)S(6)} %copy.23.refs_0_, ...), custom_call_target="tpu_custom_call" | custom-call | tf_op jit(solution)/shard_map/layers/pallas_call | solution.py:1184
  106.8 96.0 %finish.1 = (f32[960,256]{1,0:T(8,128)}, f32[120,640]{1,0:T(8,128)}, f32[120,640]{1,0:T(8,128)}, f32[120,640]{1,0:T(8,128)}, f32[120,960]{1,0:T(8,128)}, /*index...) custom-call(s32[1]{0:T(128)S(6)} %copy.23.refs_0_, bf16[960]{0:T(1024)(128)(2,1)} %refs_1_.1, ...), custom_call_target="tpu_custom_call" | custom-call | tf_op jit(solution)/shard_map/finish/pallas_call | solution.py:1236
  202.8 4.0 %emit.1 = (bf16[960,256]{1,0:T(8,128)(2,1)}, f32[960,256]{1,0:T(8,128)}, f32[120,960]{1,0:T(8,128)}, f32[320,120]{1,0:T(8,128)}, f32[320,120]{1,0:T(8,128)}, /*i...) custom-call(f32[8,128]{1,0:T(8,128)} %get-tuple-element.62.gains, ...), custom_call_target="tpu_custom_call" | custom-call | tf_op jit(solution)/shard_map/emit/pallas_call | solution.py:1245
  (2 shorter events, 0.0 us)

commit v9 on v8

--- a/solution.py
+++ b/solution.py
@@ -189,11 +189,15 @@
     return {axis: jnp.bitwise_xor(lax.axis_index(axis), distance)}
 
 
+def hail(partners):
+    for axis, distance in partners:
+        pl.semaphore_signal(
+            pltpu.get_barrier_semaphore(), inc=1, device_id=partner(axis, distance), device_id_type=MESH
+        )
+
+
 def greet(partners):
-    barrier = pltpu.get_barrier_semaphore()
-    for axis, distance in partners:
-        pl.semaphore_signal(barrier, inc=1, device_id=partner(axis, distance), device_id_type=MESH)
-    pl.semaphore_wait(barrier, len(partners))
+    pl.semaphore_wait(pltpu.get_barrier_semaphore(), len(partners))
 
 
 class Links:
@@ -583,6 +587,7 @@
     wg, wu, wd, load, send, receive = refs[69:]
     rows = h_ref.shape[0]
     core = lax.axis_index("head") % 2
+    hail((SIBLING, ACROSS, SIDE, BEYOND))
     local = Local(load)
     links = Links(send, receive)
     lates = [local.move(source, target) for source, target in zip(late_refs, late)]
@@ -912,6 +917,7 @@
     place = lax.axis_index("dp")
     head_at = lax.axis_index("head")
     core, across = head_at % 2, head_at // 2
+    hail((SIBLING, ACROSS, SIDE, BEYOND, FAR_SIDE))
     links, local = Links(send, receive), Local(load)
     sums = {}
     for index, (whole, got, order) in enumerate(zip(wholes, rooms, ORDERS)):

time: 210 us -> 210 us (level)
  no operation moved by 1% of the time
where the time goes in v9:
time: 210 us; the launch traced here: 207 us
  Pallas kernels  205 us (98%)
    pallas_call x1, Pallas kernels, layers(): call(functools.partial(layers_kernel, blocks), outs, specs, scratch, 'lay...  105 us
    pallas_call x1, Pallas kernels, finish(): call(finish_kernel, outs, specs, scratch, 'finish', 0, 2)  96 us

profile of v9, /device:TPU:0, one launch (start us, length us, event | category | flops | bytes accessed | tf_op | source)
XLA Modules:
  0.0 207.1 jit_solution(9889031371381887124)
XLA Ops:
  1.3 0.8 multiply_sine_fusion
  2.1 104.7 %layers.1 = (bf16[960,256]{1,0:T(8,128)(2,1)}, bf16[960,256]{1,0:T(8,128)(2,1)}, f32[256,960]{1,0:T(8,128)}, f32[8,960]{1,0:T(8,128)}, bf16[960,256]{1,0:T(8,128...) custom-call(s32[1]{0:T(128)S(6)} %copy.23.refs_0_, ...), custom_call_target="tpu_custom_call" | custom-call | tf_op jit(solution)/shard_map/layers/pallas_call | solution.py:1190
  106.8 96.0 %finish.1 = (f32[960,256]{1,0:T(8,128)}, f32[120,640]{1,0:T(8,128)}, f32[120,640]{1,0:T(8,128)}, f32[120,640]{1,0:T(8,128)}, f32[120,960]{1,0:T(8,128)}, /*index...) custom-call(s32[1]{0:T(128)S(6)} %copy.23.refs_0_, bf16[960]{0:T(1024)(128)(2,1)} %refs_1_.1, ...), custom_call_target="tpu_custom_call" | custom-call | tf_op jit(solution)/shard_map/finish/pallas_call | solution.py:1242
  202.9 4.0 %emit.1 = (bf16[960,256]{1,0:T(8,128)(2,1)}, f32[960,256]{1,0:T(8,128)}, f32[120,960]{1,0:T(8,128)}, f32[320,120]{1,0:T(8,128)}, f32[320,120]{1,0:T(8,128)}, /*i...) custom-call(f32[8,128]{1,0:T(8,128)} %get-tuple-element.62.gains, ...), custom_call_target="tpu_custom_call" | custom-call | tf_op jit(solution)/shard_map/emit/pallas_call | solution.py:1251
  (2 shorter events, 0.0 us)
